TPU v7x, 32 devices: a whole 2x2x4 slice. The times are simulated.
32 devices in a mesh: depth: 8 (over y, x, core), strip: 4 (over z).
Axes of the slice: x: 2, y: 2, z: 4, core: 2. Of those that a mesh axis runs over, the one named last changes fastest.
Arguments:
- density: float32 [32, 64, 2048], P('depth', 'strip'), may hold values from -6 to 6
- materials: int32 [32, 64, 2048], P('depth', 'strip'), may hold values from 0 to 3
- occupancy_flags: int32 [8, 4, 16], P('depth', 'strip'), may hold values from 0 to 1, as said below
- tf_color: float32 [4, 3, 16], replicated, may hold values from 0.1 to 1
- tf_opacity: float32 [4, 16], replicated, may hold values from 0.0005 to 0.05
Outputs:
- image: float32 [4, 64, 2048], P(None, 'strip', 'depth')
Inputs may be any that keep to these rules, and one draw needn't show every extreme that they name: `occupancy_flags`: occupied tiles cluster around one depth slab drawn from the seed; the share of occupied tiles differs strongly between depth slabs.
All inputs are finite; a program needn't handle non-finite values.
Results may differ from a plain program's by a relative error of at most 0.0003.
Values sent between devices are 32-bit elements; how exact they have to be, the bound alone decides.
No kernel may reach another device: no remote copies, remote signals or barrier semaphores. Data moves between devices by JAX's collectives and lax.ppermute only.
A program may use at most 64 MiB of HBM per device.

v0:
```python
import jax
import jax.numpy as jnp
from jax import lax
from jax.sharding import PartitionSpec as P

light_x = 1.0 / 3.0
light_y = 2.0 / 3.0
light_z = 2.0 / 3.0
ambient = 0.3
diffuse = 0.7


def with_halo(array, sides, width):
    for axis, dim in sides:
        devices, length = (lax.axis_size(axis), array.shape[dim])
        up = [(i, (i + 1) % devices) for i in range(devices - 1)]
        down = [(j, i) for i, j in up]
        last = lax.slice_in_dim(array, length - width, length, axis=dim)
        first = lax.slice_in_dim(array, 0, width, axis=dim)
        before = lax.ppermute(last, axis, up)
        after = lax.ppermute(first, axis, down)
        array = jnp.concatenate([before, array, after], axis=dim)
    return array


def shade_slice(before, here, after, material_slice, occupied, knot_table):
    sample = here[1:-1, 1:-1]
    grad_z = 0.5 * (after[1:-1, 1:-1] - before[1:-1, 1:-1])
    grad_y = 0.5 * (here[2:, 1:-1] - here[:-2, 1:-1])
    grad_x = 0.5 * (here[1:-1, 2:] - here[1:-1, :-2])
    knot_count = knot_table.shape[1]
    material_count = knot_table.shape[0] // 4
    position = jnp.clip(
        (sample.reshape(-1) + 3.0) * ((knot_count - 1) / 6.0), 0.0, knot_count - 1.0
    )
    knot_grid = jnp.arange(knot_count, dtype=jnp.float32)[:, None]
    tent_weights = jnp.maximum(0.0, 1.0 - jnp.abs(position[None, :] - knot_grid))
    looked = jnp.dot(
        knot_table,
        tent_weights,
        precision=lax.Precision.HIGHEST,
        preferred_element_type=jnp.float32,
    )
    onehot = (
        material_slice.reshape(-1)[None, :] == jnp.arange(material_count, dtype=jnp.int32)[:, None]
    ).astype(jnp.float32)
    colour = jnp.sum(
        looked[: 3 * material_count].reshape(material_count, 3, -1) * onehot[:, None, :], axis=0
    )
    density_rate = jnp.sum(looked[3 * material_count :] * onehot, axis=0) * occupied.reshape(-1)
    facing = (grad_x * light_x + grad_y * light_y + grad_z * light_z).reshape(-1)
    steepness = (grad_x * grad_x + grad_y * grad_y + grad_z * grad_z).reshape(-1)
    lighting = ambient + diffuse * jnp.abs(facing) / jnp.sqrt(1.0 + steepness)
    opacity_step = 1.0 - jnp.exp(-density_rate)
    return (colour * (lighting * opacity_step)[None, :], opacity_step)


def composite_over(nearer, farther):
    return jnp.concatenate(
        [nearer[:3] + nearer[3:] * farther[:3], nearer[3:] * farther[3:]], axis=0
    )


def on_device(density, materials, occupancy_flags, tf_color, tf_opacity):
    slab_depth, row_count, columns = density.shape
    material_count = tf_color.shape[0]
    knot_count = tf_color.shape[2]
    knot_table = jnp.concatenate(
        [tf_color.reshape(material_count * 3, knot_count), tf_opacity], axis=0
    )
    padded = with_halo(density, (("depth", 0), ("strip", 1)), 1)
    padded = jnp.pad(padded, ((0, 0), (0, 0), (1, 1)))
    tile_count = occupancy_flags.shape[2]
    tile_row = jnp.repeat(occupancy_flags[0, 0], columns // tile_count).astype(jnp.float32)
    occupied = jnp.broadcast_to(tile_row[None, :], (row_count, columns))

    def advance(state_carry, slab_index):
        radiance, transmit = state_carry
        before = lax.dynamic_index_in_dim(padded, slab_index, 0, keepdims=False)
        here = lax.dynamic_index_in_dim(padded, slab_index + 1, 0, keepdims=False)
        after = lax.dynamic_index_in_dim(padded, slab_index + 2, 0, keepdims=False)
        material_slice = lax.dynamic_index_in_dim(materials, slab_index, 0, keepdims=False)
        emitted, opacity_step = shade_slice(
            before, here, after, material_slice, occupied, knot_table
        )
        return ((radiance + transmit[None, :] * emitted, transmit * (1.0 - opacity_step)), None)

    start = (
        jnp.zeros((3, row_count * columns), jnp.float32),
        jnp.ones((row_count * columns,), jnp.float32),
    )
    (radiance, transmit), _ = lax.scan(advance, start, jnp.arange(slab_depth, dtype=jnp.int32))
    partial_value = jnp.concatenate([radiance, transmit[None, :]], axis=0).reshape(
        4, row_count, columns
    )
    groups = lax.axis_size("depth")
    levels = groups.bit_length() - 1
    block_width = columns // groups
    pieces = lax.all_to_all(partial_value, "depth", split_axis=2, concat_axis=1, tiled=True)
    pieces = pieces.reshape(4, groups, row_count, block_width)
    for section_bit in range(levels):
        pieces = composite_over(pieces[:, 0::2], pieces[:, 1::2])
    finished = pieces[:, 0]
    return jnp.concatenate([finished[:3], 1.0 - finished[3:]], axis=0)


def solution(mesh):
    placed = (
        P("depth", "strip", None),
        P("depth", "strip", None),
        P("depth", "strip", None),
        P(),
        P(),
    )
    return jax.shard_map(
        on_device, mesh=mesh, in_specs=placed, out_specs=P(None, "strip", "depth"), check_vma=False
    )
```

profile of v0, /device:TPU:0, one launch (start us, length us, event | category | flops | bytes accessed | tf_op | source)
XLA Modules:
  0.0 123.2 jit_solution(14896924852705670364)
XLA Ops:
  1.0 1.3 %collective-permute-start.1 = (f32[1,16,2048]{2,1,0:T(8,128)S(1)}, f32[1,16,2048]{2,1,0:T(8,128)S(1)}, u32[]{:S(2)}, u32[]{:S(2)}) collective-permute-start(f32[1,16,2048]{2,1,0:T(8,128)S(1)} %get-tuple-element.196), channel_id=1, source_target_pairs={{4,0},{8,4},{12,8},{16,12},{20,16},{24,20},{28,24},{5,1},{9,5},{13... | collective-permute-start | bytes 393224 | tf_op jit(solution)/shard_map/ppermute | solution.py:21
  2.3 3.0 %collective-permute-start = (f32[1,16,2048]{2,1,0:T(8,128)S(1)}, f32[1,16,2048]{2,1,0:T(8,128)S(1)}, u32[]{:S(2)}, u32[]{:S(2)}) collective-permute-start(f32[1,16,2048]{2,1,0:T(8,128)S(1)} %get-tuple-element.197), channel_id=1, source_target_pairs={{0,4},{4,8},{8,12},{12,16},{16,20},{20,24},{24,28},{1,5},{5,9},{9,... | collective-permute-start | bytes 393224 | tf_op jit(solution)/shard_map/ppermute | solution.py:20
  8.0 4.9 %collective-permute-start.2 = (f32[6,1,2048]{2,1,0:T(1,128)S(1)}, f32[6,1,2048]{2,1,0:T(1,128)S(1)}, u32[]{:S(2)}, u32[]{:S(2)}) collective-permute-start(f32[6,1,2048]{2,1,0:T(1,128)S(1)} %get-tuple-element.194), channel_id=1, source_target_pairs={{0,1},{1,2},{2,3},{4,5},{5,6},{6,7},{8,9},{9,10},{10,11},{12,13},{... | collective-permute-start | bytes 147464 | tf_op jit(solution)/shard_map/ppermute | solution.py:20
  12.9 1.3 %collective-permute-start.3 = (f32[6,1,2048]{2,1,0:T(1,128)S(1)}, f32[6,1,2048]{2,1,0:T(1,128)S(1)}, u32[]{:S(2)}, u32[]{:S(2)}) collective-permute-start(f32[6,1,2048]{2,1,0:T(1,128)S(1)} %get-tuple-element.195), channel_id=1, source_target_pairs={{1,0},{2,1},{3,2},{5,4},{6,5},{7,6},{9,8},{10,9},{11,10},{13,12},{... | collective-permute-start | bytes 147464 | tf_op jit(solution)/shard_map/ppermute | solution.py:21
  14.7 4.4 %collective-permute-done.3 = f32[6,1,2048]{2,1,0:T(1,128)S(1)} collective-permute-done((f32[6,1,2048]{2,1,0:T(1,128)S(1)}, f32[6,1,2048]{2,1,0:T(1,128)S(1)}, u32[]{:S(2)}, u32[]{:S(2)}) %collective-permute-start.3) | collective-permute-done | bytes 49184 | tf_op jit(solution)/shard_map/ppermute | solution.py:21
  19.7 65.6 %while.16 = (s32[]{:T(128)}, f32[3,32768]{1,0:T(4,128)S(1)}, f32[32768]{0:T(1024)}, s32[4]{0:T(128)S(1)}, f32[6,18,2050]{2,1,0:T(8,128)S(1)}, /*index=5*/f32[16,...) while((s32[]{:T(128)}, f32[3,32768]{1,0:T(4,128)S(1)}, ...), condition=%wide.region_3.4_spmd.clone, body=%wide.region_0.3_spmd.clone.sunk | while | flops 105480208 | bytes 23315676 | solution.py:92
  27.7 2.1 %convolution_bitcast_fusion.2 = f32[16,32768]{1,0:T(8,128)S(1)} fusion(f32[16,16]{1,0:T(8,128)S(1)} %get-tuple-element.304, f32[32768]{0:T(1024)S(1)} %bitcast.79), kind=kOutput, calls=%fused_computation.1.clone.1 | convolution fusion | flops 102760448 | bytes 2229248 | tf_op jit(solution)/shard_map/while/body/eval_jaxpr/dot_general | solution.py:38
  30.3 2.1 %reshape.152 = f32[4,3,32768]{2,1,0:T(4,128)} reshape(f32[12,32768]{1,0:T(8,128)S(1)} %bitcast.71) | data formatting | bytes 3145728 | tf_op jit(solution)/shard_map/while/body/eval_jaxpr/reshape | solution.py:48
  32.3 2.4 %multiply_reduce_fusion.2 = f32[3,32768]{1,0:T(4,128)S(1)} fusion(f32[4,3,32768]{2,1,0:T(4,128)} %reshape.152, f32[4,32768]{1,0:T(4,128)S(1)} %fusion.34), kind=kLoop, calls=%fused_computation.2.clone.1 | loop fusion | flops 688128 | bytes 2490368 | tf_op jit(solution)/shard_map/while/body/eval_jaxpr/reduce_sum | solution.py:47
  44.1 2.1 %convolution_bitcast_fusion.2 = f32[16,32768]{1,0:T(8,128)S(1)} fusion(f32[16,16]{1,0:T(8,128)S(1)} %get-tuple-element.304, f32[32768]{0:T(1024)S(1)} %bitcast.79), kind=kOutput, calls=%fused_computation.1.clone.1 | convolution fusion | flops 102760448 | bytes 2229248 | tf_op jit(solution)/shard_map/while/body/eval_jaxpr/dot_general | solution.py:38
  46.7 2.1 %reshape.152 = f32[4,3,32768]{2,1,0:T(4,128)} reshape(f32[12,32768]{1,0:T(8,128)S(1)} %bitcast.71) | data formatting | bytes 3145728 | tf_op jit(solution)/shard_map/while/body/eval_jaxpr/reshape | solution.py:48
  48.7 2.4 %multiply_reduce_fusion.2 = f32[3,32768]{1,0:T(4,128)S(1)} fusion(f32[4,3,32768]{2,1,0:T(4,128)} %reshape.152, f32[4,32768]{1,0:T(4,128)S(1)} %fusion.34), kind=kLoop, calls=%fused_computation.2.clone.1 | loop fusion | flops 688128 | bytes 2490368 | tf_op jit(solution)/shard_map/while/body/eval_jaxpr/reduce_sum | solution.py:47
  60.5 2.1 %convolution_bitcast_fusion.2 = f32[16,32768]{1,0:T(8,128)S(1)} fusion(f32[16,16]{1,0:T(8,128)S(1)} %get-tuple-element.304, f32[32768]{0:T(1024)S(1)} %bitcast.79), kind=kOutput, calls=%fused_computation.1.clone.1 | convolution fusion | flops 102760448 | bytes 2229248 | tf_op jit(solution)/shard_map/while/body/eval_jaxpr/dot_general | solution.py:38
  63.0 2.1 %reshape.152 = f32[4,3,32768]{2,1,0:T(4,128)} reshape(f32[12,32768]{1,0:T(8,128)S(1)} %bitcast.71) | data formatting | bytes 3145728 | tf_op jit(solution)/shard_map/while/body/eval_jaxpr/reshape | solution.py:48
  65.1 2.4 %multiply_reduce_fusion.2 = f32[3,32768]{1,0:T(4,128)S(1)} fusion(f32[4,3,32768]{2,1,0:T(4,128)} %reshape.152, f32[4,32768]{1,0:T(4,128)S(1)} %fusion.34), kind=kLoop, calls=%fused_computation.2.clone.1 | loop fusion | flops 688128 | bytes 2490368 | tf_op jit(solution)/shard_map/while/body/eval_jaxpr/reduce_sum | solution.py:47
  76.8 2.1 %convolution_bitcast_fusion.2 = f32[16,32768]{1,0:T(8,128)S(1)} fusion(f32[16,16]{1,0:T(8,128)S(1)} %get-tuple-element.304, f32[32768]{0:T(1024)S(1)} %bitcast.79), kind=kOutput, calls=%fused_computation.1.clone.1 | convolution fusion | flops 102760448 | bytes 2229248 | tf_op jit(solution)/shard_map/while/body/eval_jaxpr/dot_general | solution.py:38
  79.4 2.1 %reshape.152 = f32[4,3,32768]{2,1,0:T(4,128)} reshape(f32[12,32768]{1,0:T(8,128)S(1)} %bitcast.71) | data formatting | bytes 3145728 | tf_op jit(solution)/shard_map/while/body/eval_jaxpr/reshape | solution.py:48
  81.5 2.4 %multiply_reduce_fusion.2 = f32[3,32768]{1,0:T(4,128)S(1)} fusion(f32[4,3,32768]{2,1,0:T(4,128)} %reshape.152, f32[4,32768]{1,0:T(4,128)S(1)} %fusion.34), kind=kLoop, calls=%fused_computation.2.clone.1 | loop fusion | flops 688128 | bytes 2490368 | tf_op jit(solution)/shard_map/while/body/eval_jaxpr/reduce_sum | solution.py:47
  86.5 3.1 %copy.13 = f32[4,16,2048]{1,0,2:T(4,128)} copy(f32[4,16,2048]{2,1,0:T(8,128)S(1)} %pad_maximum_fusion) | data formatting | bytes 1048576 | tf_op jit(solution)/shard_map/concatenate | solution.py:93
  89.6 4.7 %reshape.149 = f32[8,1,16384]{2,1,0:T(1,128)S(1)} reshape(f32[2048,4,16]{2,1,0:T(4,128)} %bitcast.75) | data formatting | bytes 1048576
  94.3 16.3 %all_to_all.15 = f32[8,1,16384]{2,1,0:T(1,128)S(1)} all-to-all(f32[8,1,16384]{2,1,0:T(1,128)S(1)} %reshape.149), channel_id=1, replica_groups=mesh['depth'=8,'strip'=4] {'depth'}, dimensions={0} | all-to-all | bytes 1048576 | tf_op jit(solution)/shard_map/all_to_all | solution.py:99
  111.2 1.9 %reduce = f32[8,16384]{1,0:T(8,128)S(1)} reduce(f32[8,1,16384]{2,1,0:T(1,128)S(1)} %all_to_all.15, f32[]{:T(128)} %broadcast.229), dimensions={1}, to_apply=%all_to_all.11.reduce_sub_computation | reduce | bytes 1048580 | tf_op jit(solution)/shard_map/all_to_all | solution.py:99
  113.0 4.9 %reshape.150 = f32[2048,4,16]{2,1,0:T(4,128)} reshape(f32[8,16384]{1,0:T(8,128)S(1)} %reduce) | data formatting | bytes 1048576
  117.9 2.8 %copy.16 = f32[4,16,8,256]{3,2,1,0:T(8,128)S(1)} copy(f32[4,16,8,256]{1,0,3,2:T(4,128)} %bitcast.76) | data formatting | bytes 1048576 | tf_op jit(solution)/shard_map/all_to_all | solution.py:99
  (138 shorter events, 24.7 us)
Async XLA Ops:
  0.0 14.2 %copy-start.4 = (f32[4,16]{1,0:T(4,128)S(1)}, f32[4,16]{1,0:T(4,128)}, u32[]{:S(2)}) copy-start(f32[4,16]{1,0:T(4,128)} %param.11) | copy-start | bytes 772
  1.0 6.9 %collective-permute-start.1 = (f32[1,16,2048]{2,1,0:T(8,128)S(1)}, f32[1,16,2048]{2,1,0:T(8,128)S(1)}, u32[]{:S(2)}, u32[]{:S(2)}) collective-permute-start(f32[1,16,2048]{2,1,0:T(8,128)S(1)} %get-tuple-element.196), channel_id=1, source_target_pairs={{4,0},{8,4},{12,8},{16,12},{20,16},{24,20},{28,24},{5,1},{9,5},{13... | collective-permute-start | bytes 393224 | tf_op jit(solution)/shard_map/ppermute | solution.py:21
  2.3 4.5 %collective-permute-start = (f32[1,16,2048]{2,1,0:T(8,128)S(1)}, f32[1,16,2048]{2,1,0:T(8,128)S(1)}, u32[]{:S(2)}, u32[]{:S(2)}) collective-permute-start(f32[1,16,2048]{2,1,0:T(8,128)S(1)} %get-tuple-element.197), channel_id=1, source_target_pairs={{0,4},{4,8},{8,12},{12,16},{16,20},{20,24},{24,28},{1,5},{5,9},{9,... | collective-permute-start | bytes 393224 | tf_op jit(solution)/shard_map/ppermute | solution.py:20
  8.0 6.7 %collective-permute-start.2 = (f32[6,1,2048]{2,1,0:T(1,128)S(1)}, f32[6,1,2048]{2,1,0:T(1,128)S(1)}, u32[]{:S(2)}, u32[]{:S(2)}) collective-permute-start(f32[6,1,2048]{2,1,0:T(1,128)S(1)} %get-tuple-element.194), channel_id=1, source_target_pairs={{0,1},{1,2},{2,3},{4,5},{5,6},{6,7},{8,9},{9,10},{10,11},{12,13},{... | collective-permute-start | bytes 147464 | tf_op jit(solution)/shard_map/ppermute | solution.py:20
  12.9 6.2 %collective-permute-start.3 = (f32[6,1,2048]{2,1,0:T(1,128)S(1)}, f32[6,1,2048]{2,1,0:T(1,128)S(1)}, u32[]{:S(2)}, u32[]{:S(2)}) collective-permute-start(f32[6,1,2048]{2,1,0:T(1,128)S(1)} %get-tuple-element.195), channel_id=1, source_target_pairs={{1,0},{2,1},{3,2},{5,4},{6,5},{7,6},{9,8},{10,9},{11,10},{13,12},{... | collective-permute-start | bytes 147464 | tf_op jit(solution)/shard_map/ppermute | solution.py:21
  19.7 7.4 %copy-start.5 = (s32[4]{0:T(128)}, s32[4]{0:T(128)S(1)}, u32[]{:S(2)}) copy-start(s32[4]{0:T(128)S(1)} %get-tuple-element.302) | copy-start | bytes 52 | tf_op jit(solution)/shard_map/while
  19.7 7.9 %copy-start = (f32[6,18,2050]{2,1,0:T(8,128)}, f32[6,18,2050]{2,1,0:T(8,128)S(1)}, u32[]{:S(2)}) copy-start(f32[6,18,2050]{2,1,0:T(8,128)S(1)} %get-tuple-element.303) | copy-start | bytes 2656804 | tf_op jit(solution)/shard_map/while
  32.3 2.5 %copy-start.2 = (f32[32768]{0:T(1024)S(1)}, f32[32768]{0:T(1024)}, u32[]{:S(2)}) copy-start(f32[32768]{0:T(1024)} %get-tuple-element.286) | copy-start | bytes 393220 | tf_op jit(solution)/shard_map/while
  34.8 1.3 %copy-start.1 = (f32[6,18,2050]{2,1,0:T(8,128)S(1)}, f32[6,18,2050]{2,1,0:T(8,128)}, u32[]{:S(2)}) copy-start(f32[6,18,2050]{2,1,0:T(8,128)} %copy-done) | copy-start | bytes 2656804 | tf_op jit(solution)/shard_map/while
  34.8 1.3 %copy-start.6 = (s32[4]{0:T(128)S(1)}, s32[4]{0:T(128)}, u32[]{:S(2)}) copy-start(s32[4]{0:T(128)} %copy-done.5) | copy-start | bytes 52 | tf_op jit(solution)/shard_map/while
  36.1 7.4 %copy-start.5 = (s32[4]{0:T(128)}, s32[4]{0:T(128)S(1)}, u32[]{:S(2)}) copy-start(s32[4]{0:T(128)S(1)} %get-tuple-element.302) | copy-start | bytes 52 | tf_op jit(solution)/shard_map/while
  36.1 7.9 %copy-start = (f32[6,18,2050]{2,1,0:T(8,128)}, f32[6,18,2050]{2,1,0:T(8,128)S(1)}, u32[]{:S(2)}) copy-start(f32[6,18,2050]{2,1,0:T(8,128)S(1)} %get-tuple-element.303) | copy-start | bytes 2656804 | tf_op jit(solution)/shard_map/while
  48.7 2.5 %copy-start.2 = (f32[32768]{0:T(1024)S(1)}, f32[32768]{0:T(1024)}, u32[]{:S(2)}) copy-start(f32[32768]{0:T(1024)} %get-tuple-element.286) | copy-start | bytes 393220 | tf_op jit(solution)/shard_map/while
  51.2 1.3 %copy-start.1 = (f32[6,18,2050]{2,1,0:T(8,128)S(1)}, f32[6,18,2050]{2,1,0:T(8,128)}, u32[]{:S(2)}) copy-start(f32[6,18,2050]{2,1,0:T(8,128)} %copy-done) | copy-start | bytes 2656804 | tf_op jit(solution)/shard_map/while
  51.2 1.3 %copy-start.6 = (s32[4]{0:T(128)S(1)}, s32[4]{0:T(128)}, u32[]{:S(2)}) copy-start(s32[4]{0:T(128)} %copy-done.5) | copy-start | bytes 52 | tf_op jit(solution)/shard_map/while
  52.5 7.4 %copy-start.5 = (s32[4]{0:T(128)}, s32[4]{0:T(128)S(1)}, u32[]{:S(2)}) copy-start(s32[4]{0:T(128)S(1)} %get-tuple-element.302) | copy-start | bytes 52 | tf_op jit(solution)/shard_map/while
  52.5 7.9 %copy-start = (f32[6,18,2050]{2,1,0:T(8,128)}, f32[6,18,2050]{2,1,0:T(8,128)S(1)}, u32[]{:S(2)}) copy-start(f32[6,18,2050]{2,1,0:T(8,128)S(1)} %get-tuple-element.303) | copy-start | bytes 2656804 | tf_op jit(solution)/shard_map/while
  65.1 2.5 %copy-start.2 = (f32[32768]{0:T(1024)S(1)}, f32[32768]{0:T(1024)}, u32[]{:S(2)}) copy-start(f32[32768]{0:T(1024)} %get-tuple-element.286) | copy-start | bytes 393220 | tf_op jit(solution)/shard_map/while
  67.6 1.3 %copy-start.1 = (f32[6,18,2050]{2,1,0:T(8,128)S(1)}, f32[6,18,2050]{2,1,0:T(8,128)}, u32[]{:S(2)}) copy-start(f32[6,18,2050]{2,1,0:T(8,128)} %copy-done) | copy-start | bytes 2656804 | tf_op jit(solution)/shard_map/while
  67.6 1.3 %copy-start.6 = (s32[4]{0:T(128)S(1)}, s32[4]{0:T(128)}, u32[]{:S(2)}) copy-start(s32[4]{0:T(128)} %copy-done.5) | copy-start | bytes 52 | tf_op jit(solution)/shard_map/while
  68.9 7.4 %copy-start.5 = (s32[4]{0:T(128)}, s32[4]{0:T(128)S(1)}, u32[]{:S(2)}) copy-start(s32[4]{0:T(128)S(1)} %get-tuple-element.302) | copy-start | bytes 52 | tf_op jit(solution)/shard_map/while
  68.9 7.9 %copy-start = (f32[6,18,2050]{2,1,0:T(8,128)}, f32[6,18,2050]{2,1,0:T(8,128)S(1)}, u32[]{:S(2)}) copy-start(f32[6,18,2050]{2,1,0:T(8,128)S(1)} %get-tuple-element.303) | copy-start | bytes 2656804 | tf_op jit(solution)/shard_map/while
  81.5 2.5 %copy-start.2 = (f32[32768]{0:T(1024)S(1)}, f32[32768]{0:T(1024)}, u32[]{:S(2)}) copy-start(f32[32768]{0:T(1024)} %get-tuple-element.286) | copy-start | bytes 393220 | tf_op jit(solution)/shard_map/while
  84.0 1.3 %copy-start.1 = (f32[6,18,2050]{2,1,0:T(8,128)S(1)}, f32[6,18,2050]{2,1,0:T(8,128)}, u32[]{:S(2)}) copy-start(f32[6,18,2050]{2,1,0:T(8,128)} %copy-done) | copy-start | bytes 2656804 | tf_op jit(solution)/shard_map/while
  (5 other events, 4.0 us)
where the time goes:
time: 124 us; the launch traced here: 123 us
  local copies, waits for them, and re-layouts  40.4 us (33%)
  loops' own time  23 us (19%)
  other arithmetic  19.3 us (16%)
  blocking collectives  16.3 us (13%)
  starting transfers between devices  10.6 us (9%)
  matrix products  8.57 us (7%)
  waiting for transfers between devices  4.83 us (4%)
    another operation x1, loops' own time, on_device(): lax.scan(advance, start, jnp.arange(slab_depth, dtype=jnp.int32))  23 us
    all_to_all x1, blocking collectives, on_device(): lax.all_to_all(partial_value, 'depth', split_axis=2, concat_axis=1, tiled...  16.3 us
    unnamed x10, local copies, waits for them, and re-layouts  11.6 us
    reduce_sum x4, other arithmetic, shade_slice(): jnp.sum(looked[:3 * material_count].reshape(material_count, 3, -1) * oneh...  9.79 us
    dot_general x4, matrix products, shade_slice(): jnp.dot(knot_table, tent_weights, precision=lax.Precision.HIGHEST, prefer...  8.57 us
    reshape x4, local copies, waits for them, and re-layouts, shade_slice(): looked[:3 * material_count].reshape(material_count, 3, -1)  8.24 us
    ppermute x2, starting transfers between devices, with_halo(): before = lax.ppermute(last, axis, up)  7.97 us
    while x72, local copies, waits for them, and re-layouts  7.4 us
  transfers between devices with their start and end apart: 4, of which 2 were waited for; matrix products, arithmetic and copies ran while one was open for 2% of the time, Pallas kernels for 0%

commit v1 on v0

v1 whole, which is shorter than its diff:
```python
import functools

import jax
import jax.numpy as jnp
from jax import lax
from jax.experimental import pallas as pl
from jax.experimental.pallas import tpu as pltpu
from jax.sharding import PartitionSpec as P

ambient = 0.3
diffuse = 0.7
LANES = 128
ROWS = 8


def neighbours(count, first):
    pairs = []
    for low in range(first, count - 1, 2):
        pairs += [(low, low + 1), (low + 1, low)]
    return pairs


def halo(first, last, axis, exchange):
    count = lax.axis_size(axis)
    odd = lax.axis_index(axis) % 2 == 1
    inner = lax.ppermute(jnp.where(odd, first, last), axis, neighbours(count, 0))
    outer = lax.ppermute(jnp.where(odd, last, first), axis, neighbours(count, 1))
    return jnp.where(odd, inner, outer), jnp.where(odd, outer, inner)


def shade_kernel(tile_of, flags, density, materials, before, after, above, below, tables, out):
    slices, rows, columns = density.shape
    tiles = columns // LANES
    knots = tables.shape[1] // 8
    lane = lax.broadcasted_iota(jnp.int32, (ROWS, LANES), 1)
    row = lax.broadcasted_iota(jnp.int32, (ROWS, LANES), 0)
    table = [jnp.broadcast_to(tables[i : i + 1, :], (ROWS, LANES)) for i in range(4)]
    bands = rows // ROWS

    def body(i, _):
        c = tile_of[i]
        here = pl.ds(pl.multiple_of(c * LANES, LANES), LANES)
        left = pl.ds(pl.multiple_of(jnp.maximum(c - 1, 0) * LANES, LANES), LANES)
        right = pl.ds(pl.multiple_of(jnp.minimum(c + 1, tiles - 1) * LANES, LANES), LANES)
        has_left = jnp.where(c > 0, 1.0, 0.0)
        has_right = jnp.where(c < tiles - 1, 1.0, 0.0)
        occupied = flags[c].astype(jnp.float32)
        d = [[density[z, b * ROWS : (b + 1) * ROWS, here] for b in range(bands)] for z in range(slices)]
        radiance = [[None] * 3 for _ in range(bands)]
        transmit = [None] * bands
        for z in range(slices):
            up = [pltpu.roll(v, ROWS - 1, 0) for v in d[z]]
            down = [pltpu.roll(v, 1, 0) for v in d[z]]
            for b in range(bands):
                v = d[z][b]
                band = slice(b * ROWS, (b + 1) * ROWS)
                nearer = before[0, band, here] if z == 0 else d[z - 1][b]
                farther = after[0, band, here] if z == slices - 1 else d[z + 1][b]
                dz = farther - nearer
                top = down[b - 1] if b else jnp.broadcast_to(above[z, :, here], (ROWS, LANES))
                bottom = (
                    up[b + 1] if b < bands - 1 else jnp.broadcast_to(below[z, :, here], (ROWS, LANES))
                )
                dy = jnp.where(row == ROWS - 1, bottom, up[b]) - jnp.where(row == 0, top, down[b])
                vl = density[z, band, left] * has_left
                vr = density[z, band, right] * has_right
                dx = jnp.where(
                    lane == LANES - 1, pltpu.roll(vr, LANES - 1, 1), pltpu.roll(v, LANES - 1, 1)
                ) - jnp.where(lane == 0, pltpu.roll(vl, 1, 1), pltpu.roll(v, 1, 1))
                facing = jnp.abs(dx + 2.0 * (dy + dz))
                lighting = ambient + (diffuse / 3.0) * facing * lax.rsqrt(
                    4.0 + (dx * dx + dy * dy + dz * dz)
                )
                position = jnp.clip((v + 3.0) * ((knots - 1) / 6.0), 0.0, knots - 1.0)
                whole = position.astype(jnp.int32)
                part = position - whole.astype(jnp.float32)
                index = materials[z, band, here] * knots + whole
                slope_index = index + LANES // 2

                def look(t):
                    base = jnp.take_along_axis(t, index, axis=1, mode="promise_in_bounds")
                    slope = jnp.take_along_axis(t, slope_index, axis=1, mode="promise_in_bounds")
                    return base + part * slope

                rate = look(table[3]) * occupied
                clear = jnp.exp(-rate)
                weight = lighting * (1.0 - clear)
                if z:
                    weight = weight * transmit[b]
                for ch in range(3):
                    term = look(table[ch]) * weight
                    radiance[b][ch] = radiance[b][ch] + term if z else term
                transmit[b] = transmit[b] * clear if z else clear
        for b in range(bands):
            band = slice(b * ROWS, (b + 1) * ROWS)
            for ch in range(3):
                out[i, ch, band, :] = radiance[b][ch]
            out[i, 3, band, :] = transmit[b]
        return 0

    lax.fori_loop(0, out.shape[0], body, 0)


def shade(tile_of, flags, density, materials, before, after, above, below, tables):
    rows = density.shape[1]
    count = tile_of.shape[0]
    smem = pl.BlockSpec(memory_space=pltpu.SMEM)
    vmem = pl.BlockSpec(memory_space=pltpu.VMEM)
    return pl.pallas_call(
        shade_kernel,
        out_shape=jax.ShapeDtypeStruct((count, 4, rows, LANES), jnp.float32),
        in_specs=[smem, smem] + [vmem] * 7,
        out_specs=vmem,
        compiler_params=pltpu.CompilerParams(vmem_limit_bytes=16 * 1024 * 1024),
    )(tile_of, flags, density, materials, before, after, above, below, tables)


def composite_over(nearer, farther):
    return jnp.concatenate(
        [nearer[:, :3] + nearer[:, 3:] * farther[:, :3], nearer[:, 3:] * farther[:, 3:]], axis=1
    )


def lookup_tables(tf_color, tf_opacity):
    values = jnp.concatenate([tf_color.transpose(1, 0, 2), tf_opacity[None]], axis=0)
    steps = jnp.pad(values[:, :, 1:] - values[:, :, :-1], ((0, 0), (0, 0), (0, 1)))
    lanes = jnp.concatenate([values, steps], axis=1)
    return lanes.reshape(4, -1)


def on_device(density, materials, occupancy_flags, tf_color, tf_opacity):
    slices, rows, columns = density.shape
    before, after = halo(density[:1], density[-1:], "depth", None)
    above, below = halo(density[:, :1], density[:, -1:], "strip", None)
    tables = lookup_tables(tf_color, tf_opacity)
    tiles = columns // LANES
    groups = lax.axis_size("depth")
    width = columns // groups
    flags = occupancy_flags[0, 0]
    partial_value = shade(
        jnp.arange(tiles, dtype=jnp.int32), flags, density, materials, before, after, above, below, tables
    )
    if width % LANES == 0:
        pieces = lax.all_to_all(partial_value, "depth", split_axis=0, concat_axis=0, tiled=True)
        pieces = pieces.reshape(groups, width // LANES, 4, rows, LANES)
        pieces = pieces.transpose(0, 2, 3, 1, 4).reshape(groups, 4, rows, width)
    else:
        natural = partial_value.transpose(1, 2, 0, 3).reshape(4, rows, groups, width)
        pieces = lax.all_to_all(
            natural.transpose(2, 0, 1, 3), "depth", split_axis=0, concat_axis=0, tiled=True
        )
    while pieces.shape[0] > 1:
        pieces = composite_over(pieces[0::2], pieces[1::2])
    finished = pieces[0]
    return jnp.concatenate([finished[:3], 1.0 - finished[3:]], axis=0)


def solution(mesh):
    placed = (
        P("depth", "strip", None),
        P("depth", "strip", None),
        P("depth", "strip", None),
        P(),
        P(),
    )
    return jax.shard_map(
        on_device, mesh=mesh, in_specs=placed, out_specs=P(None, "strip", "depth"), check_vma=False
    )
```

time: 124 us -> 35.6 us (0.29)
  local copies, waits for them, and re-layouts: 40.4 us -> 0.83 us
  loops' own time: 23 us -> 0 us
  other arithmetic: 19.3 us -> 3.06 us
  matrix products: 8.57 us -> 0 us
  Pallas kernels: 0 us -> 4.65 us
  waiting for transfers between devices: 4.83 us -> 0.74 us
    another operation x1 -> x0, loops' own time: 23 us -> none  [on_device(): lax.scan(advance, start, jnp.arange(slab_depth, dtype=jnp.int32))]
    reduce_sum x8 -> x0, other arithmetic: 11.5 us -> none  [the longest x4 9.79 us: shade_slice(): jnp.sum(looked[:3 * material_count].reshape(material_count, 3, -1) * oneh...]
    unnamed x10, local copies, waits for them, and re-layouts: 11.6 us -> 0.65 us
    dot_general x4 -> x0, matrix products: 8.57 us -> none  [shade_slice(): jnp.dot(knot_table, tent_weights, precision=lax.Precision.HIGHEST, prefer...]
    reshape x5 -> x2, local copies, waits for them, and re-layouts: 8.25 us -> 0.13 us  [the longest x1 0.08 us: lookup_tables(): return lanes.reshape(4, -1)]
    while x72 -> x0, local copies, waits for them, and re-layouts: 7.4 us -> none
    pallas_call x0 -> x1, Pallas kernels: none -> 4.65 us  [shade(): pl.pallas_call(shade_kernel, out_shape=jax.ShapeDtypeStruct((count, 4, ro...]
    ppermute x4, waiting for transfers between devices: 4.83 us -> 0.74 us  [the longest x2 0.73 us: halo(): lax.ppermute(jnp.where(odd, first, last), axis, neighbours(count, 0))]
  transfers between devices with their start and end apart: 4 -> 4, of which waited for: 2 -> 1; matrix products, arithmetic and copies ran while one was open for 2% -> 4% of each run, Pallas kernels for 0% -> 0%
where the time goes in v1:
time: 35.6 us; the launch traced here: 35.4 us
  blocking collectives  15.8 us (44%)
  starting transfers between devices  10.2 us (29%)
  Pallas kernels  4.65 us (13%)
  other arithmetic  3.06 us (9%)
  local copies, waits for them, and re-layouts  0.83 us (2%)
  waiting for transfers between devices  0.74 us (2%)
    all_to_all x1, blocking collectives, on_device(): lax.all_to_all(partial_value, 'depth', split_axis=0, concat_axis=0, tiled...  15.8 us
    ppermute x2, starting transfers between devices, halo(): lax.ppermute(jnp.where(odd, first, last), axis, neighbours(count, 0))  8.82 us
    pallas_call x1, Pallas kernels, shade(): pl.pallas_call(shade_kernel, out_shape=jax.ShapeDtypeStruct((count, 4, ro...  4.65 us
    select_n x2, other arithmetic, halo(): jnp.where(odd, last, first)  2.16 us
    ppermute x2, starting transfers between devices, halo(): lax.ppermute(jnp.where(odd, last, first), axis, neighbours(count, 1))  1.33 us
    ppermute x2, waiting for transfers between devices, halo(): lax.ppermute(jnp.where(odd, first, last), axis, neighbours(count, 0))  0.73 us
  transfers between devices with their start and end apart: 4, of which 1 were waited for; matrix products, arithmetic and copies ran while one was open for 4% of the time, Pallas kernels for 0%

profile of v1, /device:TPU:0, one launch (start us, length us, event | category | flops | bytes accessed | tf_op | source)
XLA Modules:
  0.0 35.4 jit_solution(10145116132178915022)
XLA Ops:
  0.0 1.1 %broadcast_select_fusion.2 = (f32[4,1,2048]{2,1,0:T(1,128)S(1)}, f32[4,1,2048]{2,1,0:T(1,128)S(1)}) fusion(pred[]{:T(512)S(6)} %eq.10, f32[4,16,2048]{2,1,0:T(8,128)} %density.1), kind=kLoop, calls=%fused_computation.12 | loop fusion | flops 16384 | bytes 131073 | tf_op jit(solution)/shard_map/jit(_where)/select_n | solution.py:27
  1.1 0.7 %collective-permute-start.3 = (f32[4,1,2048]{2,1,0:T(1,128)S(1)}, f32[4,1,2048]{2,1,0:T(1,128)S(1)}, u32[]{:S(2)}, u32[]{:S(2)}) collective-permute-start(f32[4,1,2048]{2,1,0:T(1,128)S(1)} %get-tuple-element.7), channel_id=1, source_target_pairs={{1,2},{2,1},{5,6},{6,5},{9,10},{10,9},{13,14},{14,13},{17,18},{18,... | collective-permute-start | bytes 98312 | tf_op jit(solution)/shard_map/ppermute | solution.py:27
  1.8 5.9 %collective-permute-start.2 = (f32[4,1,2048]{2,1,0:T(1,128)S(1)}, f32[4,1,2048]{2,1,0:T(1,128)S(1)}, u32[]{:S(2)}, u32[]{:S(2)}) collective-permute-start(f32[4,1,2048]{2,1,0:T(1,128)S(1)} %get-tuple-element.8), channel_id=1, source_target_pairs={{0,1},{1,0},{2,3},{3,2},{4,5},{5,4},{6,7},{7,6},{8,9},{9,8},{10,11... | collective-permute-start | bytes 98312 | tf_op jit(solution)/shard_map/ppermute | solution.py:26
  7.7 0.0 copy-start.4
  7.7 0.0 copy-start.3
  7.7 1.1 %slice_select_fusion = (f32[1,16,2048]{2,1,0:T(8,128)S(1)}, f32[1,16,2048]{2,1,0:T(8,128)S(1)}) fusion(f32[4,16,2048]{2,1,0:T(8,128)} %density.1, pred[]{:T(512)S(6)} %eq.9), kind=kLoop, calls=%fused_computation.4 | loop fusion | flops 65536 | bytes 524289 | tf_op jit(solution)/shard_map/jit(_where)/select_n | solution.py:27
  8.8 0.7 %collective-permute-start.1 = (f32[1,16,2048]{2,1,0:T(8,128)S(1)}, f32[1,16,2048]{2,1,0:T(8,128)S(1)}, u32[]{:S(2)}, u32[]{:S(2)}) collective-permute-start(f32[1,16,2048]{2,1,0:T(8,128)S(1)} %get-tuple-element.9), channel_id=1, source_target_pairs={{4,8},{8,4},{12,16},{16,12},{20,24},{24,20},{5,9},{9,5},{13,17},{1... | collective-permute-start | bytes 393224 | tf_op jit(solution)/shard_map/ppermute | solution.py:27
  9.4 2.9 %collective-permute-start = (f32[1,16,2048]{2,1,0:T(8,128)S(1)}, f32[1,16,2048]{2,1,0:T(8,128)S(1)}, u32[]{:S(2)}, u32[]{:S(2)}) collective-permute-start(f32[1,16,2048]{2,1,0:T(8,128)S(1)} %get-tuple-element.10), channel_id=1, source_target_pairs={{0,4},{4,0},{8,12},{12,8},{16,20},{20,16},{24,28},{28,24},{1,5},{5... | collective-permute-start | bytes 393224 | tf_op jit(solution)/shard_map/ppermute | solution.py:26
  12.3 0.0 copy-done.4
  12.3 0.0 copy-done.3
  12.3 0.1 fusion.6
  12.4 0.1 reshape.27.tables
  12.5 0.0 collective-permute-done.3
  12.5 0.0 collective-permute-done.2
  12.6 0.0 collective-permute-done.1
  12.6 0.7 %collective-permute-done = f32[1,16,2048]{2,1,0:T(8,128)S(1)} collective-permute-done((f32[1,16,2048]{2,1,0:T(8,128)S(1)}, f32[1,16,2048]{2,1,0:T(8,128)S(1)}, u32[]{:S(2)}, u32[]{:S(2)}) %collective-permute-start) | collective-permute-done | bytes 131104 | tf_op jit(solution)/shard_map/ppermute | solution.py:26
  13.4 0.0 copy-start.2
  13.4 0.0 copy-done
  13.4 0.0 copy-done.1
  13.4 0.6 %copy-done.2 = s32[1,1,16]{2,1,0:T(1,128)S(1)} copy-done((s32[1,1,16]{2,1,0:T(1,128)S(1)}, s32[1,1,16]{2,1,0:T(1,128)}, u32[]{:S(2)}) %copy-start.2) | copy-done | bytes 88
  14.0 4.6 %shard_map.55 = f32[16,4,16,128]{3,2,1,0:T(8,128)S(1)} custom-call(s32[16]{0:T(128)S(1)} %iota.3.tile_of, s32[16]{0:T(128)S(1)} %bitcast.20, f32[4,16,2048]{2,1,0:T(8,128)S(1)} %copy-done, s32[4,16,2048]{2,1,0:T(8,128)S(1)} %copy-done.1, f32[1,16,2048]{2,1,0:T(8,128)S(1)} %get-tuple-element.16.before, f32[1,16,2048]{2,1,0:T(8,128)S(1)} %get-tuple-element.15.after, ...), custom_call_target="tpu_custom_call" | custom-call | tf_op jit(solution)/shard_map/pallas_call | solution.py:109
  18.7 15.8 %all_to_all.5 = f32[16,4,16,128]{3,2,1,0:T(8,128)S(1)} all-to-all(f32[16,4,16,128]{3,2,1,0:T(8,128)S(1)} %shard_map.55), channel_id=1, replica_groups=mesh['depth'=8,'strip'=4] {'depth'}, dimensions={0} | all-to-all | bytes 1048576 | tf_op jit(solution)/shard_map/all_to_all | solution.py:144
  34.5 0.1 copy.9
  34.7 0.6 %pad_maximum_fusion.1 = f32[4,16,256]{2,1,0:T(8,128)} fusion(f32[1,16,256]{2,1,0:T(8,128)S(1)} %get-tuple-element.22, f32[3,16,256]{2,1,0:T(8,128)S(1)} %fusion.3), kind=kLoop, calls=%fused_computation.9 | loop fusion | flops 16384 | bytes 131072 | tf_op jit(solution)/shard_map/concatenate | solution.py:155
  (15 shorter events, 0.3 us)
Async XLA Ops:
  1.1 11.4 %collective-permute-start.3 = (f32[4,1,2048]{2,1,0:T(1,128)S(1)}, f32[4,1,2048]{2,1,0:T(1,128)S(1)}, u32[]{:S(2)}, u32[]{:S(2)}) collective-permute-start(f32[4,1,2048]{2,1,0:T(1,128)S(1)} %get-tuple-element.7), channel_id=1, source_target_pairs={{1,2},{2,1},{5,6},{6,5},{9,10},{10,9},{13,14},{14,13},{17,18},{18,... | collective-permute-start | bytes 98312 | tf_op jit(solution)/shard_map/ppermute | solution.py:27
  1.8 10.8 %collective-permute-start.2 = (f32[4,1,2048]{2,1,0:T(1,128)S(1)}, f32[4,1,2048]{2,1,0:T(1,128)S(1)}, u32[]{:S(2)}, u32[]{:S(2)}) collective-permute-start(f32[4,1,2048]{2,1,0:T(1,128)S(1)} %get-tuple-element.8), channel_id=1, source_target_pairs={{0,1},{1,0},{2,3},{3,2},{4,5},{5,4},{6,7},{7,6},{8,9},{9,8},{10,11... | collective-permute-start | bytes 98312 | tf_op jit(solution)/shard_map/ppermute | solution.py:26
  7.7 4.7 %copy-start.4 = (f32[4,16]{1,0:T(4,128)S(1)}, f32[4,16]{1,0:T(4,128)}, u32[]{:S(2)}) copy-start(f32[4,16]{1,0:T(4,128)} %param.9) | copy-start | bytes 772
  7.7 4.7 %copy-start.3 = (f32[4,3,16]{2,0,1:T(4,128)S(1)}, f32[4,3,16]{2,0,1:T(4,128)}, u32[]{:S(2)}) copy-start(f32[4,3,16]{2,0,1:T(4,128)} %param.8) | copy-start | bytes 2308
  7.7 5.7 %copy-start = (f32[4,16,2048]{2,1,0:T(8,128)S(1)}, f32[4,16,2048]{2,1,0:T(8,128)}, u32[]{:S(2)}) copy-start(f32[4,16,2048]{2,1,0:T(8,128)} %density.1) | copy-start | bytes 1572868
  7.7 5.7 %copy-start.1 = (s32[4,16,2048]{2,1,0:T(8,128)S(1)}, s32[4,16,2048]{2,1,0:T(8,128)}, u32[]{:S(2)}) copy-start(s32[4,16,2048]{2,1,0:T(8,128)} %materials.1) | copy-start | bytes 1572868
  8.8 3.8 %collective-permute-start.1 = (f32[1,16,2048]{2,1,0:T(8,128)S(1)}, f32[1,16,2048]{2,1,0:T(8,128)S(1)}, u32[]{:S(2)}, u32[]{:S(2)}) collective-permute-start(f32[1,16,2048]{2,1,0:T(8,128)S(1)} %get-tuple-element.9), channel_id=1, source_target_pairs={{4,8},{8,4},{12,16},{16,12},{20,24},{24,20},{5,9},{9,5},{13,17},{1... | collective-permute-start | bytes 393224 | tf_op jit(solution)/shard_map/ppermute | solution.py:27
  9.4 3.9 %collective-permute-start = (f32[1,16,2048]{2,1,0:T(8,128)S(1)}, f32[1,16,2048]{2,1,0:T(8,128)S(1)}, u32[]{:S(2)}, u32[]{:S(2)}) collective-permute-start(f32[1,16,2048]{2,1,0:T(8,128)S(1)} %get-tuple-element.10), channel_id=1, source_target_pairs={{0,4},{4,0},{8,12},{12,8},{16,20},{20,16},{24,28},{28,24},{1,5},{5... | collective-permute-start | bytes 393224 | tf_op jit(solution)/shard_map/ppermute | solution.py:26
  13.4 0.7 %copy-start.2 = (s32[1,1,16]{2,1,0:T(1,128)S(1)}, s32[1,1,16]{2,1,0:T(1,128)}, u32[]{:S(2)}) copy-start(s32[1,1,16]{2,1,0:T(1,128)} %param.7) | copy-start | bytes 196

commit v2 on v1

v2 whole, which is shorter than its diff:
```python
import functools

import jax
import jax.numpy as jnp
from jax import lax
from jax.experimental import pallas as pl
from jax.experimental.pallas import tpu as pltpu
from jax.sharding import PartitionSpec as P

ambient = 0.3
diffuse = 0.7
LANES = 128
ROWS = 8
VMEM = pl.BlockSpec(memory_space=pltpu.VMEM)
SMEM = pl.BlockSpec(memory_space=pltpu.SMEM)


def neighbours(count, first):
    pairs = []
    for low in range(first, count - 1, 2):
        pairs += [(low, low + 1), (low + 1, low)]
    return pairs


def sent_layers(first, last, axis):
    odd = lax.axis_index(axis) % 2 == 1
    return jnp.where(odd, first, last), jnp.where(odd, last, first)


def tile(c):
    return pl.ds(pl.multiple_of(c * LANES, LANES), LANES)


def call(kernel, out_shape, in_specs, cost):
    return pl.pallas_call(
        kernel,
        out_shape=out_shape,
        in_specs=in_specs,
        out_specs=jax.tree.map(lambda _: VMEM, out_shape),
        cost_estimate=pl.CostEstimate(flops=cost, bytes_accessed=cost, transcendentals=0),
        compiler_params=pltpu.CompilerParams(vmem_limit_bytes=16 * 1024 * 1024),
    )


def array(*shape):
    return jax.ShapeDtypeStruct(shape, jnp.float32)


def lookup_kernel(flags, density, materials, tables, out):
    slices, rows, columns = density.shape
    knots = tables.shape[1] // 8
    table = [jnp.broadcast_to(tables[i : i + 1, :], (ROWS, LANES)) for i in range(4)]

    def body(c, _):
        here = tile(c)
        occupied = flags[c].astype(jnp.float32)
        for b in range(rows // ROWS):
            band = slice(b * ROWS, (b + 1) * ROWS)
            transmit = None
            for z in range(slices):
                position = jnp.clip(
                    (density[z, band, here] + 3.0) * ((knots - 1) / 6.0), 0.0, knots - 1.0
                )
                whole = position.astype(jnp.int32)
                part = position - whole.astype(jnp.float32)
                index = materials[z, band, here] * knots + whole
                slope_index = index + LANES // 2

                def look(t):
                    base = jnp.take_along_axis(t, index, axis=1, mode="promise_in_bounds")
                    slope = jnp.take_along_axis(t, slope_index, axis=1, mode="promise_in_bounds")
                    return base + part * slope

                clear = jnp.exp(-(look(table[3]) * occupied))
                weight = 1.0 - clear
                if z:
                    weight = weight * transmit
                for ch in range(3):
                    out[c, z * 3 + ch, band, :] = look(table[ch]) * weight
                transmit = transmit * clear if z else clear
            out[c, slices * 3, band, :] = transmit
        return 0

    lax.fori_loop(0, columns // LANES, body, 0, unroll=4)


def shade_kernel(order, density, weights, near_z, far_z, near_y, far_y, out):
    slices, rows, columns = density.shape
    tiles = columns // LANES
    bands = rows // ROWS
    lane = lax.broadcasted_iota(jnp.int32, (ROWS, LANES), 1)
    row = lax.broadcasted_iota(jnp.int32, (ROWS, LANES), 0)
    odd_z = lax.axis_index("depth") % 2 == 1
    odd_y = lax.axis_index("strip") % 2 == 1

    def body(i, _):
        c = order(i)
        here, left, right = tile(c), tile(jnp.maximum(c - 1, 0)), tile(jnp.minimum(c + 1, tiles - 1))
        has_left = jnp.where(c > 0, 1.0, 0.0)
        has_right = jnp.where(c < tiles - 1, 1.0, 0.0)
        d = [[density[z, b * ROWS : (b + 1) * ROWS, here] for b in range(bands)] for z in range(slices)]
        for b in range(bands):
            band = slice(b * ROWS, (b + 1) * ROWS)
            radiance = [None] * 3
            for z in range(slices):
                v = d[z][b]
                if z == 0:
                    nearer = jnp.where(odd_z, near_z[0, band, here], far_z[0, band, here])
                else:
                    nearer = d[z - 1][b]
                if z == slices - 1:
                    farther = jnp.where(odd_z, far_z[0, band, here], near_z[0, band, here])
                else:
                    farther = d[z + 1][b]
                dz = farther - nearer
                if b == 0:
                    top = jnp.where(odd_y, near_y[z, :, here], far_y[z, :, here])
                    top = jnp.broadcast_to(top, (ROWS, LANES))
                else:
                    top = d[z][b - 1]
                if b == bands - 1:
                    bottom = jnp.where(odd_y, far_y[z, :, here], near_y[z, :, here])
                    bottom = jnp.broadcast_to(bottom, (ROWS, LANES))
                else:
                    bottom = d[z][b + 1]
                dy = pltpu.roll(jnp.where(row == 0, bottom, v), ROWS - 1, 0) - pltpu.roll(
                    jnp.where(row == ROWS - 1, top, v), 1, 0
                )
                vl = density[z, band, left] * has_left
                vr = density[z, band, right] * has_right
                dx = pltpu.roll(jnp.where(lane == 0, vr, v), LANES - 1, 1) - pltpu.roll(
                    jnp.where(lane == LANES - 1, vl, v), 1, 1
                )
                facing = jnp.abs(dx + 2.0 * (dy + dz))
                lighting = ambient + (diffuse / 3.0) * facing * lax.rsqrt(
                    4.0 + (dx * dx + dy * dy + dz * dz)
                )
                for ch in range(3):
                    term = weights[c, z * 3 + ch, band, :] * lighting
                    radiance[ch] = radiance[ch] + term if z else term
            for ch in range(3):
                out[i, ch, band, :] = radiance[ch]
            out[i, 3, band, :] = weights[c, slices * 3, band, :]
        return 0

    lax.fori_loop(0, out.shape[0], body, 0, unroll=2)


def over(swap, nearer, farther):
    first = [jnp.where(swap, f, n) for n, f in zip(nearer, farther)]
    second = [jnp.where(swap, n, f) for n, f in zip(nearer, farther)]
    return [first[ch] + first[3] * second[ch] for ch in range(3)] + [first[3] * second[3]]


def merge_kernel(kept, received, *outs):
    index = lax.axis_index("depth")
    odd = index % 2 == 1
    chip = index // 2
    per = outs[0].shape[0]
    for k, out in enumerate(outs):
        for h in range(per):
            at = (chip ^ k) * per + h
            mine = [kept[at, ch] for ch in range(4)]
            other = [received[at, ch] for ch in range(4)]
            for ch, value in enumerate(over(odd, mine, other)):
                out[h, ch] = value


def finish_kernel(*refs):
    pieces, out = refs[:-1], refs[-1]
    chip = lax.axis_index("depth") // 2
    for h in range(pieces[0].shape[0]):
        values = [[piece[h, ch] for ch in range(4)] for piece in pieces]
        bit = 0
        while len(values) > 1:
            swap = (chip >> bit) % 2 == 1
            values = [over(swap, values[k], values[k + 1]) for k in range(0, len(values), 2)]
            bit += 1
        here = slice(h * LANES, (h + 1) * LANES)
        for ch in range(3):
            out[ch, :, here] = values[0][ch]
        out[3, :, here] = 1.0 - values[0][3]


def composite_over(nearer, farther):
    return jnp.concatenate(
        [nearer[:, :3] + nearer[:, 3:] * farther[:, :3], nearer[:, 3:] * farther[:, 3:]], axis=1
    )


def lookup_tables(tf_color, tf_opacity):
    values = jnp.concatenate([tf_color.transpose(1, 0, 2), tf_opacity[None]], axis=0)
    steps = jnp.pad(values[:, :, 1:] - values[:, :, :-1], ((0, 0), (0, 0), (0, 1)))
    lanes = jnp.concatenate([values, steps], axis=1)
    return lanes.reshape(4, -1)


def on_device(density, materials, occupancy_flags, tf_color, tf_opacity):
    slices, rows, columns = density.shape
    tiles = columns // LANES
    groups, strips = lax.axis_size("depth"), lax.axis_size("strip")
    width = columns // groups
    chips = groups // 2

    inner, outer = sent_layers(density[:1], density[-1:], "depth")
    far_z = lax.ppermute(outer, "depth", neighbours(groups, 1))
    inner_y, outer_y = sent_layers(density[:, :1], density[:, -1:], "strip")
    near_y = lax.ppermute(inner_y, "strip", neighbours(strips, 0))
    far_y = lax.ppermute(outer_y, "strip", neighbours(strips, 1))
    near_z = lax.ppermute(inner, "depth", neighbours(groups, 0))

    tables = lookup_tables(tf_color, tf_opacity)
    weights = call(
        lookup_kernel, array(tiles, slices * 3 + 1, rows, LANES), [SMEM] + [VMEM] * 3, 8_000_000
    )(occupancy_flags[0, 0], density, materials, tables)
    lit = (density, weights, near_z, far_z, near_y, far_y)

    paired = groups % 2 == 0 and chips & (chips - 1) == 0 and width % LANES == 0
    if paired:
        per = width // LANES
        half = array(tiles // 2, 4, rows, LANES)

        def block_order(other):
            def order(i):
                parity = (lax.axis_index("depth") + other) % 2
                return (i // per * 2 + parity) * per + i % per

            return order

        sent, kept = (
            call(functools.partial(shade_kernel, block_order(other)), half, [VMEM] * 6, 2_000_000)(*lit)
            for other in (1, 0)
        )
        received = lax.ppermute(sent, "depth", [(i, i ^ 1) for i in range(groups)])
        blocks = call(
            merge_kernel, [array(per, 4, rows, LANES)] * chips, [VMEM] * 2, 1_000_000
        )(kept, received)
        pieces = [blocks[0]] + [
            lax.ppermute(blocks[k], "depth", [(i, i ^ (2 * k)) for i in range(groups)])
            for k in range(1, chips)
        ]
        return call(finish_kernel, array(4, rows, width), [VMEM] * chips, 1_000_000)(*pieces)

    partial_value = call(
        functools.partial(shade_kernel, lambda i: i), array(tiles, 4, rows, LANES), [VMEM] * 6, 4_000_000
    )(*lit)
    natural = partial_value.transpose(1, 2, 0, 3).reshape(4, rows, groups, width)
    pieces = lax.all_to_all(
        natural.transpose(2, 0, 1, 3), "depth", split_axis=0, concat_axis=0, tiled=True
    )
    while pieces.shape[0] > 1:
        pieces = composite_over(pieces[0::2], pieces[1::2])
    finished = pieces[0]
    return jnp.concatenate([finished[:3], 1.0 - finished[3:]], axis=0)


def solution(mesh):
    placed = (
        P("depth", "strip", None),
        P("depth", "strip", None),
        P("depth", "strip", None),
        P(),
        P(),
    )
    return jax.shard_map(
        on_device, mesh=mesh, in_specs=placed, out_specs=P(None, "strip", "depth"), check_vma=False
    )
```

time: 35.6 us -> 30.2 us (0.85)
  blocking collectives: 15.8 us -> 0 us
  waiting for transfers between devices: 0.74 us -> 4.55 us
  starting transfers between devices: 10.2 us -> 13.8 us
  local copies, waits for them, and re-layouts: 0.83 us -> 2.82 us
  other arithmetic: 3.06 us -> 3.62 us
    all_to_all x1 -> x0, blocking collectives: 15.8 us -> none  [on_device(): lax.all_to_all(partial_value, 'depth', split_axis=0, concat_axis=0, tiled...]
    ppermute x4 -> x8, waiting for transfers between devices: 0.74 us -> 4.55 us  [the longest x3 3.58 us: on_device(): lax.ppermute(blocks[k], 'depth', [(i, i ^ 2 * k) for i in range(groups)])]
    ppermute x4 -> x8, starting transfers between devices: 10.2 us -> 13.8 us  [the longest x1 5.91 us: on_device(): near_y = lax.ppermute(inner_y, 'strip', neighbours(strips, 0))]
    unnamed x10 -> x6, local copies, waits for them, and re-layouts: 0.65 us -> 2.74 us
    sub x1, other arithmetic: 0.07 us -> 0.84 us  [lookup_tables(): values[:, :, 1:] - values[:, :, :-1]]
    concatenate x1, other arithmetic: 0.01 us -> 0.72 us  [lookup_tables(): lanes = jnp.concatenate([values, steps], axis=1)]
    concatenate x2 -> x0, other arithmetic: 0.65 us -> none  [the longest x1 0.64 us: on_device(): return jnp.concatenate([finished[:3], 1.0 - finished[3:]], axis=0)]
    pallas_call x1 -> x5, Pallas kernels: 4.65 us -> 4.99 us  [the longest x1 3.16 us: on_device(): call(lookup_kernel, array(tiles, slices * 3 + 1, rows, LANES), [SMEM] + [...]
  transfers between devices with their start and end apart: 4 -> 8, of which waited for: 1 -> 3; matrix products, arithmetic and copies ran while one was open for 4% -> 9% of each run, Pallas kernels for 0% -> 12%
where the time goes in v2:
time: 30.2 us; the launch traced here: 29.9 us
  starting transfers between devices  13.8 us (46%)
  Pallas kernels  4.99 us (17%)
  waiting for transfers between devices  4.55 us (15%)
  other arithmetic  3.62 us (12%)
  local copies, waits for them, and re-layouts  2.82 us (9%)
    ppermute x1, starting transfers between devices, on_device(): near_y = lax.ppermute(inner_y, 'strip', neighbours(strips, 0))  5.91 us
    ppermute x3, waiting for transfers between devices, on_device(): lax.ppermute(blocks[k], 'depth', [(i, i ^ 2 * k) for i in range(groups)])  3.58 us
    ppermute x3, starting transfers between devices, on_device(): lax.ppermute(blocks[k], 'depth', [(i, i ^ 2 * k) for i in range(groups)])  3.55 us
    pallas_call x1, Pallas kernels, on_device(): call(lookup_kernel, array(tiles, slices * 3 + 1, rows, LANES), [SMEM] + [...  3.16 us
    ppermute x1, starting transfers between devices, on_device(): near_z = lax.ppermute(inner, 'depth', neighbours(groups, 0))  2.91 us
    unnamed x6, local copies, waits for them, and re-layouts  2.74 us
    select_n x2, other arithmetic, sent_layers(): return (jnp.where(odd, first, last), jnp.where(odd, last, first))  2.06 us
    pallas_call x2, Pallas kernels, on_device(): call(functools.partial(shade_kernel, block_order(other)), half, [VMEM] *...  1.13 us
  transfers between devices with their start and end apart: 8, of which 3 were waited for; matrix products, arithmetic and copies ran while one was open for 9% of the time, Pallas kernels for 12%

profile of v2, /device:TPU:0, one launch (start us, length us, event | category | flops | bytes accessed | tf_op | source)
XLA Modules:
  0.0 29.9 jit_solution(6314568979590140057)
XLA Ops:
  0.0 1.1 %broadcast_select_fusion = (f32[4,1,2048]{2,1,0:T(1,128)S(1)}, f32[4,1,2048]{2,1,0:T(1,128)S(1)}) fusion(pred[]{:T(512)S(6)} %eq.10, f32[4,16,2048]{2,1,0:T(8,128)} %density.5), kind=kLoop, calls=%fused_computation.2 | loop fusion | flops 16384 | bytes 131073 | tf_op jit(solution)/shard_map/jit(_where)/select_n | solution.py:27
  1.1 0.7 %collective-permute-start.3 = (f32[4,1,2048]{2,1,0:T(1,128)S(1)}, f32[4,1,2048]{2,1,0:T(1,128)S(1)}, u32[]{:S(2)}, u32[]{:S(2)}) collective-permute-start(f32[4,1,2048]{2,1,0:T(1,128)S(1)} %get-tuple-element.13), channel_id=1, source_target_pairs={{1,2},{2,1},{5,6},{6,5},{9,10},{10,9},{13,14},{14,13},{17,18},{18,... | collective-permute-start | bytes 98312 | tf_op jit(solution)/shard_map/ppermute | solution.py:209
  1.8 5.9 %collective-permute-start.2 = (f32[4,1,2048]{2,1,0:T(1,128)S(1)}, f32[4,1,2048]{2,1,0:T(1,128)S(1)}, u32[]{:S(2)}, u32[]{:S(2)}) collective-permute-start(f32[4,1,2048]{2,1,0:T(1,128)S(1)} %get-tuple-element.14), channel_id=1, source_target_pairs={{0,1},{1,0},{2,3},{3,2},{4,5},{5,4},{6,7},{7,6},{8,9},{9,8},{10,11... | collective-permute-start | bytes 98312 | tf_op jit(solution)/shard_map/ppermute | solution.py:208
  7.7 1.0 %slice_select_fusion = (f32[1,16,2048]{2,1,0:T(8,128)S(1)}, f32[1,16,2048]{2,1,0:T(8,128)S(1)}) fusion(f32[4,16,2048]{2,1,0:T(8,128)} %density.5, pred[]{:T(512)S(6)} %eq.9), kind=kLoop, calls=%fused_computation | loop fusion | flops 65536 | bytes 524289 | tf_op jit(solution)/shard_map/jit(_where)/select_n | solution.py:27
  8.7 0.7 %collective-permute-start.1 = (f32[1,16,2048]{2,1,0:T(8,128)S(1)}, f32[1,16,2048]{2,1,0:T(8,128)S(1)}, u32[]{:S(2)}, u32[]{:S(2)}) collective-permute-start(f32[1,16,2048]{2,1,0:T(8,128)S(1)} %get-tuple-element.15), channel_id=1, source_target_pairs={{4,8},{8,4},{12,16},{16,12},{20,24},{24,20},{5,9},{9,5},{13,17},{1... | collective-permute-start | bytes 393224 | tf_op jit(solution)/shard_map/ppermute | solution.py:206
  9.3 2.9 %collective-permute-start = (f32[1,16,2048]{2,1,0:T(8,128)S(1)}, f32[1,16,2048]{2,1,0:T(8,128)S(1)}, u32[]{:S(2)}, u32[]{:S(2)}) collective-permute-start(f32[1,16,2048]{2,1,0:T(8,128)S(1)} %get-tuple-element.16), channel_id=1, source_target_pairs={{0,4},{4,0},{8,12},{12,8},{16,20},{20,16},{24,28},{28,24},{1,5},{5... | collective-permute-start | bytes 393224 | tf_op jit(solution)/shard_map/ppermute | solution.py:210
  12.2 0.8 %fusion = f32[4,4,15]{2,1,0:T(4,128)S(1)} fusion(f32[1,4,16]{2,1,0:T(4,128)} %bitcast.6, f32[3,4,16]{2,1,0:T(4,128)} %bitcast.4), kind=kLoop, calls=%fused_computation.7 | loop fusion | flops 720 | bytes 1984 | tf_op jit(solution)/shard_map/sub | solution.py:193
  13.1 0.7 %select_maximum_fusion = f32[4,8,16]{2,1,0:T(8,128)S(1)} fusion(f32[4,4,15]{2,1,0:T(4,128)S(1)} %fusion, f32[1,4,16]{2,1,0:T(4,128)} %bitcast.7, f32[3,4,16]{2,1,0:T(4,128)} %bitcast.5), kind=kLoop, calls=%fused_computation.4 | loop fusion | flops 2048 | bytes 4032 | tf_op jit(solution)/shard_map/concatenate | solution.py:194
  13.8 0.1 reshape.3.tables
  13.9 1.0 %copy-done = f32[4,16,2048]{2,1,0:T(8,128)S(1)} copy-done((f32[4,16,2048]{2,1,0:T(8,128)S(1)}, f32[4,16,2048]{2,1,0:T(8,128)}, u32[]{:S(2)}) %copy-start) | copy-done | bytes 524312
  14.9 1.0 %copy-done.1 = s32[4,16,2048]{2,1,0:T(8,128)S(1)} copy-done((s32[4,16,2048]{2,1,0:T(8,128)S(1)}, s32[4,16,2048]{2,1,0:T(8,128)}, u32[]{:S(2)}) %copy-start.1) | copy-done | bytes 524312
  16.0 0.7 %copy-done.2 = s32[1,1,16]{2,1,0:T(1,128)S(1)} copy-done((s32[1,1,16]{2,1,0:T(1,128)S(1)}, s32[1,1,16]{2,1,0:T(1,128)}, u32[]{:S(2)}) %copy-start.2) | copy-done | bytes 88
  16.6 3.2 %shard_map.55.weights = f32[16,13,16,128]{3,2,1,0:T(8,128)S(1)} custom-call(s32[16]{0:T(128)S(1)} %bitcast.3, f32[4,16,2048]{2,1,0:T(8,128)S(1)} %copy-done, s32[4,16,2048]{2,1,0:T(8,128)S(1)} %copy-done.1, f32[4,128]{1,0:T(4,128)S(1)} %reshape.3.tables), custom_call_target="tpu_custom_call" | custom-call | flops 8000000 | bytes 8000000 | tf_op jit(solution)/shard_map/pallas_call | solution.py:213
  19.8 0.0 collective-permute-done.2.near_y
  19.8 0.6 %shard_map.57 = f32[8,4,16,128]{3,2,1,0:T(8,128)S(1)} custom-call(f32[4,16,2048]{2,1,0:T(8,128)S(1)} %copy-done, f32[16,13,16,128]{3,2,1,0:T(8,128)S(1)} %shard_map.55.weights, f32[1,16,2048]{2,1,0:T(8,128)S(1)} %collective-permute-done.near_z, f32[1,16,2048]{2,1,0:T(8,128)S(1)} %collective-permute-done.1.far_z, ...), custom_call_target="tpu_custom_call" | custom-call | flops 2000000 | bytes 2000000 | tf_op jit(solution)/shard_map/pallas_call | solution.py:231
  20.4 0.1 collective-permute-start.4
  20.5 0.6 %shard_map.56.kept = f32[8,4,16,128]{3,2,1,0:T(8,128)S(1)} custom-call(f32[4,16,2048]{2,1,0:T(8,128)S(1)} %copy-done, f32[16,13,16,128]{3,2,1,0:T(8,128)S(1)} %shard_map.55.weights, f32[1,16,2048]{2,1,0:T(8,128)S(1)} %collective-permute-done.near_z, f32[1,16,2048]{2,1,0:T(8,128)S(1)} %collective-permute-done.1.far_z, ...), custom_call_target="tpu_custom_call" | custom-call | flops 2000000 | bytes 2000000 | tf_op jit(solution)/shard_map/pallas_call | solution.py:231
  21.1 1.0 %collective-permute-done.4.received = f32[8,4,16,128]{3,2,1,0:T(8,128)S(1)} collective-permute-done((f32[8,4,16,128]{3,2,1,0:T(8,128)S(1)}, f32[8,4,16,128]{3,2,1,0:T(8,128)S(1)}, u32[]{:S(2)}, u32[]{:S(2)}) %collective-permute-start.4) | collective-permute-done | bytes 262176 | tf_op jit(solution)/shard_map/ppermute | solution.py:234
  22.1 1.6 %collective-permute-start.5 = (f32[2,4,16,128]{3,2,1,0:T(8,128)S(1)}, f32[2,4,16,128]{3,2,1,0:T(8,128)S(1)}, u32[]{:S(2)}, u32[]{:S(2)}) collective-permute-start(f32[2,4,16,128]{3,2,1,0:T(8,128)S(1)} %get-tuple-element.10), channel_id=1, source_target_pairs={{0,8},{4,12},{8,0},{12,4},{16,24},{20,28},{24,16},{28,20},{1,9},{5... | collective-permute-start | bytes 196616 | tf_op jit(solution)/shard_map/ppermute | solution.py:239
  23.6 0.1 collective-permute-start.6
  23.7 1.9 %collective-permute-start.7 = (f32[2,4,16,128]{3,2,1,0:T(8,128)S(1)}, f32[2,4,16,128]{3,2,1,0:T(8,128)S(1)}, u32[]{:S(2)}, u32[]{:S(2)}) collective-permute-start(f32[2,4,16,128]{3,2,1,0:T(8,128)S(1)} %get-tuple-element.12), channel_id=1, source_target_pairs={{0,24},{4,28},{8,16},{12,20},{16,8},{20,12},{24,0},{28,4},{1,25},{... | collective-permute-start | bytes 196616 | tf_op jit(solution)/shard_map/ppermute | solution.py:239
  25.6 0.8 %collective-permute-done.5.refs_1_ = f32[2,4,16,128]{3,2,1,0:T(8,128)S(1)} collective-permute-done((f32[2,4,16,128]{3,2,1,0:T(8,128)S(1)}, f32[2,4,16,128]{3,2,1,0:T(8,128)S(1)}, u32[]{:S(2)}, u32[]{:S(2)}) %collective-permute-start.5) | collective-permute-done | bytes 65568 | tf_op jit(solution)/shard_map/ppermute | solution.py:239
  26.4 2.8 %collective-permute-done.6.refs_2_ = f32[2,4,16,128]{3,2,1,0:T(8,128)S(1)} collective-permute-done((f32[2,4,16,128]{3,2,1,0:T(8,128)S(1)}, f32[2,4,16,128]{3,2,1,0:T(8,128)S(1)}, u32[]{:S(2)}, u32[]{:S(2)}) %collective-permute-start.6) | collective-permute-done | bytes 65568 | tf_op jit(solution)/shard_map/ppermute | solution.py:239
  29.2 0.7 %shard_map.59 = f32[4,16,256]{2,1,0:T(8,128)} custom-call(f32[2,4,16,128]{3,2,1,0:T(8,128)S(1)} %get-tuple-element.9.refs_0_, f32[2,4,16,128]{3,2,1,0:T(8,128)S(1)} %collective-permute-done.5.refs_1_, f32[2,4,16,128]{3,2,1,0:T(8,128)S(1)} %collective-permute-done.6.refs_2_, f32[2,4,16,128]{3,2,1,0:T(8,128)S(1)} %collective-permute-done.7.refs_3_), custom_call_target="tpu_custom_call" | custom-call | flops 1000000 | bytes 1000000 | tf_op jit(solution)/shard_map/pallas_call | solution.py:242
  (8 shorter events, 0.1 us)
Async XLA Ops:
  1.1 18.7 %collective-permute-start.3 = (f32[4,1,2048]{2,1,0:T(1,128)S(1)}, f32[4,1,2048]{2,1,0:T(1,128)S(1)}, u32[]{:S(2)}, u32[]{:S(2)}) collective-permute-start(f32[4,1,2048]{2,1,0:T(1,128)S(1)} %get-tuple-element.13), channel_id=1, source_target_pairs={{1,2},{2,1},{5,6},{6,5},{9,10},{10,9},{13,14},{14,13},{17,18},{18,... | collective-permute-start | bytes 98312 | tf_op jit(solution)/shard_map/ppermute | solution.py:209
  1.8 18.1 %collective-permute-start.2 = (f32[4,1,2048]{2,1,0:T(1,128)S(1)}, f32[4,1,2048]{2,1,0:T(1,128)S(1)}, u32[]{:S(2)}, u32[]{:S(2)}) collective-permute-start(f32[4,1,2048]{2,1,0:T(1,128)S(1)} %get-tuple-element.14), channel_id=1, source_target_pairs={{0,1},{1,0},{2,3},{3,2},{4,5},{5,4},{6,7},{7,6},{8,9},{9,8},{10,11... | collective-permute-start | bytes 98312 | tf_op jit(solution)/shard_map/ppermute | solution.py:208
  8.7 11.2 %collective-permute-start.1 = (f32[1,16,2048]{2,1,0:T(8,128)S(1)}, f32[1,16,2048]{2,1,0:T(8,128)S(1)}, u32[]{:S(2)}, u32[]{:S(2)}) collective-permute-start(f32[1,16,2048]{2,1,0:T(8,128)S(1)} %get-tuple-element.15), channel_id=1, source_target_pairs={{4,8},{8,4},{12,16},{16,12},{20,24},{24,20},{5,9},{9,5},{13,17},{1... | collective-permute-start | bytes 393224 | tf_op jit(solution)/shard_map/ppermute | solution.py:206
  9.3 10.5 %collective-permute-start = (f32[1,16,2048]{2,1,0:T(8,128)S(1)}, f32[1,16,2048]{2,1,0:T(8,128)S(1)}, u32[]{:S(2)}, u32[]{:S(2)}) collective-permute-start(f32[1,16,2048]{2,1,0:T(8,128)S(1)} %get-tuple-element.16), channel_id=1, source_target_pairs={{0,4},{4,0},{8,12},{12,8},{16,20},{20,16},{24,28},{28,24},{1,5},{5... | collective-permute-start | bytes 393224 | tf_op jit(solution)/shard_map/ppermute | solution.py:210
  13.9 1.0 %copy-start = (f32[4,16,2048]{2,1,0:T(8,128)S(1)}, f32[4,16,2048]{2,1,0:T(8,128)}, u32[]{:S(2)}) copy-start(f32[4,16,2048]{2,1,0:T(8,128)} %density.5) | copy-start | bytes 1572868
  14.9 1.0 %copy-start.1 = (s32[4,16,2048]{2,1,0:T(8,128)S(1)}, s32[4,16,2048]{2,1,0:T(8,128)}, u32[]{:S(2)}) copy-start(s32[4,16,2048]{2,1,0:T(8,128)} %materials.1) | copy-start | bytes 1572868
  16.0 0.7 %copy-start.2 = (s32[1,1,16]{2,1,0:T(1,128)S(1)}, s32[1,1,16]{2,1,0:T(1,128)}, u32[]{:S(2)}) copy-start(s32[1,1,16]{2,1,0:T(1,128)} %param.7) | copy-start | bytes 196
  20.4 1.6 %collective-permute-start.4 = (f32[8,4,16,128]{3,2,1,0:T(8,128)S(1)}, f32[8,4,16,128]{3,2,1,0:T(8,128)S(1)}, u32[]{:S(2)}, u32[]{:S(2)}) collective-permute-start(f32[8,4,16,128]{3,2,1,0:T(8,128)S(1)} %shard_map.57), channel_id=1, source_target_pairs={{0,4},{4,0},{8,12},{12,8},{16,20},{20,16},{24,28},{28,24},{1,5},{5... | collective-permute-start | bytes 786440 | tf_op jit(solution)/shard_map/ppermute | solution.py:234
  22.1 4.3 %collective-permute-start.5 = (f32[2,4,16,128]{3,2,1,0:T(8,128)S(1)}, f32[2,4,16,128]{3,2,1,0:T(8,128)S(1)}, u32[]{:S(2)}, u32[]{:S(2)}) collective-permute-start(f32[2,4,16,128]{3,2,1,0:T(8,128)S(1)} %get-tuple-element.10), channel_id=1, source_target_pairs={{0,8},{4,12},{8,0},{12,4},{16,24},{20,28},{24,16},{28,20},{1,9},{5... | collective-permute-start | bytes 196616 | tf_op jit(solution)/shard_map/ppermute | solution.py:239
  23.6 5.6 %collective-permute-start.6 = (f32[2,4,16,128]{3,2,1,0:T(8,128)S(1)}, f32[2,4,16,128]{3,2,1,0:T(8,128)S(1)}, u32[]{:S(2)}, u32[]{:S(2)}) collective-permute-start(f32[2,4,16,128]{3,2,1,0:T(8,128)S(1)} %get-tuple-element.11), channel_id=1, source_target_pairs={{0,16},{4,20},{8,24},{12,28},{16,0},{20,4},{24,8},{28,12},{1,17},{... | collective-permute-start | bytes 196616 | tf_op jit(solution)/shard_map/ppermute | solution.py:239
  23.7 5.5 %collective-permute-start.7 = (f32[2,4,16,128]{3,2,1,0:T(8,128)S(1)}, f32[2,4,16,128]{3,2,1,0:T(8,128)S(1)}, u32[]{:S(2)}, u32[]{:S(2)}) collective-permute-start(f32[2,4,16,128]{3,2,1,0:T(8,128)S(1)} %get-tuple-element.12), channel_id=1, source_target_pairs={{0,24},{4,28},{8,16},{12,20},{16,8},{20,12},{24,0},{28,4},{1,25},{... | collective-permute-start | bytes 196616 | tf_op jit(solution)/shard_map/ppermute | solution.py:239

commit v3 on v2

--- a/solution.py
+++ b/solution.py
@@ -12,19 +12,22 @@
 LANES = 128
 ROWS = 8
 VMEM = pl.BlockSpec(memory_space=pltpu.VMEM)
-SMEM = pl.BlockSpec(memory_space=pltpu.SMEM)
-
-
-def neighbours(count, first):
+
+
+def inner_pairs(count):
+    return [(i, i ^ 1) for i in range(count)]
+
+
+def outer_pairs(groups, strips, axis):
     pairs = []
-    for low in range(first, count - 1, 2):
-        pairs += [(low, low + 1), (low + 1, low)]
+    for g in range(groups):
+        for s in range(strips):
+            if axis == "depth":
+                to = (g, s ^ 1) if g in (0, groups - 1) else (g + 1 if g % 2 else g - 1, s)
+            else:
+                to = (g ^ 1, s) if s in (0, strips - 1) else (g, s + 1 if s % 2 else s - 1)
+            pairs.append((g * strips + s, to[0] * strips + to[1]))
     return pairs
-
-
-def sent_layers(first, last, axis):
-    odd = lax.axis_index(axis) % 2 == 1
-    return jnp.where(odd, first, last), jnp.where(odd, last, first)
 
 
 def tile(c):
@@ -46,14 +49,56 @@
     return jax.ShapeDtypeStruct(shape, jnp.float32)
 
 
-def lookup_kernel(flags, density, materials, tables, out):
+def load_kernel(*refs):
+    given, held = refs[:5], refs[5:10]
+    inner_z, outer_z, inner_y, outer_y, sems = refs[10:]
+    copies = [pltpu.make_async_copy(x, y, sems.at[i]) for i, (x, y) in enumerate(zip(given, held))]
+    for copy in copies:
+        copy.start()
+    density = held[0]
     slices, rows, columns = density.shape
-    knots = tables.shape[1] // 8
-    table = [jnp.broadcast_to(tables[i : i + 1, :], (ROWS, LANES)) for i in range(4)]
+    odd_z = lax.axis_index("depth") % 2
+    odd_y = lax.axis_index("strip") % 2 == 1
+    copies[0].wait()
+    inner_z[0] = density[(slices - 1) * (1 - odd_z)]
+    outer_z[0] = density[(slices - 1) * odd_z]
+    for z in range(slices):
+        first, last = density[z, :1, :], density[z, rows - 1 :, :]
+        inner_y[z : z + 1, :] = jnp.where(odd_y, first, last)
+        outer_y[z : z + 1, :] = jnp.where(odd_y, last, first)
+    for copy in copies[1:]:
+        copy.wait()
+
+
+def by_lane(table):
+    here = [table[m : m + 1, :] for m in range(table.shape[0])]
+    last = table.shape[1] - 1
+    further = [jnp.concatenate([t[:, 1:], t[:, last:]], axis=1) for t in here]
+    return jnp.concatenate(here + here, axis=1), jnp.concatenate(further + further, axis=1)
+
+
+def lookup_kernel(density, materials, flags, tf_color, tf_opacity, out):
+    slices, rows, columns = density.shape
+    knots = tf_opacity.shape[1]
+    lane = lax.broadcasted_iota(jnp.int32, (1, LANES), 1)
+    table = []
+    for ch in range(3):
+        value, further = by_lane(tf_color[ch])
+        low = (further * 65535.0 + 0.5).astype(jnp.int32)
+        high = jnp.floor((value * (32767.0 * 65536.0) - low.astype(jnp.float32)) * (1.0 / 65536.0) + 0.5)
+        table.append(jnp.broadcast_to(high.astype(jnp.int32) * 65536 + low, (ROWS, LANES)))
+    value, further = by_lane(tf_opacity[...])
+    rates = jnp.broadcast_to(jnp.where(lane < LANES // 2, value, further - value), (ROWS, LANES))
+
+    occupied = [flags[:, :].astype(jnp.float32)] * (LANES // flags.shape[1])
+    occupied = jnp.broadcast_to(jnp.concatenate(occupied, axis=1), (ROWS, LANES))
+
+    def look(t, index):
+        return jnp.take_along_axis(t, index, axis=1, mode="promise_in_bounds")
 
     def body(c, _):
         here = tile(c)
-        occupied = flags[c].astype(jnp.float32)
+        present = look(occupied, jnp.full((ROWS, LANES), c, jnp.int32))
         for b in range(rows // ROWS):
             band = slice(b * ROWS, (b + 1) * ROWS)
             transmit = None
@@ -64,19 +109,17 @@
                 whole = position.astype(jnp.int32)
                 part = position - whole.astype(jnp.float32)
                 index = materials[z, band, here] * knots + whole
-                slope_index = index + LANES // 2
-
-                def look(t):
-                    base = jnp.take_along_axis(t, index, axis=1, mode="promise_in_bounds")
-                    slope = jnp.take_along_axis(t, slope_index, axis=1, mode="promise_in_bounds")
-                    return base + part * slope
-
-                clear = jnp.exp(-(look(table[3]) * occupied))
+                rate = look(rates, index) + part * look(rates, index + LANES // 2)
+                clear = jnp.exp(-(rate * present))
                 weight = 1.0 - clear
                 if z:
                     weight = weight * transmit
+                of_low = (part * weight) * (1.0 / 65535.0)
+                of_high = (weight - part * weight) * (1.0 / (32767.0 * 65536.0))
                 for ch in range(3):
-                    out[c, z * 3 + ch, band, :] = look(table[ch]) * weight
+                    both = look(table[ch], index)
+                    low = (both & 65535).astype(jnp.float32)
+                    out[c, z * 3 + ch, band, :] = both.astype(jnp.float32) * of_high + low * of_low
                 transmit = transmit * clear if z else clear
             out[c, slices * 3, band, :] = transmit
         return 0
@@ -90,8 +133,12 @@
     bands = rows // ROWS
     lane = lax.broadcasted_iota(jnp.int32, (ROWS, LANES), 1)
     row = lax.broadcasted_iota(jnp.int32, (ROWS, LANES), 0)
-    odd_z = lax.axis_index("depth") % 2 == 1
-    odd_y = lax.axis_index("strip") % 2 == 1
+    at_z, at_y = lax.axis_index("depth"), lax.axis_index("strip")
+    odd_z, odd_y = at_z % 2 == 1, at_y % 2 == 1
+    has_nearer = jnp.where(at_z > 0, 1.0, 0.0)
+    has_farther = jnp.where(at_z < lax.axis_size("depth") - 1, 1.0, 0.0)
+    has_top = jnp.where(at_y > 0, 1.0, 0.0)
+    has_bottom = jnp.where(at_y < lax.axis_size("strip") - 1, 1.0, 0.0)
 
     def body(i, _):
         c = order(i)
@@ -105,22 +152,22 @@
             for z in range(slices):
                 v = d[z][b]
                 if z == 0:
-                    nearer = jnp.where(odd_z, near_z[0, band, here], far_z[0, band, here])
+                    nearer = jnp.where(odd_z, near_z[0, band, here], far_z[0, band, here]) * has_nearer
                 else:
                     nearer = d[z - 1][b]
                 if z == slices - 1:
-                    farther = jnp.where(odd_z, far_z[0, band, here], near_z[0, band, here])
+                    farther = jnp.where(odd_z, far_z[0, band, here], near_z[0, band, here]) * has_farther
                 else:
                     farther = d[z + 1][b]
                 dz = farther - nearer
                 if b == 0:
-                    top = jnp.where(odd_y, near_y[z, :, here], far_y[z, :, here])
-                    top = jnp.broadcast_to(top, (ROWS, LANES))
+                    top = jnp.where(odd_y, near_y[z : z + 1, here], far_y[z : z + 1, here])
+                    top = jnp.broadcast_to(top * has_top, (ROWS, LANES))
                 else:
                     top = d[z][b - 1]
                 if b == bands - 1:
-                    bottom = jnp.where(odd_y, far_y[z, :, here], near_y[z, :, here])
-                    bottom = jnp.broadcast_to(bottom, (ROWS, LANES))
+                    bottom = jnp.where(odd_y, far_y[z : z + 1, here], near_y[z : z + 1, here])
+                    bottom = jnp.broadcast_to(bottom * has_bottom, (ROWS, LANES))
                 else:
                     bottom = d[z][b + 1]
                 dy = pltpu.roll(jnp.where(row == 0, bottom, v), ROWS - 1, 0) - pltpu.roll(
@@ -188,13 +235,6 @@
     )
 
 
-def lookup_tables(tf_color, tf_opacity):
-    values = jnp.concatenate([tf_color.transpose(1, 0, 2), tf_opacity[None]], axis=0)
-    steps = jnp.pad(values[:, :, 1:] - values[:, :, :-1], ((0, 0), (0, 0), (0, 1)))
-    lanes = jnp.concatenate([values, steps], axis=1)
-    return lanes.reshape(4, -1)
-
-
 def on_device(density, materials, occupancy_flags, tf_color, tf_opacity):
     slices, rows, columns = density.shape
     tiles = columns // LANES
@@ -202,17 +242,25 @@
     width = columns // groups
     chips = groups // 2
 
-    inner, outer = sent_layers(density[:1], density[-1:], "depth")
-    far_z = lax.ppermute(outer, "depth", neighbours(groups, 1))
-    inner_y, outer_y = sent_layers(density[:, :1], density[:, -1:], "strip")
-    near_y = lax.ppermute(inner_y, "strip", neighbours(strips, 0))
-    far_y = lax.ppermute(outer_y, "strip", neighbours(strips, 1))
-    near_z = lax.ppermute(inner, "depth", neighbours(groups, 0))
-
-    tables = lookup_tables(tf_color, tf_opacity)
+    given = (density, materials, occupancy_flags[0], tf_color.transpose(1, 0, 2), tf_opacity)
+    layer, edge = array(1, rows, columns), array(slices, columns)
+    density, materials, flags, tf_color, tf_opacity, inner_z, outer_z, inner_y, outer_y = pl.pallas_call(
+        load_kernel,
+        out_shape=[jax.ShapeDtypeStruct(x.shape, x.dtype) for x in given] + [layer, layer, edge, edge],
+        in_specs=[pl.BlockSpec(memory_space=pltpu.HBM)] * 5,
+        out_specs=[VMEM] * 9,
+        scratch_shapes=[pltpu.SemaphoreType.DMA((5,))],
+        compiler_params=pltpu.CompilerParams(vmem_limit_bytes=16 * 1024 * 1024),
+    )(*[pltpu.with_memory_space_constraint(x, pltpu.HBM) for x in given])
+    both = ("depth", "strip")
+    far_z = lax.ppermute(outer_z, both, outer_pairs(groups, strips, "depth"))
+    near_z = lax.ppermute(inner_z, "depth", inner_pairs(groups))
+    near_y = lax.ppermute(inner_y, "strip", inner_pairs(strips))
+    far_y = lax.ppermute(outer_y, both, outer_pairs(groups, strips, "strip"))
+
     weights = call(
-        lookup_kernel, array(tiles, slices * 3 + 1, rows, LANES), [SMEM] + [VMEM] * 3, 8_000_000
-    )(occupancy_flags[0, 0], density, materials, tables)
+        lookup_kernel, array(tiles, slices * 3 + 1, rows, LANES), [VMEM] * 5, 8_000_000
+    )(density, materials, flags, tf_color, tf_opacity)
     lit = (density, weights, near_z, far_z, near_y, far_y)
 
     paired = groups % 2 == 0 and chips & (chips - 1) == 0 and width % LANES == 0
@@ -231,7 +279,7 @@
             call(functools.partial(shade_kernel, block_order(other)), half, [VMEM] * 6, 2_000_000)(*lit)
             for other in (1, 0)
         )
-        received = lax.ppermute(sent, "depth", [(i, i ^ 1) for i in range(groups)])
+        received = lax.ppermute(sent, "depth", inner_pairs(groups))
         blocks = call(
             merge_kernel, [array(per, 4, rows, LANES)] * chips, [VMEM] * 2, 1_000_000
         )(kept, received)

time: 30.2 us -> 19.4 us (0.64)
  starting transfers between devices: 13.8 us -> 8.34 us
  other arithmetic: 3.62 us -> 0 us
  local copies, waits for them, and re-layouts: 2.82 us -> 0 us
  waiting for transfers between devices: 4.55 us -> 5.83 us
    ppermute x5, starting transfers between devices: 10.2 us -> 4.56 us  [the longest x1 2.65 us: on_device(): far_z = lax.ppermute(outer_z, both, outer_pairs(groups, strips, 'depth'))]
    unnamed x6 -> x0, local copies, waits for them, and re-layouts: 2.74 us -> none
    select_n x2 -> x0, other arithmetic: 2.06 us -> none  [sent_layers(): return (jnp.where(odd, first, last), jnp.where(odd, last, first))]
    sub x1 -> x0, other arithmetic: 0.84 us -> none  [lookup_tables(): values[:, :, 1:] - values[:, :, :-1]]
    concatenate x1 -> x0, other arithmetic: 0.72 us -> none  [lookup_tables(): lanes = jnp.concatenate([values, steps], axis=1)]
    ppermute x3, waiting for transfers between devices: 3.58 us -> 4.23 us  [on_device(): lax.ppermute(blocks[k], 'depth', [(i, i ^ 2 * k) for i in range(groups)])]
    ppermute x5, waiting for transfers between devices: 0.97 us -> 1.6 us  [the longest x1 0.94 us: on_device(): received = lax.ppermute(sent, 'depth', inner_pairs(groups))]
    pallas_call x1 -> x2, Pallas kernels: 3.16 us -> 3.17 us  [the longest x1 1.92 us: on_device(): call(lookup_kernel, array(tiles, slices * 3 + 1, rows, LANES), [VMEM] * 5...]
  transfers between devices with their start and end apart: 8 -> 8, of which waited for: 3 -> 5; matrix products, arithmetic and copies ran while one was open for 9% -> 0% of each run, Pallas kernels for 12% -> 13%
where the time goes in v3:
time: 19.4 us; the launch traced here: 19.3 us
  starting transfers between devices  8.34 us (43%)
  waiting for transfers between devices  5.83 us (30%)
  Pallas kernels  5.04 us (26%)
    ppermute x3, waiting for transfers between devices, on_device(): lax.ppermute(blocks[k], 'depth', [(i, i ^ 2 * k) for i in range(groups)])  4.23 us
    ppermute x3, starting transfers between devices, on_device(): lax.ppermute(blocks[k], 'depth', [(i, i ^ 2 * k) for i in range(groups)])  3.78 us
    ppermute x1, starting transfers between devices, on_device(): far_z = lax.ppermute(outer_z, both, outer_pairs(groups, strips, 'depth'))  2.65 us
    pallas_call x1, Pallas kernels, on_device(): call(lookup_kernel, array(tiles, slices * 3 + 1, rows, LANES), [VMEM] * 5...  1.92 us
    ppermute x1, starting transfers between devices, on_device(): far_y = lax.ppermute(outer_y, both, outer_pairs(groups, strips, 'strip'))  1.25 us
    pallas_call x1, Pallas kernels, on_device(): pl.pallas_call(load_kernel, out_shape=[jax.ShapeDtypeStruct(x.shape, x.dt...  1.25 us
    pallas_call x2, Pallas kernels, on_device(): call(functools.partial(shade_kernel, block_order(other)), half, [VMEM] *...  1.17 us
    ppermute x1, waiting for transfers between devices, on_device(): received = lax.ppermute(sent, 'depth', inner_pairs(groups))  0.94 us
  transfers between devices with their start and end apart: 8, of which 5 were waited for; matrix products, arithmetic and copies ran while one was open for 0% of the time, Pallas kernels for 13%

profile of v3, /device:TPU:0, one launch (start us, length us, event | category | flops | bytes accessed | tf_op | source)
XLA Modules:
  0.0 19.3 jit_solution(17745450862642847243)
XLA Ops:
  0.0 1.2 %shard_map.55 = (f32[4,16,2048]{2,1,0:T(8,128)S(1)}, s32[4,16,2048]{2,1,0:T(8,128)S(1)}, s32[1,16]{1,0:T(1,128)S(1)}, f32[3,4,16]{2,1,0:T(4,128)S(1)}, f32[4,16]...) custom-call(f32[4,16,2048]{2,1,0:T(8,128)} %refs_0_.1, ...), custom_call_target="tpu_custom_call" | custom-call | tf_op jit(solution)/shard_map/pallas_call | solution.py:247
  1.3 0.5 %collective-permute-start = (f32[1,16,2048]{2,1,0:T(8,128)S(1)}, f32[1,16,2048]{2,1,0:T(8,128)S(1)}, u32[]{:S(2)}, u32[]{:S(2)}) collective-permute-start(f32[1,16,2048]{2,1,0:T(8,128)S(1)} %get-tuple-element.23), channel_id=1, source_target_pairs={{0,4},{4,0},{8,12},{12,8},{16,20},{20,16},{24,28},{28,24},{1,5},{5... | collective-permute-start | bytes 393224 | tf_op jit(solution)/shard_map/ppermute | solution.py:257
  1.8 2.6 %collective-permute-start.1 = (f32[1,16,2048]{2,1,0:T(8,128)S(1)}, f32[1,16,2048]{2,1,0:T(8,128)S(1)}, u32[]{:S(2)}, u32[]{:S(2)}) collective-permute-start(f32[1,16,2048]{2,1,0:T(8,128)S(1)} %get-tuple-element.24), channel_id=1, source_target_pairs={{0,1},{1,0},{2,3},{3,2},{4,8},{5,9},{6,10},{7,11},{8,4},{9,5},{10,... | collective-permute-start | bytes 393224 | tf_op jit(solution)/shard_map/ppermute | solution.py:256
  4.4 0.1 collective-permute-start.2
  4.5 1.2 %collective-permute-start.3 = (f32[4,2048]{1,0:T(4,128)S(1)}, f32[4,2048]{1,0:T(4,128)S(1)}, u32[]{:S(2)}, u32[]{:S(2)}) collective-permute-start(f32[4,2048]{1,0:T(4,128)S(1)} %get-tuple-element.26), channel_id=1, source_target_pairs={{0,4},{1,2},{2,1},{3,7},{4,0},{5,6},{6,5},{7,3},{8,12},{9,10},{10,... | collective-permute-start | bytes 98312 | tf_op jit(solution)/shard_map/ppermute | solution.py:259
  5.8 1.9 %shard_map.56.weights = f32[16,13,16,128]{3,2,1,0:T(8,128)S(1)} custom-call(f32[4,16,2048]{2,1,0:T(8,128)S(1)} %get-tuple-element.18.density, s32[4,16,2048]{2,1,0:T(8,128)S(1)} %get-tuple-element.19.materials, s32[1,16]{1,0:T(1,128)S(1)} %get-tuple-element.20.flags, f32[3,4,16]{2,1,0:T(4,128)S(1)} %get-tuple-element.21.tf_color, ...), custom_call_target="tpu_custom_call" | custom-call | flops 8000000 | bytes 8000000 | tf_op jit(solution)/shard_map/pallas_call | solution.py:261
  7.7 0.7 %collective-permute-done.2.near_y = f32[4,2048]{1,0:T(4,128)S(1)} collective-permute-done((f32[4,2048]{1,0:T(4,128)S(1)}, f32[4,2048]{1,0:T(4,128)S(1)}, u32[]{:S(2)}, u32[]{:S(2)}) %collective-permute-start.2) | collective-permute-done | bytes 32800 | tf_op jit(solution)/shard_map/ppermute | solution.py:258
  8.3 0.0 collective-permute-done.3.far_y
  8.3 0.0 collective-permute-done.near_z
  8.3 0.0 collective-permute-done.1.far_z
  8.4 0.6 %shard_map.58 = f32[8,4,16,128]{3,2,1,0:T(8,128)S(1)} custom-call(f32[4,16,2048]{2,1,0:T(8,128)S(1)} %get-tuple-element.18.density, f32[16,13,16,128]{3,2,1,0:T(8,128)S(1)} %shard_map.56.weights, f32[1,16,2048]{2,1,0:T(8,128)S(1)} %collective-permute-done.near_z, f32[1,16,2048]{2,1,0:T(8,128)S(1)} %collective-permute-done.1.far_z, ...), custom_call_target="tpu_custom_call" | custom-call | flops 2000000 | bytes 2000000 | tf_op jit(solution)/shard_map/pallas_call | solution.py:279
  9.0 0.1 collective-permute-start.4
  9.0 0.6 %shard_map.57.kept = f32[8,4,16,128]{3,2,1,0:T(8,128)S(1)} custom-call(f32[4,16,2048]{2,1,0:T(8,128)S(1)} %get-tuple-element.18.density, f32[16,13,16,128]{3,2,1,0:T(8,128)S(1)} %shard_map.56.weights, f32[1,16,2048]{2,1,0:T(8,128)S(1)} %collective-permute-done.near_z, f32[1,16,2048]{2,1,0:T(8,128)S(1)} %collective-permute-done.1.far_z, ...), custom_call_target="tpu_custom_call" | custom-call | flops 2000000 | bytes 2000000 | tf_op jit(solution)/shard_map/pallas_call | solution.py:279
  9.6 0.9 %collective-permute-done.4.received = f32[8,4,16,128]{3,2,1,0:T(8,128)S(1)} collective-permute-done((f32[8,4,16,128]{3,2,1,0:T(8,128)S(1)}, f32[8,4,16,128]{3,2,1,0:T(8,128)S(1)}, u32[]{:S(2)}, u32[]{:S(2)}) %collective-permute-start.4) | collective-permute-done | bytes 262176 | tf_op jit(solution)/shard_map/ppermute | solution.py:282
  10.6 2.2 %collective-permute-start.5 = (f32[2,4,16,128]{3,2,1,0:T(8,128)S(1)}, f32[2,4,16,128]{3,2,1,0:T(8,128)S(1)}, u32[]{:S(2)}, u32[]{:S(2)}) collective-permute-start(f32[2,4,16,128]{3,2,1,0:T(8,128)S(1)} %get-tuple-element.28), channel_id=1, source_target_pairs={{0,8},{4,12},{8,0},{12,4},{16,24},{20,28},{24,16},{28,20},{1,9},{5... | collective-permute-start | bytes 196616 | tf_op jit(solution)/shard_map/ppermute | solution.py:287
  12.8 0.6 %collective-permute-start.6 = (f32[2,4,16,128]{3,2,1,0:T(8,128)S(1)}, f32[2,4,16,128]{3,2,1,0:T(8,128)S(1)}, u32[]{:S(2)}, u32[]{:S(2)}) collective-permute-start(f32[2,4,16,128]{3,2,1,0:T(8,128)S(1)} %get-tuple-element.29), channel_id=1, source_target_pairs={{0,16},{4,20},{8,24},{12,28},{16,0},{20,4},{24,8},{28,12},{1,17},{... | collective-permute-start | bytes 196616 | tf_op jit(solution)/shard_map/ppermute | solution.py:287
  13.4 0.9 %collective-permute-start.7 = (f32[2,4,16,128]{3,2,1,0:T(8,128)S(1)}, f32[2,4,16,128]{3,2,1,0:T(8,128)S(1)}, u32[]{:S(2)}, u32[]{:S(2)}) collective-permute-start(f32[2,4,16,128]{3,2,1,0:T(8,128)S(1)} %get-tuple-element.30), channel_id=1, source_target_pairs={{0,24},{4,28},{8,16},{12,20},{16,8},{20,12},{24,0},{28,4},{1,25},{... | collective-permute-start | bytes 196616 | tf_op jit(solution)/shard_map/ppermute | solution.py:287
  14.4 1.1 %collective-permute-done.5.refs_1_ = f32[2,4,16,128]{3,2,1,0:T(8,128)S(1)} collective-permute-done((f32[2,4,16,128]{3,2,1,0:T(8,128)S(1)}, f32[2,4,16,128]{3,2,1,0:T(8,128)S(1)}, u32[]{:S(2)}, u32[]{:S(2)}) %collective-permute-start.5) | collective-permute-done | bytes 65568 | tf_op jit(solution)/shard_map/ppermute | solution.py:287
  15.4 2.4 %collective-permute-done.6.refs_2_ = f32[2,4,16,128]{3,2,1,0:T(8,128)S(1)} collective-permute-done((f32[2,4,16,128]{3,2,1,0:T(8,128)S(1)}, f32[2,4,16,128]{3,2,1,0:T(8,128)S(1)}, u32[]{:S(2)}, u32[]{:S(2)}) %collective-permute-start.6) | collective-permute-done | bytes 65568 | tf_op jit(solution)/shard_map/ppermute | solution.py:287
  17.8 0.8 %collective-permute-done.7.refs_3_ = f32[2,4,16,128]{3,2,1,0:T(8,128)S(1)} collective-permute-done((f32[2,4,16,128]{3,2,1,0:T(8,128)S(1)}, f32[2,4,16,128]{3,2,1,0:T(8,128)S(1)}, u32[]{:S(2)}, u32[]{:S(2)}) %collective-permute-start.7) | collective-permute-done | bytes 65568 | tf_op jit(solution)/shard_map/ppermute | solution.py:287
  18.6 0.7 %shard_map.60 = f32[4,16,256]{2,1,0:T(8,128)} custom-call(f32[2,4,16,128]{3,2,1,0:T(8,128)S(1)} %get-tuple-element.27.refs_0_, f32[2,4,16,128]{3,2,1,0:T(8,128)S(1)} %collective-permute-done.5.refs_1_, f32[2,4,16,128]{3,2,1,0:T(8,128)S(1)} %collective-permute-done.6.refs_2_, f32[2,4,16,128]{3,2,1,0:T(8,128)S(1)} %collective-permute-done.7.refs_3_), custom_call_target="tpu_custom_call" | custom-call | flops 1000000 | bytes 1000000 | tf_op jit(solution)/shard_map/pallas_call | solution.py:290
  (1 shorter events, 0.0 us)
Async XLA Ops:
  1.3 7.1 %collective-permute-start = (f32[1,16,2048]{2,1,0:T(8,128)S(1)}, f32[1,16,2048]{2,1,0:T(8,128)S(1)}, u32[]{:S(2)}, u32[]{:S(2)}) collective-permute-start(f32[1,16,2048]{2,1,0:T(8,128)S(1)} %get-tuple-element.23), channel_id=1, source_target_pairs={{0,4},{4,0},{8,12},{12,8},{16,20},{20,16},{24,28},{28,24},{1,5},{5... | collective-permute-start | bytes 393224 | tf_op jit(solution)/shard_map/ppermute | solution.py:257
  1.8 6.6 %collective-permute-start.1 = (f32[1,16,2048]{2,1,0:T(8,128)S(1)}, f32[1,16,2048]{2,1,0:T(8,128)S(1)}, u32[]{:S(2)}, u32[]{:S(2)}) collective-permute-start(f32[1,16,2048]{2,1,0:T(8,128)S(1)} %get-tuple-element.24), channel_id=1, source_target_pairs={{0,1},{1,0},{2,3},{3,2},{4,8},{5,9},{6,10},{7,11},{8,4},{9,5},{10,... | collective-permute-start | bytes 393224 | tf_op jit(solution)/shard_map/ppermute | solution.py:256
  4.4 3.9 %collective-permute-start.2 = (f32[4,2048]{1,0:T(4,128)S(1)}, f32[4,2048]{1,0:T(4,128)S(1)}, u32[]{:S(2)}, u32[]{:S(2)}) collective-permute-start(f32[4,2048]{1,0:T(4,128)S(1)} %get-tuple-element.25), channel_id=1, source_target_pairs={{0,1},{1,0},{2,3},{3,2},{4,5},{5,4},{6,7},{7,6},{8,9},{9,8},{10,11... | collective-permute-start | bytes 98312 | tf_op jit(solution)/shard_map/ppermute | solution.py:258
  4.5 3.8 %collective-permute-start.3 = (f32[4,2048]{1,0:T(4,128)S(1)}, f32[4,2048]{1,0:T(4,128)S(1)}, u32[]{:S(2)}, u32[]{:S(2)}) collective-permute-start(f32[4,2048]{1,0:T(4,128)S(1)} %get-tuple-element.26), channel_id=1, source_target_pairs={{0,4},{1,2},{2,1},{3,7},{4,0},{5,6},{6,5},{7,3},{8,12},{9,10},{10,... | collective-permute-start | bytes 98312 | tf_op jit(solution)/shard_map/ppermute | solution.py:259
  9.0 1.6 %collective-permute-start.4 = (f32[8,4,16,128]{3,2,1,0:T(8,128)S(1)}, f32[8,4,16,128]{3,2,1,0:T(8,128)S(1)}, u32[]{:S(2)}, u32[]{:S(2)}) collective-permute-start(f32[8,4,16,128]{3,2,1,0:T(8,128)S(1)} %shard_map.58), channel_id=1, source_target_pairs={{0,4},{4,0},{8,12},{12,8},{16,20},{20,16},{24,28},{28,24},{1,5},{5... | collective-permute-start | bytes 786440 | tf_op jit(solution)/shard_map/ppermute | solution.py:282
  10.6 4.9 %collective-permute-start.5 = (f32[2,4,16,128]{3,2,1,0:T(8,128)S(1)}, f32[2,4,16,128]{3,2,1,0:T(8,128)S(1)}, u32[]{:S(2)}, u32[]{:S(2)}) collective-permute-start(f32[2,4,16,128]{3,2,1,0:T(8,128)S(1)} %get-tuple-element.28), channel_id=1, source_target_pairs={{0,8},{4,12},{8,0},{12,4},{16,24},{20,28},{24,16},{28,20},{1,9},{5... | collective-permute-start | bytes 196616 | tf_op jit(solution)/shard_map/ppermute | solution.py:287
  12.8 5.0 %collective-permute-start.6 = (f32[2,4,16,128]{3,2,1,0:T(8,128)S(1)}, f32[2,4,16,128]{3,2,1,0:T(8,128)S(1)}, u32[]{:S(2)}, u32[]{:S(2)}) collective-permute-start(f32[2,4,16,128]{3,2,1,0:T(8,128)S(1)} %get-tuple-element.29), channel_id=1, source_target_pairs={{0,16},{4,20},{8,24},{12,28},{16,0},{20,4},{24,8},{28,12},{1,17},{... | collective-permute-start | bytes 196616 | tf_op jit(solution)/shard_map/ppermute | solution.py:287
  13.4 5.2 %collective-permute-start.7 = (f32[2,4,16,128]{3,2,1,0:T(8,128)S(1)}, f32[2,4,16,128]{3,2,1,0:T(8,128)S(1)}, u32[]{:S(2)}, u32[]{:S(2)}) collective-permute-start(f32[2,4,16,128]{3,2,1,0:T(8,128)S(1)} %get-tuple-element.30), channel_id=1, source_target_pairs={{0,24},{4,28},{8,16},{12,20},{16,8},{20,12},{24,0},{28,4},{1,25},{... | collective-permute-start | bytes 196616 | tf_op jit(solution)/shard_map/ppermute | solution.py:287

commit v4 on v3

--- a/solution.py
+++ b/solution.py
@@ -213,8 +213,13 @@
                 out[h, ch] = value
 
 
+def finish_order(chips):
+    return [0] + sorted(range(1, chips), key=lambda k: (-k.bit_count(), k))
+
+
 def finish_kernel(*refs):
-    pieces, out = refs[:-1], refs[-1]
+    given, out = dict(zip(finish_order(len(refs) - 1), refs)), refs[-1]
+    pieces = [given[k] for k in range(len(given))]
     chip = lax.axis_index("depth") // 2
     for h in range(pieces[0].shape[0]):
         values = [[piece[h, ch] for ch in range(4)] for piece in pieces]
@@ -287,7 +292,7 @@
             lax.ppermute(blocks[k], "depth", [(i, i ^ (2 * k)) for i in range(groups)])
             for k in range(1, chips)
         ]
-        return call(finish_kernel, array(4, rows, width), [VMEM] * chips, 1_000_000)(*pieces)
+        return call(finish_kernel, array(4, rows, width), [VMEM] * chips, 1_000_000)(*[pieces[k] for k in finish_order(chips)])
 
     partial_value = call(
         functools.partial(shade_kernel, lambda i: i), array(tiles, 4, rows, LANES), [VMEM] * 6, 4_000_000

time: 19.4 us -> 19 us (0.979)
  waiting for transfers between devices: 5.83 us -> 5.46 us
    ppermute x3, waiting for transfers between devices: 4.23 us -> 3.86 us  [on_device(): lax.ppermute(blocks[k], 'depth', [(i, i ^ 2 * k) for i in range(groups)])]
where the time goes in v4:
time: 19 us; the launch traced here: 18.8 us
  starting transfers between devices  8.26 us (43%)
  waiting for transfers between devices  5.46 us (29%)
  Pallas kernels  5.04 us (27%)
    ppermute x3, waiting for transfers between devices, on_device(): lax.ppermute(blocks[k], 'depth', [(i, i ^ 2 * k) for i in range(groups)])  3.86 us
    ppermute x3, starting transfers between devices, on_device(): lax.ppermute(blocks[k], 'depth', [(i, i ^ 2 * k) for i in range(groups)])  3.7 us
    ppermute x1, starting transfers between devices, on_device(): far_z = lax.ppermute(outer_z, both, outer_pairs(groups, strips, 'depth'))  2.65 us
    pallas_call x1, Pallas kernels, on_device(): call(lookup_kernel, array(tiles, slices * 3 + 1, rows, LANES), [VMEM] * 5...  1.92 us
    ppermute x1, starting transfers between devices, on_device(): far_y = lax.ppermute(outer_y, both, outer_pairs(groups, strips, 'strip'))  1.25 us
    pallas_call x1, Pallas kernels, on_device(): pl.pallas_call(load_kernel, out_shape=[jax.ShapeDtypeStruct(x.shape, x.dt...  1.25 us
    pallas_call x2, Pallas kernels, on_device(): call(functools.partial(shade_kernel, block_order(other)), half, [VMEM] *...  1.17 us
    ppermute x1, waiting for transfers between devices, on_device(): received = lax.ppermute(sent, 'depth', inner_pairs(groups))  0.94 us
  transfers between devices with their start and end apart: 8, of which 5 were waited for; matrix products, arithmetic and copies ran while one was open for 0% of the time, Pallas kernels for 13%

profile of v4, /device:TPU:0, one launch (start us, length us, event | category | flops | bytes accessed | tf_op | source)
XLA Modules:
  0.0 18.8 jit_solution(8470307205315519962)
XLA Ops:
  0.0 1.2 %shard_map.55 = (f32[4,16,2048]{2,1,0:T(8,128)S(1)}, s32[4,16,2048]{2,1,0:T(8,128)S(1)}, s32[1,16]{1,0:T(1,128)S(1)}, f32[3,4,16]{2,1,0:T(4,128)S(1)}, f32[4,16]...) custom-call(f32[4,16,2048]{2,1,0:T(8,128)} %refs_0_.1, ...), custom_call_target="tpu_custom_call" | custom-call | tf_op jit(solution)/shard_map/pallas_call | solution.py:252
  1.3 0.5 %collective-permute-start = (f32[1,16,2048]{2,1,0:T(8,128)S(1)}, f32[1,16,2048]{2,1,0:T(8,128)S(1)}, u32[]{:S(2)}, u32[]{:S(2)}) collective-permute-start(f32[1,16,2048]{2,1,0:T(8,128)S(1)} %get-tuple-element.23), channel_id=1, source_target_pairs={{0,4},{4,0},{8,12},{12,8},{16,20},{20,16},{24,28},{28,24},{1,5},{5... | collective-permute-start | bytes 393224 | tf_op jit(solution)/shard_map/ppermute | solution.py:262
  1.8 2.6 %collective-permute-start.1 = (f32[1,16,2048]{2,1,0:T(8,128)S(1)}, f32[1,16,2048]{2,1,0:T(8,128)S(1)}, u32[]{:S(2)}, u32[]{:S(2)}) collective-permute-start(f32[1,16,2048]{2,1,0:T(8,128)S(1)} %get-tuple-element.24), channel_id=1, source_target_pairs={{0,1},{1,0},{2,3},{3,2},{4,8},{5,9},{6,10},{7,11},{8,4},{9,5},{10,... | collective-permute-start | bytes 393224 | tf_op jit(solution)/shard_map/ppermute | solution.py:261
  4.4 0.1 collective-permute-start.2
  4.5 1.2 %collective-permute-start.3 = (f32[4,2048]{1,0:T(4,128)S(1)}, f32[4,2048]{1,0:T(4,128)S(1)}, u32[]{:S(2)}, u32[]{:S(2)}) collective-permute-start(f32[4,2048]{1,0:T(4,128)S(1)} %get-tuple-element.26), channel_id=1, source_target_pairs={{0,4},{1,2},{2,1},{3,7},{4,0},{5,6},{6,5},{7,3},{8,12},{9,10},{10,... | collective-permute-start | bytes 98312 | tf_op jit(solution)/shard_map/ppermute | solution.py:264
  5.8 1.9 %shard_map.56.weights = f32[16,13,16,128]{3,2,1,0:T(8,128)S(1)} custom-call(f32[4,16,2048]{2,1,0:T(8,128)S(1)} %get-tuple-element.18.density, s32[4,16,2048]{2,1,0:T(8,128)S(1)} %get-tuple-element.19.materials, s32[1,16]{1,0:T(1,128)S(1)} %get-tuple-element.20.flags, f32[3,4,16]{2,1,0:T(4,128)S(1)} %get-tuple-element.21.tf_color, ...), custom_call_target="tpu_custom_call" | custom-call | flops 8000000 | bytes 8000000 | tf_op jit(solution)/shard_map/pallas_call | solution.py:266
  7.7 0.7 %collective-permute-done.2.near_y = f32[4,2048]{1,0:T(4,128)S(1)} collective-permute-done((f32[4,2048]{1,0:T(4,128)S(1)}, f32[4,2048]{1,0:T(4,128)S(1)}, u32[]{:S(2)}, u32[]{:S(2)}) %collective-permute-start.2) | collective-permute-done | bytes 32800 | tf_op jit(solution)/shard_map/ppermute | solution.py:263
  8.3 0.0 collective-permute-done.3.far_y
  8.3 0.0 collective-permute-done.near_z
  8.3 0.0 collective-permute-done.1.far_z
  8.4 0.6 %shard_map.58 = f32[8,4,16,128]{3,2,1,0:T(8,128)S(1)} custom-call(f32[4,16,2048]{2,1,0:T(8,128)S(1)} %get-tuple-element.18.density, f32[16,13,16,128]{3,2,1,0:T(8,128)S(1)} %shard_map.56.weights, f32[1,16,2048]{2,1,0:T(8,128)S(1)} %collective-permute-done.near_z, f32[1,16,2048]{2,1,0:T(8,128)S(1)} %collective-permute-done.1.far_z, ...), custom_call_target="tpu_custom_call" | custom-call | flops 2000000 | bytes 2000000 | tf_op jit(solution)/shard_map/pallas_call | solution.py:284
  9.0 0.1 collective-permute-start.4
  9.0 0.6 %shard_map.57.kept = f32[8,4,16,128]{3,2,1,0:T(8,128)S(1)} custom-call(f32[4,16,2048]{2,1,0:T(8,128)S(1)} %get-tuple-element.18.density, f32[16,13,16,128]{3,2,1,0:T(8,128)S(1)} %shard_map.56.weights, f32[1,16,2048]{2,1,0:T(8,128)S(1)} %collective-permute-done.near_z, f32[1,16,2048]{2,1,0:T(8,128)S(1)} %collective-permute-done.1.far_z, ...), custom_call_target="tpu_custom_call" | custom-call | flops 2000000 | bytes 2000000 | tf_op jit(solution)/shard_map/pallas_call | solution.py:284
  9.6 0.9 %collective-permute-done.4.received = f32[8,4,16,128]{3,2,1,0:T(8,128)S(1)} collective-permute-done((f32[8,4,16,128]{3,2,1,0:T(8,128)S(1)}, f32[8,4,16,128]{3,2,1,0:T(8,128)S(1)}, u32[]{:S(2)}, u32[]{:S(2)}) %collective-permute-start.4) | collective-permute-done | bytes 262176 | tf_op jit(solution)/shard_map/ppermute | solution.py:287
  10.6 2.3 %collective-permute-start.5 = (f32[2,4,16,128]{3,2,1,0:T(8,128)S(1)}, f32[2,4,16,128]{3,2,1,0:T(8,128)S(1)}, u32[]{:S(2)}, u32[]{:S(2)}) collective-permute-start(f32[2,4,16,128]{3,2,1,0:T(8,128)S(1)} %get-tuple-element.28), channel_id=1, source_target_pairs={{0,24},{4,28},{8,16},{12,20},{16,8},{20,12},{24,0},{28,4},{1,25},{... | collective-permute-start | bytes 196616 | tf_op jit(solution)/shard_map/ppermute | solution.py:292
  12.9 1.0 %collective-permute-start.6 = (f32[2,4,16,128]{3,2,1,0:T(8,128)S(1)}, f32[2,4,16,128]{3,2,1,0:T(8,128)S(1)}, u32[]{:S(2)}, u32[]{:S(2)}) collective-permute-start(f32[2,4,16,128]{3,2,1,0:T(8,128)S(1)} %get-tuple-element.29), channel_id=1, source_target_pairs={{0,8},{4,12},{8,0},{12,4},{16,24},{20,28},{24,16},{28,20},{1,9},{5... | collective-permute-start | bytes 196616 | tf_op jit(solution)/shard_map/ppermute | solution.py:292
  13.9 0.4 %collective-permute-start.7 = (f32[2,4,16,128]{3,2,1,0:T(8,128)S(1)}, f32[2,4,16,128]{3,2,1,0:T(8,128)S(1)}, u32[]{:S(2)}, u32[]{:S(2)}) collective-permute-start(f32[2,4,16,128]{3,2,1,0:T(8,128)S(1)} %get-tuple-element.30), channel_id=1, source_target_pairs={{0,16},{4,20},{8,24},{12,28},{16,0},{20,4},{24,8},{28,12},{1,17},{... | collective-permute-start | bytes 196616 | tf_op jit(solution)/shard_map/ppermute | solution.py:292
  14.3 1.5 %collective-permute-done.5.refs_1_ = f32[2,4,16,128]{3,2,1,0:T(8,128)S(1)} collective-permute-done((f32[2,4,16,128]{3,2,1,0:T(8,128)S(1)}, f32[2,4,16,128]{3,2,1,0:T(8,128)S(1)}, u32[]{:S(2)}, u32[]{:S(2)}) %collective-permute-start.5) | collective-permute-done | bytes 65568 | tf_op jit(solution)/shard_map/ppermute | solution.py:292
  15.8 1.6 %collective-permute-done.6.refs_2_ = f32[2,4,16,128]{3,2,1,0:T(8,128)S(1)} collective-permute-done((f32[2,4,16,128]{3,2,1,0:T(8,128)S(1)}, f32[2,4,16,128]{3,2,1,0:T(8,128)S(1)}, u32[]{:S(2)}, u32[]{:S(2)}) %collective-permute-start.6) | collective-permute-done | bytes 65568 | tf_op jit(solution)/shard_map/ppermute | solution.py:292
  17.4 0.7 %collective-permute-done.7.refs_3_ = f32[2,4,16,128]{3,2,1,0:T(8,128)S(1)} collective-permute-done((f32[2,4,16,128]{3,2,1,0:T(8,128)S(1)}, f32[2,4,16,128]{3,2,1,0:T(8,128)S(1)}, u32[]{:S(2)}, u32[]{:S(2)}) %collective-permute-start.7) | collective-permute-done | bytes 65568 | tf_op jit(solution)/shard_map/ppermute | solution.py:292
  18.2 0.7 %shard_map.60 = f32[4,16,256]{2,1,0:T(8,128)} custom-call(f32[2,4,16,128]{3,2,1,0:T(8,128)S(1)} %get-tuple-element.27.refs_0_, f32[2,4,16,128]{3,2,1,0:T(8,128)S(1)} %collective-permute-done.5.refs_1_, f32[2,4,16,128]{3,2,1,0:T(8,128)S(1)} %collective-permute-done.6.refs_2_, f32[2,4,16,128]{3,2,1,0:T(8,128)S(1)} %collective-permute-done.7.refs_3_), custom_call_target="tpu_custom_call" | custom-call | flops 1000000 | bytes 1000000 | tf_op jit(solution)/shard_map/pallas_call | solution.py:295
  (1 shorter events, 0.0 us)
Async XLA Ops:
  1.3 7.1 %collective-permute-start = (f32[1,16,2048]{2,1,0:T(8,128)S(1)}, f32[1,16,2048]{2,1,0:T(8,128)S(1)}, u32[]{:S(2)}, u32[]{:S(2)}) collective-permute-start(f32[1,16,2048]{2,1,0:T(8,128)S(1)} %get-tuple-element.23), channel_id=1, source_target_pairs={{0,4},{4,0},{8,12},{12,8},{16,20},{20,16},{24,28},{28,24},{1,5},{5... | collective-permute-start | bytes 393224 | tf_op jit(solution)/shard_map/ppermute | solution.py:262
  1.8 6.6 %collective-permute-start.1 = (f32[1,16,2048]{2,1,0:T(8,128)S(1)}, f32[1,16,2048]{2,1,0:T(8,128)S(1)}, u32[]{:S(2)}, u32[]{:S(2)}) collective-permute-start(f32[1,16,2048]{2,1,0:T(8,128)S(1)} %get-tuple-element.24), channel_id=1, source_target_pairs={{0,1},{1,0},{2,3},{3,2},{4,8},{5,9},{6,10},{7,11},{8,4},{9,5},{10,... | collective-permute-start | bytes 393224 | tf_op jit(solution)/shard_map/ppermute | solution.py:261
  4.4 3.9 %collective-permute-start.2 = (f32[4,2048]{1,0:T(4,128)S(1)}, f32[4,2048]{1,0:T(4,128)S(1)}, u32[]{:S(2)}, u32[]{:S(2)}) collective-permute-start(f32[4,2048]{1,0:T(4,128)S(1)} %get-tuple-element.25), channel_id=1, source_target_pairs={{0,1},{1,0},{2,3},{3,2},{4,5},{5,4},{6,7},{7,6},{8,9},{9,8},{10,11... | collective-permute-start | bytes 98312 | tf_op jit(solution)/shard_map/ppermute | solution.py:263
  4.5 3.8 %collective-permute-start.3 = (f32[4,2048]{1,0:T(4,128)S(1)}, f32[4,2048]{1,0:T(4,128)S(1)}, u32[]{:S(2)}, u32[]{:S(2)}) collective-permute-start(f32[4,2048]{1,0:T(4,128)S(1)} %get-tuple-element.26), channel_id=1, source_target_pairs={{0,4},{1,2},{2,1},{3,7},{4,0},{5,6},{6,5},{7,3},{8,12},{9,10},{10,... | collective-permute-start | bytes 98312 | tf_op jit(solution)/shard_map/ppermute | solution.py:264
  9.0 1.6 %collective-permute-start.4 = (f32[8,4,16,128]{3,2,1,0:T(8,128)S(1)}, f32[8,4,16,128]{3,2,1,0:T(8,128)S(1)}, u32[]{:S(2)}, u32[]{:S(2)}) collective-permute-start(f32[8,4,16,128]{3,2,1,0:T(8,128)S(1)} %shard_map.58), channel_id=1, source_target_pairs={{0,4},{4,0},{8,12},{12,8},{16,20},{20,16},{24,28},{28,24},{1,5},{5... | collective-permute-start | bytes 786440 | tf_op jit(solution)/shard_map/ppermute | solution.py:287
  10.6 5.2 %collective-permute-start.5 = (f32[2,4,16,128]{3,2,1,0:T(8,128)S(1)}, f32[2,4,16,128]{3,2,1,0:T(8,128)S(1)}, u32[]{:S(2)}, u32[]{:S(2)}) collective-permute-start(f32[2,4,16,128]{3,2,1,0:T(8,128)S(1)} %get-tuple-element.28), channel_id=1, source_target_pairs={{0,24},{4,28},{8,16},{12,20},{16,8},{20,12},{24,0},{28,4},{1,25},{... | collective-permute-start | bytes 196616 | tf_op jit(solution)/shard_map/ppermute | solution.py:292
  12.9 4.6 %collective-permute-start.6 = (f32[2,4,16,128]{3,2,1,0:T(8,128)S(1)}, f32[2,4,16,128]{3,2,1,0:T(8,128)S(1)}, u32[]{:S(2)}, u32[]{:S(2)}) collective-permute-start(f32[2,4,16,128]{3,2,1,0:T(8,128)S(1)} %get-tuple-element.29), channel_id=1, source_target_pairs={{0,8},{4,12},{8,0},{12,4},{16,24},{20,28},{24,16},{28,20},{1,9},{5... | collective-permute-start | bytes 196616 | tf_op jit(solution)/shard_map/ppermute | solution.py:292
  13.9 4.3 %collective-permute-start.7 = (f32[2,4,16,128]{3,2,1,0:T(8,128)S(1)}, f32[2,4,16,128]{3,2,1,0:T(8,128)S(1)}, u32[]{:S(2)}, u32[]{:S(2)}) collective-permute-start(f32[2,4,16,128]{3,2,1,0:T(8,128)S(1)} %get-tuple-element.30), channel_id=1, source_target_pairs={{0,16},{4,20},{8,24},{12,28},{16,0},{20,4},{24,8},{28,12},{1,17},{... | collective-permute-start | bytes 196616 | tf_op jit(solution)/shard_map/ppermute | solution.py:292

commit v5 on v4

--- a/solution.py
+++ b/solution.py
@@ -124,10 +124,10 @@
             out[c, slices * 3, band, :] = transmit
         return 0
 
-    lax.fori_loop(0, columns // LANES, body, 0, unroll=4)
-
-
-def shade_kernel(order, density, weights, near_z, far_z, near_y, far_y, out):
+    lax.fori_loop(0, columns // LANES, body, 0, unroll=16)
+
+
+def shade_kernel(order, density, weights, far_z, near_y, far_y, near_z, out):
     slices, rows, columns = density.shape
     tiles = columns // LANES
     bands = rows // ROWS
@@ -190,7 +190,7 @@
             out[i, 3, band, :] = weights[c, slices * 3, band, :]
         return 0
 
-    lax.fori_loop(0, out.shape[0], body, 0, unroll=2)
+    lax.fori_loop(0, out.shape[0], body, 0, unroll=8)
 
 
 def over(swap, nearer, farther):
@@ -266,7 +266,7 @@
     weights = call(
         lookup_kernel, array(tiles, slices * 3 + 1, rows, LANES), [VMEM] * 5, 8_000_000
     )(density, materials, flags, tf_color, tf_opacity)
-    lit = (density, weights, near_z, far_z, near_y, far_y)
+    lit = (density, weights, far_z, near_y, far_y, near_z)
 
     paired = groups % 2 == 0 and chips & (chips - 1) == 0 and width % LANES == 0
     if paired:

time: 19 us -> 18.7 us (0.984)
  Pallas kernels: 5.04 us -> 4.38 us
  waiting for transfers between devices: 5.46 us -> 5.76 us
    ppermute x1, starting transfers between devices: 0.08 us -> 1.58 us  [on_device(): near_y = lax.ppermute(inner_y, 'strip', inner_pairs(strips))]
    ppermute x1, starting transfers between devices: 1.25 us -> 0.01 us  [on_device(): far_y = lax.ppermute(outer_y, both, outer_pairs(groups, strips, 'strip'))]
    ppermute x1, starting transfers between devices: 0.52 us -> 0.03 us  [on_device(): near_z = lax.ppermute(inner_z, 'depth', inner_pairs(groups))]
    ppermute x1, starting transfers between devices: 2.65 us -> 3.09 us  [on_device(): far_z = lax.ppermute(outer_z, both, outer_pairs(groups, strips, 'depth'))]
    pallas_call x2, Pallas kernels: 1.17 us -> 0.77 us  [on_device(): call(functools.partial(shade_kernel, block_order(other)), half, [VMEM] *...]
    pallas_call x1, Pallas kernels: 1.92 us -> 1.67 us  [on_device(): call(lookup_kernel, array(tiles, slices * 3 + 1, rows, LANES), [VMEM] * 5...]
    ppermute x1, waiting for transfers between devices: 0.94 us -> 1.14 us  [on_device(): received = lax.ppermute(sent, 'depth', inner_pairs(groups))]
  transfers between devices with their start and end apart: 8 -> 8, of which waited for: 5 -> 5; matrix products, arithmetic and copies ran while one was open for 0% -> 0% of each run, Pallas kernels for 13% -> 11%
where the time goes in v5:
time: 18.7 us; the launch traced here: 18.6 us
  starting transfers between devices  8.37 us (45%)
  waiting for transfers between devices  5.76 us (31%)
  Pallas kernels  4.38 us (23%)
    ppermute x3, waiting for transfers between devices, on_device(): lax.ppermute(blocks[k], 'depth', [(i, i ^ 2 * k) for i in range(groups)])  3.95 us
    ppermute x3, starting transfers between devices, on_device(): lax.ppermute(blocks[k], 'depth', [(i, i ^ 2 * k) for i in range(groups)])  3.6 us
    ppermute x1, starting transfers between devices, on_device(): far_z = lax.ppermute(outer_z, both, outer_pairs(groups, strips, 'depth'))  3.09 us
    pallas_call x1, Pallas kernels, on_device(): call(lookup_kernel, array(tiles, slices * 3 + 1, rows, LANES), [VMEM] * 5...  1.67 us
    ppermute x1, starting transfers between devices, on_device(): near_y = lax.ppermute(inner_y, 'strip', inner_pairs(strips))  1.58 us
    pallas_call x1, Pallas kernels, on_device(): pl.pallas_call(load_kernel, out_shape=[jax.ShapeDtypeStruct(x.shape, x.dt...  1.25 us
    ppermute x1, waiting for transfers between devices, on_device(): received = lax.ppermute(sent, 'depth', inner_pairs(groups))  1.14 us
    pallas_call x2, Pallas kernels, on_device(): call(functools.partial(shade_kernel, block_order(other)), half, [VMEM] *...  0.77 us
  transfers between devices with their start and end apart: 8, of which 5 were waited for; matrix products, arithmetic and copies ran while one was open for 0% of the time, Pallas kernels for 11%

profile of v5, /device:TPU:0, one launch (start us, length us, event | category | flops | bytes accessed | tf_op | source)
XLA Modules:
  0.0 18.6 jit_solution(6306135582871529302)
XLA Ops:
  0.0 1.2 %shard_map.55 = (f32[4,16,2048]{2,1,0:T(8,128)S(1)}, s32[4,16,2048]{2,1,0:T(8,128)S(1)}, s32[1,16]{1,0:T(1,128)S(1)}, f32[3,4,16]{2,1,0:T(4,128)S(1)}, f32[4,16]...) custom-call(f32[4,16,2048]{2,1,0:T(8,128)} %refs_0_.1, ...), custom_call_target="tpu_custom_call" | custom-call | tf_op jit(solution)/shard_map/pallas_call | solution.py:252
  1.3 3.1 %collective-permute-start = (f32[1,16,2048]{2,1,0:T(8,128)S(1)}, f32[1,16,2048]{2,1,0:T(8,128)S(1)}, u32[]{:S(2)}, u32[]{:S(2)}) collective-permute-start(f32[1,16,2048]{2,1,0:T(8,128)S(1)} %get-tuple-element.23), channel_id=1, source_target_pairs={{0,1},{1,0},{2,3},{3,2},{4,8},{5,9},{6,10},{7,11},{8,4},{9,5},{10,... | collective-permute-start | bytes 393224 | tf_op jit(solution)/shard_map/ppermute | solution.py:261
  4.3 0.0 collective-permute-start.3
  4.4 1.6 %collective-permute-start.1 = (f32[4,2048]{1,0:T(4,128)S(1)}, f32[4,2048]{1,0:T(4,128)S(1)}, u32[]{:S(2)}, u32[]{:S(2)}) collective-permute-start(f32[4,2048]{1,0:T(4,128)S(1)} %get-tuple-element.24), channel_id=1, source_target_pairs={{0,1},{1,0},{2,3},{3,2},{4,5},{5,4},{6,7},{7,6},{8,9},{9,8},{10,11... | collective-permute-start | bytes 98312 | tf_op jit(solution)/shard_map/ppermute | solution.py:263
  6.0 0.0 collective-permute-start.2
  6.0 1.7 %shard_map.56.weights = f32[16,13,16,128]{3,2,1,0:T(8,128)S(1)} custom-call(f32[4,16,2048]{2,1,0:T(8,128)S(1)} %get-tuple-element.18.density, s32[4,16,2048]{2,1,0:T(8,128)S(1)} %get-tuple-element.19.materials, s32[1,16]{1,0:T(1,128)S(1)} %get-tuple-element.20.flags, f32[3,4,16]{2,1,0:T(4,128)S(1)} %get-tuple-element.21.tf_color, ...), custom_call_target="tpu_custom_call" | custom-call | flops 8000000 | bytes 8000000 | tf_op jit(solution)/shard_map/pallas_call | solution.py:266
  7.6 0.7 %collective-permute-done.1.near_y = f32[4,2048]{1,0:T(4,128)S(1)} collective-permute-done((f32[4,2048]{1,0:T(4,128)S(1)}, f32[4,2048]{1,0:T(4,128)S(1)}, u32[]{:S(2)}, u32[]{:S(2)}) %collective-permute-start.1) | collective-permute-done | bytes 32800 | tf_op jit(solution)/shard_map/ppermute | solution.py:263
  8.3 0.0 collective-permute-done.2.far_y
  8.3 0.0 collective-permute-done.far_z
  8.3 0.0 collective-permute-done.3.near_z
  8.3 0.4 %shard_map.58 = f32[8,4,16,128]{3,2,1,0:T(8,128)S(1)} custom-call(f32[4,16,2048]{2,1,0:T(8,128)S(1)} %get-tuple-element.18.density, f32[16,13,16,128]{3,2,1,0:T(8,128)S(1)} %shard_map.56.weights, f32[1,16,2048]{2,1,0:T(8,128)S(1)} %collective-permute-done.far_z, f32[4,2048]{1,0:T(4,128)S(1)} %collective-permute-done.1.near_y, ...), custom_call_target="tpu_custom_call" | custom-call | flops 2000000 | bytes 2000000 | tf_op jit(solution)/shard_map/pallas_call | solution.py:284
  8.7 0.1 collective-permute-start.4
  8.8 0.4 %shard_map.57.kept = f32[8,4,16,128]{3,2,1,0:T(8,128)S(1)} custom-call(f32[4,16,2048]{2,1,0:T(8,128)S(1)} %get-tuple-element.18.density, f32[16,13,16,128]{3,2,1,0:T(8,128)S(1)} %shard_map.56.weights, f32[1,16,2048]{2,1,0:T(8,128)S(1)} %collective-permute-done.far_z, f32[4,2048]{1,0:T(4,128)S(1)} %collective-permute-done.1.near_y, ...), custom_call_target="tpu_custom_call" | custom-call | flops 2000000 | bytes 2000000 | tf_op jit(solution)/shard_map/pallas_call | solution.py:284
  9.1 1.1 %collective-permute-done.4.received = f32[8,4,16,128]{3,2,1,0:T(8,128)S(1)} collective-permute-done((f32[8,4,16,128]{3,2,1,0:T(8,128)S(1)}, f32[8,4,16,128]{3,2,1,0:T(8,128)S(1)}, u32[]{:S(2)}, u32[]{:S(2)}) %collective-permute-start.4) | collective-permute-done | bytes 262176 | tf_op jit(solution)/shard_map/ppermute | solution.py:287
  10.3 2.7 %collective-permute-start.5 = (f32[2,4,16,128]{3,2,1,0:T(8,128)S(1)}, f32[2,4,16,128]{3,2,1,0:T(8,128)S(1)}, u32[]{:S(2)}, u32[]{:S(2)}) collective-permute-start(f32[2,4,16,128]{3,2,1,0:T(8,128)S(1)} %get-tuple-element.28), channel_id=1, source_target_pairs={{0,24},{4,28},{8,16},{12,20},{16,8},{20,12},{24,0},{28,4},{1,25},{... | collective-permute-start | bytes 196616 | tf_op jit(solution)/shard_map/ppermute | solution.py:292
  13.1 0.6 %collective-permute-start.6 = (f32[2,4,16,128]{3,2,1,0:T(8,128)S(1)}, f32[2,4,16,128]{3,2,1,0:T(8,128)S(1)}, u32[]{:S(2)}, u32[]{:S(2)}) collective-permute-start(f32[2,4,16,128]{3,2,1,0:T(8,128)S(1)} %get-tuple-element.29), channel_id=1, source_target_pairs={{0,8},{4,12},{8,0},{12,4},{16,24},{20,28},{24,16},{28,20},{1,9},{5... | collective-permute-start | bytes 196616 | tf_op jit(solution)/shard_map/ppermute | solution.py:292
  13.6 0.3 %collective-permute-start.7 = (f32[2,4,16,128]{3,2,1,0:T(8,128)S(1)}, f32[2,4,16,128]{3,2,1,0:T(8,128)S(1)}, u32[]{:S(2)}, u32[]{:S(2)}) collective-permute-start(f32[2,4,16,128]{3,2,1,0:T(8,128)S(1)} %get-tuple-element.30), channel_id=1, source_target_pairs={{0,16},{4,20},{8,24},{12,28},{16,0},{20,4},{24,8},{28,12},{1,17},{... | collective-permute-start | bytes 196616 | tf_op jit(solution)/shard_map/ppermute | solution.py:292
  13.9 1.6 %collective-permute-done.5.refs_1_ = f32[2,4,16,128]{3,2,1,0:T(8,128)S(1)} collective-permute-done((f32[2,4,16,128]{3,2,1,0:T(8,128)S(1)}, f32[2,4,16,128]{3,2,1,0:T(8,128)S(1)}, u32[]{:S(2)}, u32[]{:S(2)}) %collective-permute-start.5) | collective-permute-done | bytes 65568 | tf_op jit(solution)/shard_map/ppermute | solution.py:292
  15.6 1.8 %collective-permute-done.6.refs_2_ = f32[2,4,16,128]{3,2,1,0:T(8,128)S(1)} collective-permute-done((f32[2,4,16,128]{3,2,1,0:T(8,128)S(1)}, f32[2,4,16,128]{3,2,1,0:T(8,128)S(1)}, u32[]{:S(2)}, u32[]{:S(2)}) %collective-permute-start.6) | collective-permute-done | bytes 65568 | tf_op jit(solution)/shard_map/ppermute | solution.py:292
  17.3 0.6 %collective-permute-done.7.refs_3_ = f32[2,4,16,128]{3,2,1,0:T(8,128)S(1)} collective-permute-done((f32[2,4,16,128]{3,2,1,0:T(8,128)S(1)}, f32[2,4,16,128]{3,2,1,0:T(8,128)S(1)}, u32[]{:S(2)}, u32[]{:S(2)}) %collective-permute-start.7) | collective-permute-done | bytes 65568 | tf_op jit(solution)/shard_map/ppermute | solution.py:292
  17.9 0.7 %shard_map.60 = f32[4,16,256]{2,1,0:T(8,128)} custom-call(f32[2,4,16,128]{3,2,1,0:T(8,128)S(1)} %get-tuple-element.27.refs_0_, f32[2,4,16,128]{3,2,1,0:T(8,128)S(1)} %collective-permute-done.5.refs_1_, f32[2,4,16,128]{3,2,1,0:T(8,128)S(1)} %collective-permute-done.6.refs_2_, f32[2,4,16,128]{3,2,1,0:T(8,128)S(1)} %collective-permute-done.7.refs_3_), custom_call_target="tpu_custom_call" | custom-call | flops 1000000 | bytes 1000000 | tf_op jit(solution)/shard_map/pallas_call | solution.py:295
  (1 shorter events, 0.0 us)
Async XLA Ops:
  1.3 7.0 %collective-permute-start = (f32[1,16,2048]{2,1,0:T(8,128)S(1)}, f32[1,16,2048]{2,1,0:T(8,128)S(1)}, u32[]{:S(2)}, u32[]{:S(2)}) collective-permute-start(f32[1,16,2048]{2,1,0:T(8,128)S(1)} %get-tuple-element.23), channel_id=1, source_target_pairs={{0,1},{1,0},{2,3},{3,2},{4,8},{5,9},{6,10},{7,11},{8,4},{9,5},{10,... | collective-permute-start | bytes 393224 | tf_op jit(solution)/shard_map/ppermute | solution.py:261
  4.3 4.0 %collective-permute-start.3 = (f32[1,16,2048]{2,1,0:T(8,128)S(1)}, f32[1,16,2048]{2,1,0:T(8,128)S(1)}, u32[]{:S(2)}, u32[]{:S(2)}) collective-permute-start(f32[1,16,2048]{2,1,0:T(8,128)S(1)} %get-tuple-element.26), channel_id=1, source_target_pairs={{0,4},{4,0},{8,12},{12,8},{16,20},{20,16},{24,28},{28,24},{1,5},{5... | collective-permute-start | bytes 393224 | tf_op jit(solution)/shard_map/ppermute | solution.py:262
  4.4 3.9 %collective-permute-start.1 = (f32[4,2048]{1,0:T(4,128)S(1)}, f32[4,2048]{1,0:T(4,128)S(1)}, u32[]{:S(2)}, u32[]{:S(2)}) collective-permute-start(f32[4,2048]{1,0:T(4,128)S(1)} %get-tuple-element.24), channel_id=1, source_target_pairs={{0,1},{1,0},{2,3},{3,2},{4,5},{5,4},{6,7},{7,6},{8,9},{9,8},{10,11... | collective-permute-start | bytes 98312 | tf_op jit(solution)/shard_map/ppermute | solution.py:263
  6.0 2.3 %collective-permute-start.2 = (f32[4,2048]{1,0:T(4,128)S(1)}, f32[4,2048]{1,0:T(4,128)S(1)}, u32[]{:S(2)}, u32[]{:S(2)}) collective-permute-start(f32[4,2048]{1,0:T(4,128)S(1)} %get-tuple-element.25), channel_id=1, source_target_pairs={{0,4},{1,2},{2,1},{3,7},{4,0},{5,6},{6,5},{7,3},{8,12},{9,10},{10,... | collective-permute-start | bytes 98312 | tf_op jit(solution)/shard_map/ppermute | solution.py:264
  8.7 1.6 %collective-permute-start.4 = (f32[8,4,16,128]{3,2,1,0:T(8,128)S(1)}, f32[8,4,16,128]{3,2,1,0:T(8,128)S(1)}, u32[]{:S(2)}, u32[]{:S(2)}) collective-permute-start(f32[8,4,16,128]{3,2,1,0:T(8,128)S(1)} %shard_map.58), channel_id=1, source_target_pairs={{0,4},{4,0},{8,12},{12,8},{16,20},{20,16},{24,28},{28,24},{1,5},{5... | collective-permute-start | bytes 786440 | tf_op jit(solution)/shard_map/ppermute | solution.py:287
  10.3 5.2 %collective-permute-start.5 = (f32[2,4,16,128]{3,2,1,0:T(8,128)S(1)}, f32[2,4,16,128]{3,2,1,0:T(8,128)S(1)}, u32[]{:S(2)}, u32[]{:S(2)}) collective-permute-start(f32[2,4,16,128]{3,2,1,0:T(8,128)S(1)} %get-tuple-element.28), channel_id=1, source_target_pairs={{0,24},{4,28},{8,16},{12,20},{16,8},{20,12},{24,0},{28,4},{1,25},{... | collective-permute-start | bytes 196616 | tf_op jit(solution)/shard_map/ppermute | solution.py:292
  13.1 4.3 %collective-permute-start.6 = (f32[2,4,16,128]{3,2,1,0:T(8,128)S(1)}, f32[2,4,16,128]{3,2,1,0:T(8,128)S(1)}, u32[]{:S(2)}, u32[]{:S(2)}) collective-permute-start(f32[2,4,16,128]{3,2,1,0:T(8,128)S(1)} %get-tuple-element.29), channel_id=1, source_target_pairs={{0,8},{4,12},{8,0},{12,4},{16,24},{20,28},{24,16},{28,20},{1,9},{5... | collective-permute-start | bytes 196616 | tf_op jit(solution)/shard_map/ppermute | solution.py:292
  13.6 4.3 %collective-permute-start.7 = (f32[2,4,16,128]{3,2,1,0:T(8,128)S(1)}, f32[2,4,16,128]{3,2,1,0:T(8,128)S(1)}, u32[]{:S(2)}, u32[]{:S(2)}) collective-permute-start(f32[2,4,16,128]{3,2,1,0:T(8,128)S(1)} %get-tuple-element.30), channel_id=1, source_target_pairs={{0,16},{4,20},{8,24},{12,28},{16,0},{20,4},{24,8},{28,12},{1,17},{... | collective-permute-start | bytes 196616 | tf_op jit(solution)/shard_map/ppermute | solution.py:292

commit v6 on v3

v6 whole, which is shorter than its diff:
```python
import functools

import jax
import jax.numpy as jnp
from jax import lax
from jax.experimental import pallas as pl
from jax.experimental.pallas import tpu as pltpu
from jax.sharding import PartitionSpec as P

ambient = 0.3
diffuse = 0.7
LANES = 128
ROWS = 8
VMEM = pl.BlockSpec(memory_space=pltpu.VMEM)


def inner_pairs(count):
    return [(i, i ^ 1) for i in range(count)]


def outer_pairs(groups, strips, axis):
    pairs = []
    for g in range(groups):
        for s in range(strips):
            if axis == "depth":
                to = (g, s ^ 1) if g in (0, groups - 1) else (g + 1 if g % 2 else g - 1, s)
            else:
                to = (g ^ 1, s) if s in (0, strips - 1) else (g, s + 1 if s % 2 else s - 1)
            pairs.append((g * strips + s, to[0] * strips + to[1]))
    return pairs


def tile(c):
    return pl.ds(pl.multiple_of(c * LANES, LANES), LANES)


def call(kernel, out_shape, args, after=()):
    count = len(args)

    def body(*refs):
        kernel(*refs[:count], *refs[count + len(after) :])

    return pl.pallas_call(
        body,
        out_shape=out_shape,
        in_specs=[VMEM] * count + [pl.BlockSpec(memory_space=pl.ANY)] * len(after),
        out_specs=jax.tree.map(lambda _: VMEM, out_shape),
        cost_estimate=pl.CostEstimate(flops=2_000_000, bytes_accessed=2_000_000, transcendentals=0),
        compiler_params=pltpu.CompilerParams(vmem_limit_bytes=16 * 1024 * 1024),
    )(*args, *after)


def array(*shape):
    return jax.ShapeDtypeStruct(shape, jnp.float32)


def load_kernel(order, *refs):
    density, materials, flags, tf_color, tf_opacity = refs[:5]
    brick, held_materials, held_color, held_opacity, layer, inner_y, outer_y, held_flags, sems = refs[5:]
    slices, rows, columns = density.shape
    pairs = (
        (density, brick.at[:, :, pl.ds(0, columns)]),
        (materials, held_materials),
        (flags, held_flags),
        (tf_color, held_color),
        (tf_opacity, held_opacity),
    )
    copies = [pltpu.make_async_copy(x, y, sems.at[i]) for i, (x, y) in enumerate(pairs)]
    for copy in copies:
        copy.start()
    odd_z = lax.axis_index("depth") % 2
    odd_y = lax.axis_index("strip") % 2 == 1
    copies[0].wait()
    layer[0] = brick[(slices - 1) * odd_z, :, :columns]
    for z in range(slices):
        first, last = brick[z, :1, :columns], brick[z, rows - 1 :, :columns]
        inner_y[z : z + 1, :] = jnp.where(odd_y, first, last)
        outer_y[z : z + 1, :] = jnp.where(odd_y, last, first)
    for copy in copies[1:]:
        copy.wait()
    half = columns // LANES // 2
    for i in range(half):
        given = held_materials[:, :, tile(order(1, i))].astype(jnp.float32)
        brick[:, :, columns + i * LANES : columns + (i + 1) * LANES] = given
    occupied = [held_flags[:, :].astype(jnp.float32)] * (LANES // flags.shape[1])
    occupied = jnp.concatenate(occupied, axis=1)
    brick[0, :ROWS, columns + half * LANES :] = jnp.broadcast_to(occupied, (ROWS, LANES))


def by_lane(table):
    here = [table[m : m + 1, :] for m in range(table.shape[0])]
    last = table.shape[1] - 1
    further = [jnp.concatenate([t[:, 1:], t[:, last:]], axis=1) for t in here]
    return jnp.concatenate(here + here, axis=1), jnp.concatenate(further + further, axis=1)


def lookup_kernel(order, columns, start, brick, tf_color, tf_opacity, *refs):
    materials, out = refs if len(refs) == 2 else (None, refs[0])
    slices, rows = brick.shape[:2]
    knots = tf_opacity.shape[1]
    lane = lax.broadcasted_iota(jnp.int32, (1, LANES), 1)
    table = []
    for ch in range(3):
        value, further = by_lane(tf_color[ch])
        low = (further * 65535.0 + 0.5).astype(jnp.int32)
        high = jnp.floor((value * (32767.0 * 65536.0) - low.astype(jnp.float32)) * (1.0 / 65536.0) + 0.5)
        table.append(jnp.broadcast_to(high.astype(jnp.int32) * 65536 + low, (ROWS, LANES)))
    value, further = by_lane(tf_opacity[...])
    rates = jnp.broadcast_to(jnp.where(lane < LANES // 2, value, further - value), (ROWS, LANES))

    occupied = brick[0, :ROWS, columns + columns // 2 :]

    def look(t, index):
        return jnp.take_along_axis(t, index, axis=1, mode="promise_in_bounds")

    def body(at, _):
        i = start + at
        c = order(0, i)
        here = tile(c)
        present = look(occupied, jnp.full((ROWS, LANES), c, jnp.int32))
        for b in range(rows // ROWS):
            band = slice(b * ROWS, (b + 1) * ROWS)
            transmit = None
            for z in range(slices):
                position = jnp.clip(
                    (brick[z, band, here] + 3.0) * ((knots - 1) / 6.0), 0.0, knots - 1.0
                )
                whole = position.astype(jnp.int32)
                part = position - whole.astype(jnp.float32)
                if materials is None:
                    material = brick[z, band, tile(columns // LANES + i)].astype(jnp.int32)
                else:
                    material = materials[z, band, here]
                index = material * knots + whole
                rate = look(rates, index) + part * look(rates, index + LANES // 2)
                clear = jnp.exp(-(rate * present))
                weight = 1.0 - clear
                if z:
                    weight = weight * transmit
                of_low = (part * weight) * (1.0 / 65535.0)
                of_high = (weight - part * weight) * (1.0 / (32767.0 * 65536.0))
                for ch in range(3):
                    both = look(table[ch], index)
                    low = (both & 65535).astype(jnp.float32)
                    out[at, z * 3 + ch, band, :] = both.astype(jnp.float32) * of_high + low * of_low
                transmit = transmit * clear if z else clear
            out[at, slices * 3, band, :] = transmit
        return 0

    lax.fori_loop(0, out.shape[0], body, 0, unroll=out.shape[0])


def over(swap, nearer, farther):
    first = [jnp.where(swap, f, n) for n, f in zip(nearer, farther)]
    second = [jnp.where(swap, n, f) for n, f in zip(nearer, farther)]
    return [first[ch] + first[3] * second[ch] for ch in range(3)] + [first[3] * second[3]]


def hand_kernel(order, far_z, near_y, far_y, out):
    _, rows, _ = far_z.shape
    slices = near_y.shape[0]
    for i in range(out.shape[0]):
        here = tile(order(1, i))
        out[i, :rows, :] = far_z[0, :, here]
        out[i, rows : rows + slices, :] = near_y[:, here]
        out[i, rows + slices :, :] = far_y[:, here]


def shade(order, columns, start, outs, brick, beside, weights, layer, near_row, far_row, odd_slab, finish):
    slices, rows = brick.shape[:2]
    tiles, bands = columns // LANES, rows // ROWS
    lane = lax.broadcasted_iota(jnp.int32, (ROWS, LANES), 1)
    row = lax.broadcasted_iota(jnp.int32, (ROWS, LANES), 0)
    chip, chips = lax.axis_index("depth") // 2, lax.axis_size("depth") // 2
    at_y = lax.axis_index("strip")
    odd_y = at_y % 2 == 1
    has_nearer = jnp.where(chip > 0, 1.0, 0.0)
    has_farther = jnp.where(chip < chips - 1, 1.0, 0.0)
    has_top = jnp.where(at_y > 0, 1.0, 0.0)
    has_bottom = jnp.where(at_y < lax.axis_size("strip") - 1, 1.0, 0.0)
    facing_layer = jnp.where(odd_slab, slices - 1, 0)
    work = [(out, h) for out in outs for h in range(out.shape[0])]
    for i, (out, h) in enumerate(work, start):
        c = order(0, i)
        here, left, right = tile(c), tile(jnp.maximum(c - 1, 0)), tile(jnp.minimum(c + 1, tiles - 1))
        has_left = jnp.where(c > 0, 1.0, 0.0)
        has_right = jnp.where(c < tiles - 1, 1.0, 0.0)
        d = [[brick[z, b * ROWS : (b + 1) * ROWS, here] for b in range(bands)] for z in range(slices)]
        for b in range(bands):
            band = slice(b * ROWS, (b + 1) * ROWS)
            radiance = [None] * 3
            for z in range(slices):
                v = d[z][b]
                if z == 0:
                    nearer = jnp.where(odd_slab, beside[facing_layer, band, here], layer(i, c, band) * has_nearer)
                else:
                    nearer = d[z - 1][b]
                if z == slices - 1:
                    farther = jnp.where(odd_slab, layer(i, c, band) * has_farther, beside[facing_layer, band, here])
                else:
                    farther = d[z + 1][b]
                dz = farther - nearer
                if b == 0:
                    top = jnp.where(odd_y, near_row(i, c, z), far_row(i, c, z))
                    top = jnp.broadcast_to(top * has_top, (ROWS, LANES))
                else:
                    top = d[z][b - 1]
                if b == bands - 1:
                    bottom = jnp.where(odd_y, far_row(i, c, z), near_row(i, c, z))
                    bottom = jnp.broadcast_to(bottom * has_bottom, (ROWS, LANES))
                else:
                    bottom = d[z][b + 1]
                dy = pltpu.roll(jnp.where(row == 0, bottom, v), ROWS - 1, 0) - pltpu.roll(
                    jnp.where(row == ROWS - 1, top, v), 1, 0
                )
                vl = brick[z, band, left] * has_left
                vr = brick[z, band, right] * has_right
                dx = pltpu.roll(jnp.where(lane == 0, vr, v), LANES - 1, 1) - pltpu.roll(
                    jnp.where(lane == LANES - 1, vl, v), 1, 1
                )
                facing = jnp.abs(dx + 2.0 * (dy + dz))
                lighting = ambient + (diffuse / 3.0) * facing * lax.rsqrt(
                    4.0 + (dx * dx + dy * dy + dz * dz)
                )
                for ch in range(3):
                    term = weights[i - start, z * 3 + ch, band, :] * lighting
                    radiance[ch] = radiance[ch] + term if z else term
            image = finish(i - start, band, radiance + [weights[i - start, slices * 3, band, :]])
            for ch in range(4):
                out[h, ch, band, :] = image[ch]


def own_kernel(order, columns, start, brick, beside, weights, far_z, near_y, far_y, out):
    shade(
        order,
        columns,
        start,
        [out],
        brick,
        beside,
        weights,
        lambda i, c, band: far_z[0, band, tile(c)],
        lambda i, c, z: near_y[z : z + 1, tile(c)],
        lambda i, c, z: far_y[z : z + 1, tile(c)],
        lax.axis_index("depth") % 2 == 1,
        lambda i, band, image: image,
    )


def chip_kernel(order, columns, start, brick, beside, weights, handed, mine, *outs):
    slices, rows = brick.shape[:2]
    odd = lax.axis_index("depth") % 2 == 1
    shade(
        order,
        columns,
        start,
        outs,
        brick,
        beside,
        weights,
        lambda i, c, band: handed[i, band, :],
        lambda i, c, z: handed[i, rows + z : rows + z + 1, :],
        lambda i, c, z: handed[i, rows + slices + z : rows + slices + z + 1, :],
        lax.axis_index("depth") % 2 == 0,
        lambda i, band, image: over(odd, [mine[i, ch, band, :] for ch in range(4)], image),
    )


def chip_order(chips):
    return sorted(range(chips), key=lambda k: (-k.bit_count(), k))


def finish_kernel(*refs):
    given, out = dict(zip(chip_order(len(refs) - 1), refs)), refs[-1]
    pieces = [given[k] for k in range(len(given))]
    chip = lax.axis_index("depth") // 2
    for h in range(pieces[0].shape[0]):
        values = [[piece[h, ch] for ch in range(4)] for piece in pieces]
        bit = 0
        while len(values) > 1:
            swap = (chip >> bit) % 2 == 1
            values = [over(swap, values[k], values[k + 1]) for k in range(0, len(values), 2)]
            bit += 1
        here = slice(h * LANES, (h + 1) * LANES)
        for ch in range(3):
            out[ch, :, here] = values[0][ch]
        out[3, :, here] = 1.0 - values[0][3]


def composite_over(nearer, farther):
    return jnp.concatenate(
        [nearer[:, :3] + nearer[:, 3:] * farther[:, :3], nearer[:, 3:] * farther[:, 3:]], axis=1
    )


def on_device(density, materials, occupancy_flags, tf_color, tf_opacity):
    slices, rows, columns = density.shape
    tiles = columns // LANES
    groups, strips = lax.axis_size("depth"), lax.axis_size("strip")
    width = columns // groups
    chips, half = groups // 2, tiles // 2
    paired = chips & (chips - 1) == 0 and width % LANES == 0
    per = width // LANES if paired else half
    ks = chip_order(chips) if paired else [0]

    def order(other, i):
        index = lax.axis_index("depth")
        parity = (index + other) % 2
        if not paired:
            return parity * half + i
        k = sum(jnp.where(i // per == n, ks[n], 0) for n in range(chips))
        return ((index // 2 ^ k) * 2 + parity) * per + i % per

    given = (density, materials, occupancy_flags[0], tf_color.transpose(1, 0, 2), tf_opacity)
    whole = array(slices, rows, columns + half * LANES + LANES)
    edge = array(slices, columns)
    brick, materials, tf_color, tf_opacity, layer, inner_y, outer_y = pl.pallas_call(
        functools.partial(load_kernel, order),
        out_shape=[whole]
        + [jax.ShapeDtypeStruct(given[n].shape, given[n].dtype) for n in (1, 3, 4)]
        + [array(1, rows, columns), edge, edge],
        in_specs=[pl.BlockSpec(memory_space=pltpu.HBM)] * 5,
        out_specs=[VMEM] * 7,
        scratch_shapes=[pltpu.VMEM(given[2].shape, jnp.int32), pltpu.SemaphoreType.DMA((5,))],
        compiler_params=pltpu.CompilerParams(vmem_limit_bytes=16 * 1024 * 1024),
    )(*[pltpu.with_memory_space_constraint(x, pltpu.HBM) for x in given])
    both = ("depth", "strip")
    beside = lax.ppermute(brick, "depth", inner_pairs(groups))
    far_z = lax.ppermute(layer, both, outer_pairs(groups, strips, "depth"))
    near_y = lax.ppermute(inner_y, "strip", inner_pairs(strips))
    far_y = lax.ppermute(outer_y, both, outer_pairs(groups, strips, "strip"))

    far = (chips - 1) * per if paired else half

    def weigh(first, count, after=()):
        lookup = functools.partial(lookup_kernel, order, columns, first)
        shape = array(count, slices * 3 + 1, rows, LANES)
        mine = call(lookup, shape, (brick, tf_color, tf_opacity, materials), after)
        return mine, call(lookup, shape, (beside, tf_color, tf_opacity), (mine,))

    weights, weights_beside = weigh(0, far)
    handing = call(
        functools.partial(hand_kernel, order),
        array(half, rows + 2 * slices, LANES),
        (far_z, near_y, far_y),
        (weights_beside,),
    )
    handed = lax.ppermute(handing, "depth", inner_pairs(groups))

    def images(first, count, blocks, weights, weights_beside):
        mine = call(
            functools.partial(own_kernel, order, columns, first),
            array(count, 4, rows, LANES),
            (brick, beside, weights, far_z, near_y, far_y),
        )
        return call(
            functools.partial(chip_kernel, order, columns, first),
            [array(count // blocks, 4, rows, LANES)] * blocks,
            (beside, brick, weights_beside, handed, mine),
        )

    if paired:
        sent = images(0, far, chips - 1, weights, weights_beside)
        moved = [
            lax.ppermute(image, "depth", [(i, i ^ (2 * k)) for i in range(groups)])
            for image, k in zip(sent, ks)
        ]
        (kept,) = images(far, per, 1, *weigh(far, per, sent[-1:]))
        return call(finish_kernel, array(4, rows, width), (*moved, kept))

    (image,) = images(0, half, 1, weights, weights_beside)
    clear = jnp.zeros_like(image).at[:, 3].set(1.0)
    odd = lax.axis_index("depth") % 2 == 1
    partial_value = jnp.concatenate(
        [jnp.where(odd, clear, image), jnp.where(odd, image, clear)], axis=0
    )
    natural = partial_value.transpose(1, 2, 0, 3).reshape(4, rows, groups, width)
    pieces = lax.all_to_all(
        natural.transpose(2, 0, 1, 3), "depth", split_axis=0, concat_axis=0, tiled=True
    )
    while pieces.shape[0] > 1:
        pieces = composite_over(pieces[0::2], pieces[1::2])
    finished = pieces[0]
    return jnp.concatenate([finished[:3], 1.0 - finished[3:]], axis=0)


def solution(mesh):
    placed = (
        P("depth", "strip", None),
        P("depth", "strip", None),
        P("depth", "strip", None),
        P(),
        P(),
    )
    return jax.shard_map(
        on_device, mesh=mesh, in_specs=placed, out_specs=P(None, "strip", "depth"), check_vma=False
    )
```

time: 19.4 us -> 18.5 us (0.954)
  waiting for transfers between devices: 5.83 us -> 4.62 us
  Pallas kernels: 5.04 us -> 5.37 us
    ppermute x6, waiting for transfers between devices: 5.17 us -> 3.65 us  [the longest x3 2.64 us: on_device(): lax.ppermute(image, 'depth', [(i, i ^ 2 * k) for i in range(groups)])]
    pallas_call x6 -> x11, Pallas kernels: 5.04 us -> 5.37 us  [the longest x10 4.04 us: call(): pl.pallas_call(body, out_shape=out_shape, in_specs=[VMEM] * count + [pl.B...]
    ppermute x1, waiting for transfers between devices: 0.66 us -> 0.97 us  [on_device(): near_y = lax.ppermute(inner_y, 'strip', inner_pairs(strips))]
  transfers between devices with their start and end apart: 8 -> 8, of which waited for: 5 -> 5; matrix products, arithmetic and copies ran while one was open for 0% -> 0% of each run, Pallas kernels for 13% -> 17%
where the time goes in v6:
time: 18.5 us; the launch traced here: 18.4 us
  starting transfers between devices  8.32 us (45%)
  Pallas kernels  5.37 us (29%)
  waiting for transfers between devices  4.62 us (25%)
    pallas_call x10, Pallas kernels, call(): pl.pallas_call(body, out_shape=out_shape, in_specs=[VMEM] * count + [pl.B...  4.04 us
    ppermute x3, starting transfers between devices, on_device(): lax.ppermute(image, 'depth', [(i, i ^ 2 * k) for i in range(groups)])  3.75 us
    ppermute x1, starting transfers between devices, on_device(): far_z = lax.ppermute(layer, both, outer_pairs(groups, strips, 'depth'))  2.65 us
    ppermute x3, waiting for transfers between devices, on_device(): lax.ppermute(image, 'depth', [(i, i ^ 2 * k) for i in range(groups)])  2.64 us
    pallas_call x1, Pallas kernels, on_device(): pl.pallas_call(functools.partial(load_kernel, order), out_shape=[whole] +...  1.33 us
    ppermute x1, starting transfers between devices, on_device(): far_y = lax.ppermute(outer_y, both, outer_pairs(groups, strips, 'strip'))  1.25 us
    ppermute x1, waiting for transfers between devices, on_device(): handed = lax.ppermute(handing, 'depth', inner_pairs(groups))  1 us
    ppermute x1, waiting for transfers between devices, on_device(): near_y = lax.ppermute(inner_y, 'strip', inner_pairs(strips))  0.97 us
  transfers between devices with their start and end apart: 8, of which 5 were waited for; matrix products, arithmetic and copies ran while one was open for 0% of the time, Pallas kernels for 17%

profile of v6, /device:TPU:0, one launch (start us, length us, event | category | flops | bytes accessed | tf_op | source)
XLA Modules:
  0.0 18.4 jit_solution(4267640048133241505)
XLA Ops:
  0.0 1.3 %shard_map.55 = (f32[4,16,3200]{2,1,0:T(8,128)S(1)}, s32[4,16,2048]{2,1,0:T(8,128)S(1)}, f32[3,4,16]{2,1,0:T(4,128)S(1)}, f32[4,16]{1,0:T(4,128)S(1)}, f32[1,16,...) custom-call(f32[4,16,2048]{2,1,0:T(8,128)} %refs_0_.1, s32[4,16,2048]{2,1,0:T(8,128)} %refs_1_.1, ...), custom_call_target="tpu_custom_call" | custom-call | tf_op jit(solution)/shard_map/pallas_call | solution.py:317
  1.3 0.5 %collective-permute-start = (f32[4,16,3200]{2,1,0:T(8,128)S(1)}, f32[4,16,3200]{2,1,0:T(8,128)S(1)}, u32[]{:S(2)}, u32[]{:S(2)}) collective-permute-start(f32[4,16,3200]{2,1,0:T(8,128)S(1)} %get-tuple-element.15.refs_0_.refs_1_), channel_id=1, source_target_pairs={{0,4},{4,0},{8,12},{12,8},{16,20},{20,16},{24,28},{28,24},{1,5},{5... | collective-permute-start | bytes 2457608 | tf_op jit(solution)/shard_map/ppermute | solution.py:328
  1.9 2.6 %collective-permute-start.1 = (f32[1,16,2048]{2,1,0:T(8,128)S(1)}, f32[1,16,2048]{2,1,0:T(8,128)S(1)}, u32[]{:S(2)}, u32[]{:S(2)}) collective-permute-start(f32[1,16,2048]{2,1,0:T(8,128)S(1)} %get-tuple-element.19), channel_id=1, source_target_pairs={{0,1},{1,0},{2,3},{3,2},{4,8},{5,9},{6,10},{7,11},{8,4},{9,5},{10,... | collective-permute-start | bytes 393224 | tf_op jit(solution)/shard_map/ppermute | solution.py:329
  4.5 0.1 collective-permute-start.2
  4.6 1.2 %collective-permute-start.3 = (f32[4,2048]{1,0:T(4,128)S(1)}, f32[4,2048]{1,0:T(4,128)S(1)}, u32[]{:S(2)}, u32[]{:S(2)}) collective-permute-start(f32[4,2048]{1,0:T(4,128)S(1)} %get-tuple-element.21), channel_id=1, source_target_pairs={{0,4},{1,2},{2,1},{3,7},{4,0},{5,6},{6,5},{7,3},{8,12},{9,10},{10,... | collective-permute-start | bytes 98312 | tf_op jit(solution)/shard_map/ppermute | solution.py:331
  5.8 0.8 %shard_map.56.refs_3_.refs_2_ = f32[6,13,16,128]{3,2,1,0:T(8,128)S(1)} custom-call(f32[4,16,3200]{2,1,0:T(8,128)S(1)} %get-tuple-element.15.refs_0_.refs_1_, f32[3,4,16]{2,1,0:T(4,128)S(1)} %get-tuple-element.16.refs_1_, f32[4,16]{1,0:T(4,128)S(1)} %get-tuple-element.17.refs_2_, s32[4,16,2048]{2,1,0:T(8,128)S(1)} %get-tuple-element.18.refs_3_), custom_call_target="tpu_custom_call" | custom-call | flops 2000000 | bytes 2000000 | tf_op jit(solution)/shard_map/pallas_call | solution.py:43
  6.6 0.0 collective-permute-done.refs_0_.refs_1_
  6.6 0.8 %shard_map.57.refs_3_.refs_2_ = f32[6,13,16,128]{3,2,1,0:T(8,128)S(1)} custom-call(f32[4,16,3200]{2,1,0:T(8,128)S(1)} %collective-permute-done.refs_0_.refs_1_, f32[3,4,16]{2,1,0:T(4,128)S(1)} %get-tuple-element.16.refs_1_, f32[4,16]{1,0:T(4,128)S(1)} %get-tuple-element.17.refs_2_, f32[6,13,16,128]{3,2,1,0:T(8,128)S(1)} %shard_map.56.refs_3_.refs_2_), custom_call_target="tpu_custom_call" | custom-call | flops 2000000 | bytes 2000000 | tf_op jit(solution)/shard_map/pallas_call | solution.py:43
  7.4 1.0 %collective-permute-done.2.refs_1_.refs_4_ = f32[4,2048]{1,0:T(4,128)S(1)} collective-permute-done((f32[4,2048]{1,0:T(4,128)S(1)}, f32[4,2048]{1,0:T(4,128)S(1)}, u32[]{:S(2)}, u32[]{:S(2)}) %collective-permute-start.2) | collective-permute-done | bytes 32800 | tf_op jit(solution)/shard_map/ppermute | solution.py:330
  8.5 0.1 collective-permute-start.4
  8.5 0.3 %shard_map.59.refs_4_ = f32[6,4,16,128]{3,2,1,0:T(8,128)S(1)} custom-call(f32[4,16,3200]{2,1,0:T(8,128)S(1)} %get-tuple-element.15.refs_0_.refs_1_, f32[4,16,3200]{2,1,0:T(8,128)S(1)} %collective-permute-done.refs_0_.refs_1_, f32[6,13,16,128]{3,2,1,0:T(8,128)S(1)} %shard_map.56.refs_3_.refs_2_, f32[1,16,2048]{2,1,0:T(8,128)S(1)} %collective-permute-done.1.refs_0_.refs_3_, ...), custom_call_target="tpu_custom_call" | custom-call | flops 2000000 | bytes 2000000 | tf_op jit(solution)/shard_map/pallas_call | solution.py:43
  8.8 1.0 %collective-permute-done.4.refs_3_ = f32[8,24,128]{2,1,0:T(8,128)S(1)} collective-permute-done((f32[8,24,128]{2,1,0:T(8,128)S(1)}, f32[8,24,128]{2,1,0:T(8,128)S(1)}, u32[]{:S(2)}, u32[]{:S(2)}) %collective-permute-start.4) | collective-permute-done | bytes 98336 | tf_op jit(solution)/shard_map/ppermute | solution.py:348
  9.8 0.3 %shard_map.60 = (f32[2,4,16,128]{3,2,1,0:T(8,128)S(1)}, f32[2,4,16,128]{3,2,1,0:T(8,128)S(1)}, f32[2,4,16,128]{3,2,1,0:T(8,128)S(1)}) custom-call(f32[4,16,3200]{2,1,0:T(8,128)S(1)} %collective-permute-done.refs_0_.refs_1_, f32[4,16,3200]{2,1,0:T(8,128)S(1)} %get-tuple-element.15.refs_0_.refs_1_, f32[6,13,16,128]{3,2,1,0:T(8,128)S(1)} %shard_map.57.refs_3_.refs_2_, ...), custom_call_target="tpu_custom_call" | custom-call | flops 2000000 | bytes 2000000 | tf_op jit(solution)/shard_map/pallas_call | solution.py:43
  10.1 2.3 %collective-permute-start.5 = (f32[2,4,16,128]{3,2,1,0:T(8,128)S(1)}, f32[2,4,16,128]{3,2,1,0:T(8,128)S(1)}, u32[]{:S(2)}, u32[]{:S(2)}) collective-permute-start(f32[2,4,16,128]{3,2,1,0:T(8,128)S(1)} %get-tuple-element.22), channel_id=1, source_target_pairs={{0,24},{4,28},{8,16},{12,20},{16,8},{20,12},{24,0},{28,4},{1,25},{... | collective-permute-start | bytes 196616 | tf_op jit(solution)/shard_map/ppermute | solution.py:365
  12.4 1.0 %collective-permute-start.6 = (f32[2,4,16,128]{3,2,1,0:T(8,128)S(1)}, f32[2,4,16,128]{3,2,1,0:T(8,128)S(1)}, u32[]{:S(2)}, u32[]{:S(2)}) collective-permute-start(f32[2,4,16,128]{3,2,1,0:T(8,128)S(1)} %get-tuple-element.23), channel_id=1, source_target_pairs={{0,8},{4,12},{8,0},{12,4},{16,24},{20,28},{24,16},{28,20},{1,9},{5... | collective-permute-start | bytes 196616 | tf_op jit(solution)/shard_map/ppermute | solution.py:365
  13.4 0.4 %collective-permute-start.7 = (f32[2,4,16,128]{3,2,1,0:T(8,128)S(1)}, f32[2,4,16,128]{3,2,1,0:T(8,128)S(1)}, u32[]{:S(2)}, u32[]{:S(2)}) collective-permute-start(f32[2,4,16,128]{3,2,1,0:T(8,128)S(1)} %get-tuple-element.24.refs_4_), channel_id=1, source_target_pairs={{0,16},{4,20},{8,24},{12,28},{16,0},{20,4},{24,8},{28,12},{1,17},{... | collective-permute-start | bytes 196616 | tf_op jit(solution)/shard_map/ppermute | solution.py:365
  13.9 0.4 %shard_map.61.refs_3_.refs_2_ = f32[2,13,16,128]{3,2,1,0:T(8,128)S(1)} custom-call(f32[4,16,3200]{2,1,0:T(8,128)S(1)} %get-tuple-element.15.refs_0_.refs_1_, f32[3,4,16]{2,1,0:T(4,128)S(1)} %get-tuple-element.16.refs_1_, f32[4,16]{1,0:T(4,128)S(1)} %get-tuple-element.17.refs_2_, s32[4,16,2048]{2,1,0:T(8,128)S(1)} %get-tuple-element.18.refs_3_, ...), custom_call_target="tpu_custom_call" | custom-call | flops 2000000 | bytes 2000000 | tf_op jit(solution)/shard_map/pallas_call | solution.py:43
  14.3 0.1 shard_map.63.refs_4_
  14.5 0.4 %shard_map.62.refs_2_ = f32[2,13,16,128]{3,2,1,0:T(8,128)S(1)} custom-call(f32[4,16,3200]{2,1,0:T(8,128)S(1)} %collective-permute-done.refs_0_.refs_1_, f32[3,4,16]{2,1,0:T(4,128)S(1)} %get-tuple-element.16.refs_1_, f32[4,16]{1,0:T(4,128)S(1)} %get-tuple-element.17.refs_2_, f32[2,13,16,128]{3,2,1,0:T(8,128)S(1)} %shard_map.61.refs_3_.refs_2_), custom_call_target="tpu_custom_call" | custom-call | flops 2000000 | bytes 2000000 | tf_op jit(solution)/shard_map/pallas_call | solution.py:43
  14.9 0.2 shard_map.64.refs_3_
  15.1 0.3 %collective-permute-done.5.refs_0_ = f32[2,4,16,128]{3,2,1,0:T(8,128)S(1)} collective-permute-done((f32[2,4,16,128]{3,2,1,0:T(8,128)S(1)}, f32[2,4,16,128]{3,2,1,0:T(8,128)S(1)}, u32[]{:S(2)}, u32[]{:S(2)}) %collective-permute-start.5) | collective-permute-done | bytes 65568 | tf_op jit(solution)/shard_map/ppermute | solution.py:365
  15.3 1.7 %collective-permute-done.6.refs_1_ = f32[2,4,16,128]{3,2,1,0:T(8,128)S(1)} collective-permute-done((f32[2,4,16,128]{3,2,1,0:T(8,128)S(1)}, f32[2,4,16,128]{3,2,1,0:T(8,128)S(1)}, u32[]{:S(2)}, u32[]{:S(2)}) %collective-permute-start.6) | collective-permute-done | bytes 65568 | tf_op jit(solution)/shard_map/ppermute | solution.py:365
  17.0 0.7 %collective-permute-done.7.refs_2_ = f32[2,4,16,128]{3,2,1,0:T(8,128)S(1)} collective-permute-done((f32[2,4,16,128]{3,2,1,0:T(8,128)S(1)}, f32[2,4,16,128]{3,2,1,0:T(8,128)S(1)}, u32[]{:S(2)}, u32[]{:S(2)}) %collective-permute-start.7) | collective-permute-done | bytes 65568 | tf_op jit(solution)/shard_map/ppermute | solution.py:365
  17.7 0.7 %shard_map.65 = f32[4,16,256]{2,1,0:T(8,128)} custom-call(f32[2,4,16,128]{3,2,1,0:T(8,128)S(1)} %collective-permute-done.5.refs_0_, f32[2,4,16,128]{3,2,1,0:T(8,128)S(1)} %collective-permute-done.6.refs_1_, f32[2,4,16,128]{3,2,1,0:T(8,128)S(1)} %collective-permute-done.7.refs_2_, f32[2,4,16,128]{3,2,1,0:T(8,128)S(1)} %shard_map.64.refs_3_), custom_call_target="tpu_custom_call" | custom-call | flops 2000000 | bytes 2000000 | tf_op jit(solution)/shard_map/pallas_call | solution.py:43
  (3 shorter events, 0.0 us)
Async XLA Ops:
  1.3 5.3 %collective-permute-start = (f32[4,16,3200]{2,1,0:T(8,128)S(1)}, f32[4,16,3200]{2,1,0:T(8,128)S(1)}, u32[]{:S(2)}, u32[]{:S(2)}) collective-permute-start(f32[4,16,3200]{2,1,0:T(8,128)S(1)} %get-tuple-element.15.refs_0_.refs_1_), channel_id=1, source_target_pairs={{0,4},{4,0},{8,12},{12,8},{16,20},{20,16},{24,28},{28,24},{1,5},{5... | collective-permute-start | bytes 2457608 | tf_op jit(solution)/shard_map/ppermute | solution.py:328
  1.9 6.6 %collective-permute-start.1 = (f32[1,16,2048]{2,1,0:T(8,128)S(1)}, f32[1,16,2048]{2,1,0:T(8,128)S(1)}, u32[]{:S(2)}, u32[]{:S(2)}) collective-permute-start(f32[1,16,2048]{2,1,0:T(8,128)S(1)} %get-tuple-element.19), channel_id=1, source_target_pairs={{0,1},{1,0},{2,3},{3,2},{4,8},{5,9},{6,10},{7,11},{8,4},{9,5},{10,... | collective-permute-start | bytes 393224 | tf_op jit(solution)/shard_map/ppermute | solution.py:329
  4.5 3.9 %collective-permute-start.2 = (f32[4,2048]{1,0:T(4,128)S(1)}, f32[4,2048]{1,0:T(4,128)S(1)}, u32[]{:S(2)}, u32[]{:S(2)}) collective-permute-start(f32[4,2048]{1,0:T(4,128)S(1)} %get-tuple-element.20), channel_id=1, source_target_pairs={{0,1},{1,0},{2,3},{3,2},{4,5},{5,4},{6,7},{7,6},{8,9},{9,8},{10,11... | collective-permute-start | bytes 98312 | tf_op jit(solution)/shard_map/ppermute | solution.py:330
  4.6 3.8 %collective-permute-start.3 = (f32[4,2048]{1,0:T(4,128)S(1)}, f32[4,2048]{1,0:T(4,128)S(1)}, u32[]{:S(2)}, u32[]{:S(2)}) collective-permute-start(f32[4,2048]{1,0:T(4,128)S(1)} %get-tuple-element.21), channel_id=1, source_target_pairs={{0,4},{1,2},{2,1},{3,7},{4,0},{5,6},{6,5},{7,3},{8,12},{9,10},{10,... | collective-permute-start | bytes 98312 | tf_op jit(solution)/shard_map/ppermute | solution.py:331
  8.5 1.4 %collective-permute-start.4 = (f32[8,24,128]{2,1,0:T(8,128)S(1)}, f32[8,24,128]{2,1,0:T(8,128)S(1)}, u32[]{:S(2)}, u32[]{:S(2)}) collective-permute-start(f32[8,24,128]{2,1,0:T(8,128)S(1)} %shard_map.58), channel_id=1, source_target_pairs={{0,4},{4,0},{8,12},{12,8},{16,20},{20,16},{24,28},{28,24},{1,5},{5... | collective-permute-start | bytes 294920 | tf_op jit(solution)/shard_map/ppermute | solution.py:348
  10.1 5.2 %collective-permute-start.5 = (f32[2,4,16,128]{3,2,1,0:T(8,128)S(1)}, f32[2,4,16,128]{3,2,1,0:T(8,128)S(1)}, u32[]{:S(2)}, u32[]{:S(2)}) collective-permute-start(f32[2,4,16,128]{3,2,1,0:T(8,128)S(1)} %get-tuple-element.22), channel_id=1, source_target_pairs={{0,24},{4,28},{8,16},{12,20},{16,8},{20,12},{24,0},{28,4},{1,25},{... | collective-permute-start | bytes 196616 | tf_op jit(solution)/shard_map/ppermute | solution.py:365
  12.4 4.6 %collective-permute-start.6 = (f32[2,4,16,128]{3,2,1,0:T(8,128)S(1)}, f32[2,4,16,128]{3,2,1,0:T(8,128)S(1)}, u32[]{:S(2)}, u32[]{:S(2)}) collective-permute-start(f32[2,4,16,128]{3,2,1,0:T(8,128)S(1)} %get-tuple-element.23), channel_id=1, source_target_pairs={{0,8},{4,12},{8,0},{12,4},{16,24},{20,28},{24,16},{28,20},{1,9},{5... | collective-permute-start | bytes 196616 | tf_op jit(solution)/shard_map/ppermute | solution.py:365
  13.4 4.3 %collective-permute-start.7 = (f32[2,4,16,128]{3,2,1,0:T(8,128)S(1)}, f32[2,4,16,128]{3,2,1,0:T(8,128)S(1)}, u32[]{:S(2)}, u32[]{:S(2)}) collective-permute-start(f32[2,4,16,128]{3,2,1,0:T(8,128)S(1)} %get-tuple-element.24.refs_4_), channel_id=1, source_target_pairs={{0,16},{4,20},{8,24},{12,28},{16,0},{20,4},{24,8},{28,12},{1,17},{... | collective-permute-start | bytes 196616 | tf_op jit(solution)/shard_map/ppermute | solution.py:365

commit v7 on v6

--- a/solution.py
+++ b/solution.py
@@ -66,16 +66,10 @@
         (tf_opacity, held_opacity),
     )
     copies = [pltpu.make_async_copy(x, y, sems.at[i]) for i, (x, y) in enumerate(pairs)]
-    for copy in copies:
+    for copy in copies[1:] + copies[:1]:
         copy.start()
     odd_z = lax.axis_index("depth") % 2
     odd_y = lax.axis_index("strip") % 2 == 1
-    copies[0].wait()
-    layer[0] = brick[(slices - 1) * odd_z, :, :columns]
-    for z in range(slices):
-        first, last = brick[z, :1, :columns], brick[z, rows - 1 :, :columns]
-        inner_y[z : z + 1, :] = jnp.where(odd_y, first, last)
-        outer_y[z : z + 1, :] = jnp.where(odd_y, last, first)
     for copy in copies[1:]:
         copy.wait()
     half = columns // LANES // 2
@@ -85,6 +79,12 @@
     occupied = [held_flags[:, :].astype(jnp.float32)] * (LANES // flags.shape[1])
     occupied = jnp.concatenate(occupied, axis=1)
     brick[0, :ROWS, columns + half * LANES :] = jnp.broadcast_to(occupied, (ROWS, LANES))
+    copies[0].wait()
+    layer[0] = brick[(slices - 1) * odd_z, :, :columns]
+    for z in range(slices):
+        first, last = brick[z, :1, :columns], brick[z, rows - 1 :, :columns]
+        inner_y[z : z + 1, :] = jnp.where(odd_y, first, last)
+        outer_y[z : z + 1, :] = jnp.where(odd_y, last, first)
 
 
 def by_lane(table):
@@ -156,11 +156,11 @@
     return [first[ch] + first[3] * second[ch] for ch in range(3)] + [first[3] * second[3]]
 
 
-def hand_kernel(order, far_z, near_y, far_y, out):
+def hand_kernel(order, start, far_z, near_y, far_y, out):
     _, rows, _ = far_z.shape
     slices = near_y.shape[0]
     for i in range(out.shape[0]):
-        here = tile(order(1, i))
+        here = tile(order(1, start + i))
         out[i, :rows, :] = far_z[0, :, here]
         out[i, rows : rows + slices, :] = near_y[:, here]
         out[i, rows + slices :, :] = far_y[:, here]
@@ -258,9 +258,9 @@
         brick,
         beside,
         weights,
-        lambda i, c, band: handed[i, band, :],
-        lambda i, c, z: handed[i, rows + z : rows + z + 1, :],
-        lambda i, c, z: handed[i, rows + slices + z : rows + slices + z + 1, :],
+        lambda i, c, band: handed[i - start, band, :],
+        lambda i, c, z: handed[i - start, rows + z : rows + z + 1, :],
+        lambda i, c, z: handed[i - start, rows + slices + z : rows + slices + z + 1, :],
         lax.axis_index("depth") % 2 == 0,
         lambda i, band, image: over(odd, [mine[i, ch, band, :] for ch in range(4)], image),
     )
@@ -339,15 +339,18 @@
         return mine, call(lookup, shape, (beside, tf_color, tf_opacity), (mine,))
 
     weights, weights_beside = weigh(0, far)
-    handing = call(
-        functools.partial(hand_kernel, order),
-        array(half, rows + 2 * slices, LANES),
-        (far_z, near_y, far_y),
-        (weights_beside,),
-    )
-    handed = lax.ppermute(handing, "depth", inner_pairs(groups))
-
-    def images(first, count, blocks, weights, weights_beside):
+    def hand(first, count, after):
+        handing = call(
+            functools.partial(hand_kernel, order, first),
+            array(count, rows + 2 * slices, LANES),
+            (far_z, near_y, far_y),
+            after,
+        )
+        return lax.ppermute(handing, "depth", inner_pairs(groups))
+
+    handed = hand(0, far, (weights_beside,))
+
+    def images(first, count, blocks, handed, weights, weights_beside):
         mine = call(
             functools.partial(own_kernel, order, columns, first),
             array(count, 4, rows, LANES),
@@ -360,15 +363,16 @@
         )
 
     if paired:
-        sent = images(0, far, chips - 1, weights, weights_beside)
+        sent = images(0, far, chips - 1, handed, weights, weights_beside)
         moved = [
             lax.ppermute(image, "depth", [(i, i ^ (2 * k)) for i in range(groups)])
             for image, k in zip(sent, ks)
         ]
-        (kept,) = images(far, per, 1, *weigh(far, per, sent[-1:]))
+        late = sent[-1:]
+        (kept,) = images(far, per, 1, hand(far, per, late), *weigh(far, per, late))
         return call(finish_kernel, array(4, rows, width), (*moved, kept))
 
-    (image,) = images(0, half, 1, weights, weights_beside)
+    (image,) = images(0, half, 1, handed, weights, weights_beside)
     clear = jnp.zeros_like(image).at[:, 3].set(1.0)
     odd = lax.axis_index("depth") % 2 == 1
     partial_value = jnp.concatenate(

time: 18.5 us -> 18.5 us (level)
    ppermute x1 -> x2, waiting for transfers between devices: 1 us -> 1.11 us  [hand(): return lax.ppermute(handing, 'depth', inner_pairs(groups))]
    pallas_call x10 -> x11, Pallas kernels: 4.04 us -> 4.03 us  [call(): pl.pallas_call(body, out_shape=out_shape, in_specs=[VMEM] * count + [pl.B...]
  transfers between devices with their start and end apart: 8 -> 9, of which waited for: 5 -> 6; matrix products, arithmetic and copies ran while one was open for 0% -> 0% of each run, Pallas kernels for 17% -> 17%
where the time goes in v7:
time: 18.5 us; the launch traced here: 18.3 us
  starting transfers between devices  8.31 us (45%)
  Pallas kernels  5.34 us (29%)
  waiting for transfers between devices  4.6 us (25%)
    pallas_call x11, Pallas kernels, call(): pl.pallas_call(body, out_shape=out_shape, in_specs=[VMEM] * count + [pl.B...  4.03 us
    ppermute x3, starting transfers between devices, on_device(): lax.ppermute(image, 'depth', [(i, i ^ 2 * k) for i in range(groups)])  3.74 us
    ppermute x1, starting transfers between devices, on_device(): far_z = lax.ppermute(layer, both, outer_pairs(groups, strips, 'depth'))  2.65 us
    ppermute x3, waiting for transfers between devices, on_device(): lax.ppermute(image, 'depth', [(i, i ^ 2 * k) for i in range(groups)])  2.51 us
    pallas_call x1, Pallas kernels, on_device(): pl.pallas_call(functools.partial(load_kernel, order), out_shape=[whole] +...  1.31 us
    ppermute x1, starting transfers between devices, on_device(): far_y = lax.ppermute(outer_y, both, outer_pairs(groups, strips, 'strip'))  1.25 us
    ppermute x2, waiting for transfers between devices, hand(): return lax.ppermute(handing, 'depth', inner_pairs(groups))  1.11 us
    ppermute x1, waiting for transfers between devices, on_device(): near_y = lax.ppermute(inner_y, 'strip', inner_pairs(strips))  0.97 us
  transfers between devices with their start and end apart: 9, of which 6 were waited for; matrix products, arithmetic and copies ran while one was open for 0% of the time, Pallas kernels for 17%

profile of v7, /device:TPU:0, one launch (start us, length us, event | category | flops | bytes accessed | tf_op | source)
XLA Modules:
  0.0 18.3 jit_solution(13201362527503618819)
XLA Ops:
  0.0 1.3 %shard_map.55 = (f32[4,16,3200]{2,1,0:T(8,128)S(1)}, s32[4,16,2048]{2,1,0:T(8,128)S(1)}, f32[3,4,16]{2,1,0:T(4,128)S(1)}, f32[4,16]{1,0:T(4,128)S(1)}, f32[1,16,...) custom-call(f32[4,16,2048]{2,1,0:T(8,128)} %refs_0_.1, s32[4,16,2048]{2,1,0:T(8,128)} %refs_1_.1, ...), custom_call_target="tpu_custom_call" | custom-call | tf_op jit(solution)/shard_map/pallas_call | solution.py:317
  1.3 0.5 %collective-permute-start = (f32[4,16,3200]{2,1,0:T(8,128)S(1)}, f32[4,16,3200]{2,1,0:T(8,128)S(1)}, u32[]{:S(2)}, u32[]{:S(2)}) collective-permute-start(f32[4,16,3200]{2,1,0:T(8,128)S(1)} %get-tuple-element.15.refs_0_.refs_1_), channel_id=1, source_target_pairs={{0,4},{4,0},{8,12},{12,8},{16,20},{20,16},{24,28},{28,24},{1,5},{5... | collective-permute-start | bytes 2457608 | tf_op jit(solution)/shard_map/ppermute | solution.py:328
  1.8 2.6 %collective-permute-start.1 = (f32[1,16,2048]{2,1,0:T(8,128)S(1)}, f32[1,16,2048]{2,1,0:T(8,128)S(1)}, u32[]{:S(2)}, u32[]{:S(2)}) collective-permute-start(f32[1,16,2048]{2,1,0:T(8,128)S(1)} %get-tuple-element.19), channel_id=1, source_target_pairs={{0,1},{1,0},{2,3},{3,2},{4,8},{5,9},{6,10},{7,11},{8,4},{9,5},{10,... | collective-permute-start | bytes 393224 | tf_op jit(solution)/shard_map/ppermute | solution.py:329
  4.5 0.1 collective-permute-start.2
  4.6 1.2 %collective-permute-start.3 = (f32[4,2048]{1,0:T(4,128)S(1)}, f32[4,2048]{1,0:T(4,128)S(1)}, u32[]{:S(2)}, u32[]{:S(2)}) collective-permute-start(f32[4,2048]{1,0:T(4,128)S(1)} %get-tuple-element.21), channel_id=1, source_target_pairs={{0,4},{1,2},{2,1},{3,7},{4,0},{5,6},{6,5},{7,3},{8,12},{9,10},{10,... | collective-permute-start | bytes 98312 | tf_op jit(solution)/shard_map/ppermute | solution.py:331
  5.8 0.8 %shard_map.56.refs_3_.refs_2_ = f32[6,13,16,128]{3,2,1,0:T(8,128)S(1)} custom-call(f32[4,16,3200]{2,1,0:T(8,128)S(1)} %get-tuple-element.15.refs_0_.refs_1_, f32[3,4,16]{2,1,0:T(4,128)S(1)} %get-tuple-element.16.refs_1_, f32[4,16]{1,0:T(4,128)S(1)} %get-tuple-element.17.refs_2_, s32[4,16,2048]{2,1,0:T(8,128)S(1)} %get-tuple-element.18.refs_3_), custom_call_target="tpu_custom_call" | custom-call | flops 2000000 | bytes 2000000 | tf_op jit(solution)/shard_map/pallas_call | solution.py:43
  6.6 0.8 %shard_map.57.refs_3_.refs_2_ = f32[6,13,16,128]{3,2,1,0:T(8,128)S(1)} custom-call(f32[4,16,3200]{2,1,0:T(8,128)S(1)} %collective-permute-done.refs_0_.refs_1_, f32[3,4,16]{2,1,0:T(4,128)S(1)} %get-tuple-element.16.refs_1_, f32[4,16]{1,0:T(4,128)S(1)} %get-tuple-element.17.refs_2_, f32[6,13,16,128]{3,2,1,0:T(8,128)S(1)} %shard_map.56.refs_3_.refs_2_), custom_call_target="tpu_custom_call" | custom-call | flops 2000000 | bytes 2000000 | tf_op jit(solution)/shard_map/pallas_call | solution.py:43
  7.4 1.0 %collective-permute-done.2.refs_1_.refs_4_ = f32[4,2048]{1,0:T(4,128)S(1)} collective-permute-done((f32[4,2048]{1,0:T(4,128)S(1)}, f32[4,2048]{1,0:T(4,128)S(1)}, u32[]{:S(2)}, u32[]{:S(2)}) %collective-permute-start.2) | collective-permute-done | bytes 32800 | tf_op jit(solution)/shard_map/ppermute | solution.py:330
  8.4 0.1 collective-permute-start.4
  8.5 0.3 %shard_map.59.refs_4_ = f32[6,4,16,128]{3,2,1,0:T(8,128)S(1)} custom-call(f32[4,16,3200]{2,1,0:T(8,128)S(1)} %get-tuple-element.15.refs_0_.refs_1_, f32[4,16,3200]{2,1,0:T(8,128)S(1)} %collective-permute-done.refs_0_.refs_1_, f32[6,13,16,128]{3,2,1,0:T(8,128)S(1)} %shard_map.56.refs_3_.refs_2_, f32[1,16,2048]{2,1,0:T(8,128)S(1)} %collective-permute-done.1.refs_0_.refs_3_, ...), custom_call_target="tpu_custom_call" | custom-call | flops 2000000 | bytes 2000000 | tf_op jit(solution)/shard_map/pallas_call | solution.py:43
  8.8 1.0 %collective-permute-done.4.refs_3_ = f32[6,24,128]{2,1,0:T(8,128)S(1)} collective-permute-done((f32[6,24,128]{2,1,0:T(8,128)S(1)}, f32[6,24,128]{2,1,0:T(8,128)S(1)}, u32[]{:S(2)}, u32[]{:S(2)}) %collective-permute-start.4) | collective-permute-done | bytes 73760 | tf_op jit(solution)/shard_map/ppermute | solution.py:349
  9.8 0.3 %shard_map.60 = (f32[2,4,16,128]{3,2,1,0:T(8,128)S(1)}, f32[2,4,16,128]{3,2,1,0:T(8,128)S(1)}, f32[2,4,16,128]{3,2,1,0:T(8,128)S(1)}) custom-call(f32[4,16,3200]{2,1,0:T(8,128)S(1)} %collective-permute-done.refs_0_.refs_1_, f32[4,16,3200]{2,1,0:T(8,128)S(1)} %get-tuple-element.15.refs_0_.refs_1_, f32[6,13,16,128]{3,2,1,0:T(8,128)S(1)} %shard_map.57.refs_3_.refs_2_, ...), custom_call_target="tpu_custom_call" | custom-call | flops 2000000 | bytes 2000000 | tf_op jit(solution)/shard_map/pallas_call | solution.py:43
  10.1 2.3 %collective-permute-start.5 = (f32[2,4,16,128]{3,2,1,0:T(8,128)S(1)}, f32[2,4,16,128]{3,2,1,0:T(8,128)S(1)}, u32[]{:S(2)}, u32[]{:S(2)}) collective-permute-start(f32[2,4,16,128]{3,2,1,0:T(8,128)S(1)} %get-tuple-element.22), channel_id=1, source_target_pairs={{0,24},{4,28},{8,16},{12,20},{16,8},{20,12},{24,0},{28,4},{1,25},{... | collective-permute-start | bytes 196616 | tf_op jit(solution)/shard_map/ppermute | solution.py:368
  12.4 1.0 %collective-permute-start.6 = (f32[2,4,16,128]{3,2,1,0:T(8,128)S(1)}, f32[2,4,16,128]{3,2,1,0:T(8,128)S(1)}, u32[]{:S(2)}, u32[]{:S(2)}) collective-permute-start(f32[2,4,16,128]{3,2,1,0:T(8,128)S(1)} %get-tuple-element.23), channel_id=1, source_target_pairs={{0,8},{4,12},{8,0},{12,4},{16,24},{20,28},{24,16},{28,20},{1,9},{5... | collective-permute-start | bytes 196616 | tf_op jit(solution)/shard_map/ppermute | solution.py:368
  13.4 0.4 %collective-permute-start.7 = (f32[2,4,16,128]{3,2,1,0:T(8,128)S(1)}, f32[2,4,16,128]{3,2,1,0:T(8,128)S(1)}, u32[]{:S(2)}, u32[]{:S(2)}) collective-permute-start(f32[2,4,16,128]{3,2,1,0:T(8,128)S(1)} %get-tuple-element.24.refs_4_.refs_3_), channel_id=1, source_target_pairs={{0,16},{4,20},{8,24},{12,28},{16,0},{20,4},{24,8},{28,12},{1,17},{... | collective-permute-start | bytes 196616 | tf_op jit(solution)/shard_map/ppermute | solution.py:368
  13.8 0.4 %shard_map.61.refs_3_.refs_2_ = f32[2,13,16,128]{3,2,1,0:T(8,128)S(1)} custom-call(f32[4,16,3200]{2,1,0:T(8,128)S(1)} %get-tuple-element.15.refs_0_.refs_1_, f32[3,4,16]{2,1,0:T(4,128)S(1)} %get-tuple-element.16.refs_1_, f32[4,16]{1,0:T(4,128)S(1)} %get-tuple-element.17.refs_2_, s32[4,16,2048]{2,1,0:T(8,128)S(1)} %get-tuple-element.18.refs_3_, ...), custom_call_target="tpu_custom_call" | custom-call | flops 2000000 | bytes 2000000 | tf_op jit(solution)/shard_map/pallas_call | solution.py:43
  14.3 0.1 shard_map.64.refs_4_
  14.4 0.4 %shard_map.62.refs_2_ = f32[2,13,16,128]{3,2,1,0:T(8,128)S(1)} custom-call(f32[4,16,3200]{2,1,0:T(8,128)S(1)} %collective-permute-done.refs_0_.refs_1_, f32[3,4,16]{2,1,0:T(4,128)S(1)} %get-tuple-element.16.refs_1_, f32[4,16]{1,0:T(4,128)S(1)} %get-tuple-element.17.refs_2_, f32[2,13,16,128]{3,2,1,0:T(8,128)S(1)} %shard_map.61.refs_3_.refs_2_), custom_call_target="tpu_custom_call" | custom-call | flops 2000000 | bytes 2000000 | tf_op jit(solution)/shard_map/pallas_call | solution.py:43
  14.9 0.1 collective-permute-done.8.refs_3_
  15.0 0.1 shard_map.65.refs_3_
  15.1 0.1 collective-permute-done.5.refs_0_
  15.3 1.7 %collective-permute-done.6.refs_1_ = f32[2,4,16,128]{3,2,1,0:T(8,128)S(1)} collective-permute-done((f32[2,4,16,128]{3,2,1,0:T(8,128)S(1)}, f32[2,4,16,128]{3,2,1,0:T(8,128)S(1)}, u32[]{:S(2)}, u32[]{:S(2)}) %collective-permute-start.6) | collective-permute-done | bytes 65568 | tf_op jit(solution)/shard_map/ppermute | solution.py:368
  16.9 0.7 %collective-permute-done.7.refs_2_ = f32[2,4,16,128]{3,2,1,0:T(8,128)S(1)} collective-permute-done((f32[2,4,16,128]{3,2,1,0:T(8,128)S(1)}, f32[2,4,16,128]{3,2,1,0:T(8,128)S(1)}, u32[]{:S(2)}, u32[]{:S(2)}) %collective-permute-start.7) | collective-permute-done | bytes 65568 | tf_op jit(solution)/shard_map/ppermute | solution.py:368
  17.7 0.7 %shard_map.66 = f32[4,16,256]{2,1,0:T(8,128)} custom-call(f32[2,4,16,128]{3,2,1,0:T(8,128)S(1)} %collective-permute-done.5.refs_0_, f32[2,4,16,128]{3,2,1,0:T(8,128)S(1)} %collective-permute-done.6.refs_1_, f32[2,4,16,128]{3,2,1,0:T(8,128)S(1)} %collective-permute-done.7.refs_2_, f32[2,4,16,128]{3,2,1,0:T(8,128)S(1)} %shard_map.65.refs_3_), custom_call_target="tpu_custom_call" | custom-call | flops 2000000 | bytes 2000000 | tf_op jit(solution)/shard_map/pallas_call | solution.py:43
  (6 shorter events, 0.0 us)
Async XLA Ops:
  1.3 5.3 %collective-permute-start = (f32[4,16,3200]{2,1,0:T(8,128)S(1)}, f32[4,16,3200]{2,1,0:T(8,128)S(1)}, u32[]{:S(2)}, u32[]{:S(2)}) collective-permute-start(f32[4,16,3200]{2,1,0:T(8,128)S(1)} %get-tuple-element.15.refs_0_.refs_1_), channel_id=1, source_target_pairs={{0,4},{4,0},{8,12},{12,8},{16,20},{20,16},{24,28},{28,24},{1,5},{5... | collective-permute-start | bytes 2457608 | tf_op jit(solution)/shard_map/ppermute | solution.py:328
  1.8 6.6 %collective-permute-start.1 = (f32[1,16,2048]{2,1,0:T(8,128)S(1)}, f32[1,16,2048]{2,1,0:T(8,128)S(1)}, u32[]{:S(2)}, u32[]{:S(2)}) collective-permute-start(f32[1,16,2048]{2,1,0:T(8,128)S(1)} %get-tuple-element.19), channel_id=1, source_target_pairs={{0,1},{1,0},{2,3},{3,2},{4,8},{5,9},{6,10},{7,11},{8,4},{9,5},{10,... | collective-permute-start | bytes 393224 | tf_op jit(solution)/shard_map/ppermute | solution.py:329
  4.5 3.9 %collective-permute-start.2 = (f32[4,2048]{1,0:T(4,128)S(1)}, f32[4,2048]{1,0:T(4,128)S(1)}, u32[]{:S(2)}, u32[]{:S(2)}) collective-permute-start(f32[4,2048]{1,0:T(4,128)S(1)} %get-tuple-element.20), channel_id=1, source_target_pairs={{0,1},{1,0},{2,3},{3,2},{4,5},{5,4},{6,7},{7,6},{8,9},{9,8},{10,11... | collective-permute-start | bytes 98312 | tf_op jit(solution)/shard_map/ppermute | solution.py:330
  4.6 3.8 %collective-permute-start.3 = (f32[4,2048]{1,0:T(4,128)S(1)}, f32[4,2048]{1,0:T(4,128)S(1)}, u32[]{:S(2)}, u32[]{:S(2)}) collective-permute-start(f32[4,2048]{1,0:T(4,128)S(1)} %get-tuple-element.21), channel_id=1, source_target_pairs={{0,4},{1,2},{2,1},{3,7},{4,0},{5,6},{6,5},{7,3},{8,12},{9,10},{10,... | collective-permute-start | bytes 98312 | tf_op jit(solution)/shard_map/ppermute | solution.py:331
  8.4 1.3 %collective-permute-start.4 = (f32[6,24,128]{2,1,0:T(8,128)S(1)}, f32[6,24,128]{2,1,0:T(8,128)S(1)}, u32[]{:S(2)}, u32[]{:S(2)}) collective-permute-start(f32[6,24,128]{2,1,0:T(8,128)S(1)} %shard_map.58), channel_id=1, source_target_pairs={{0,4},{4,0},{8,12},{12,8},{16,20},{20,16},{24,28},{28,24},{1,5},{5... | collective-permute-start | bytes 221192 | tf_op jit(solution)/shard_map/ppermute | solution.py:349
  10.1 5.2 %collective-permute-start.5 = (f32[2,4,16,128]{3,2,1,0:T(8,128)S(1)}, f32[2,4,16,128]{3,2,1,0:T(8,128)S(1)}, u32[]{:S(2)}, u32[]{:S(2)}) collective-permute-start(f32[2,4,16,128]{3,2,1,0:T(8,128)S(1)} %get-tuple-element.22), channel_id=1, source_target_pairs={{0,24},{4,28},{8,16},{12,20},{16,8},{20,12},{24,0},{28,4},{1,25},{... | collective-permute-start | bytes 196616 | tf_op jit(solution)/shard_map/ppermute | solution.py:368
  12.4 4.6 %collective-permute-start.6 = (f32[2,4,16,128]{3,2,1,0:T(8,128)S(1)}, f32[2,4,16,128]{3,2,1,0:T(8,128)S(1)}, u32[]{:S(2)}, u32[]{:S(2)}) collective-permute-start(f32[2,4,16,128]{3,2,1,0:T(8,128)S(1)} %get-tuple-element.23), channel_id=1, source_target_pairs={{0,8},{4,12},{8,0},{12,4},{16,24},{20,28},{24,16},{28,20},{1,9},{5... | collective-permute-start | bytes 196616 | tf_op jit(solution)/shard_map/ppermute | solution.py:368
  13.4 4.3 %collective-permute-start.7 = (f32[2,4,16,128]{3,2,1,0:T(8,128)S(1)}, f32[2,4,16,128]{3,2,1,0:T(8,128)S(1)}, u32[]{:S(2)}, u32[]{:S(2)}) collective-permute-start(f32[2,4,16,128]{3,2,1,0:T(8,128)S(1)} %get-tuple-element.24.refs_4_.refs_3_), channel_id=1, source_target_pairs={{0,16},{4,20},{8,24},{12,28},{16,0},{20,4},{24,8},{28,12},{1,17},{... | collective-permute-start | bytes 196616 | tf_op jit(solution)/shard_map/ppermute | solution.py:368
  13.8 1.2 %collective-permute-start.8 = (f32[2,24,128]{2,1,0:T(8,128)S(1)}, f32[2,24,128]{2,1,0:T(8,128)S(1)}, u32[]{:S(2)}, u32[]{:S(2)}) collective-permute-start(f32[2,24,128]{2,1,0:T(8,128)S(1)} %shard_map.63), channel_id=1, source_target_pairs={{0,4},{4,0},{8,12},{12,8},{16,20},{20,16},{24,28},{28,24},{1,5},{5... | collective-permute-start | bytes 73736 | tf_op jit(solution)/shard_map/ppermute | solution.py:349

commit v8 on v7

--- a/solution.py
+++ b/solution.py
@@ -166,10 +166,29 @@
         out[i, rows + slices :, :] = far_y[:, here]
 
 
-def shade(order, columns, start, outs, brick, beside, weights, layer, near_row, far_row, odd_slab, finish):
+def column_step(brick, columns, c, z, band, v):
+    tiles = columns // LANES
+    lane = lax.broadcasted_iota(jnp.int32, (ROWS, LANES), 1)
+    vl = brick[z, band, tile(jnp.maximum(c - 1, 0))] * jnp.where(c > 0, 1.0, 0.0)
+    vr = brick[z, band, tile(jnp.minimum(c + 1, tiles - 1))] * jnp.where(c < tiles - 1, 1.0, 0.0)
+    return pltpu.roll(jnp.where(lane == 0, vr, v), LANES - 1, 1) - pltpu.roll(
+        jnp.where(lane == LANES - 1, vl, v), 1, 1
+    )
+
+
+def steps_kernel(order, columns, start, brick, out):
     slices, rows = brick.shape[:2]
-    tiles, bands = columns // LANES, rows // ROWS
-    lane = lax.broadcasted_iota(jnp.int32, (ROWS, LANES), 1)
+    for i in range(out.shape[0]):
+        c = order(0, start + i)
+        for z in range(slices):
+            for b in range(rows // ROWS):
+                band = slice(b * ROWS, (b + 1) * ROWS)
+                out[i, z, band, :] = column_step(brick, columns, c, z, band, brick[z, band, tile(c)])
+
+
+def shade(order, columns, start, outs, brick, beside, weights, layer, near_row, far_row, across, odd_slab, finish):
+    slices, rows = brick.shape[:2]
+    bands = rows // ROWS
     row = lax.broadcasted_iota(jnp.int32, (ROWS, LANES), 0)
     chip, chips = lax.axis_index("depth") // 2, lax.axis_size("depth") // 2
     at_y = lax.axis_index("strip")
@@ -182,9 +201,7 @@
     work = [(out, h) for out in outs for h in range(out.shape[0])]
     for i, (out, h) in enumerate(work, start):
         c = order(0, i)
-        here, left, right = tile(c), tile(jnp.maximum(c - 1, 0)), tile(jnp.minimum(c + 1, tiles - 1))
-        has_left = jnp.where(c > 0, 1.0, 0.0)
-        has_right = jnp.where(c < tiles - 1, 1.0, 0.0)
+        here = tile(c)
         d = [[brick[z, b * ROWS : (b + 1) * ROWS, here] for b in range(bands)] for z in range(slices)]
         for b in range(bands):
             band = slice(b * ROWS, (b + 1) * ROWS)
@@ -213,11 +230,7 @@
                 dy = pltpu.roll(jnp.where(row == 0, bottom, v), ROWS - 1, 0) - pltpu.roll(
                     jnp.where(row == ROWS - 1, top, v), 1, 0
                 )
-                vl = brick[z, band, left] * has_left
-                vr = brick[z, band, right] * has_right
-                dx = pltpu.roll(jnp.where(lane == 0, vr, v), LANES - 1, 1) - pltpu.roll(
-                    jnp.where(lane == LANES - 1, vl, v), 1, 1
-                )
+                dx = across(i, c, z, band, v)
                 facing = jnp.abs(dx + 2.0 * (dy + dz))
                 lighting = ambient + (diffuse / 3.0) * facing * lax.rsqrt(
                     4.0 + (dx * dx + dy * dy + dz * dz)
@@ -242,12 +255,13 @@
         lambda i, c, band: far_z[0, band, tile(c)],
         lambda i, c, z: near_y[z : z + 1, tile(c)],
         lambda i, c, z: far_y[z : z + 1, tile(c)],
+        lambda i, c, z, band, v: column_step(brick, columns, c, z, band, v),
         lax.axis_index("depth") % 2 == 1,
         lambda i, band, image: image,
     )
 
 
-def chip_kernel(order, columns, start, brick, beside, weights, handed, mine, *outs):
+def chip_kernel(order, columns, start, brick, beside, weights, steps, handed, mine, *outs):
     slices, rows = brick.shape[:2]
     odd = lax.axis_index("depth") % 2 == 1
     shade(
@@ -258,33 +272,39 @@
         brick,
         beside,
         weights,
-        lambda i, c, band: handed[i - start, band, :],
-        lambda i, c, z: handed[i - start, rows + z : rows + z + 1, :],
-        lambda i, c, z: handed[i - start, rows + slices + z : rows + slices + z + 1, :],
+        lambda i, c, band: handed[i, band, :],
+        lambda i, c, z: handed[i, rows + z : rows + z + 1, :],
+        lambda i, c, z: handed[i, rows + slices + z : rows + slices + z + 1, :],
+        lambda i, c, z, band, v: steps[i - start, z, band, :],
         lax.axis_index("depth") % 2 == 0,
         lambda i, band, image: over(odd, [mine[i, ch, band, :] for ch in range(4)], image),
     )
 
 
-def chip_order(chips):
-    return sorted(range(chips), key=lambda k: (-k.bit_count(), k))
-
-
-def finish_kernel(*refs):
-    given, out = dict(zip(chip_order(len(refs) - 1), refs)), refs[-1]
-    pieces = [given[k] for k in range(len(given))]
-    chip = lax.axis_index("depth") // 2
-    for h in range(pieces[0].shape[0]):
-        values = [[piece[h, ch] for ch in range(4)] for piece in pieces]
-        bit = 0
-        while len(values) > 1:
-            swap = (chip >> bit) % 2 == 1
-            values = [over(swap, values[k], values[k + 1]) for k in range(0, len(values), 2)]
-            bit += 1
+def pass_kernel(received, out):
+    per = out.shape[0]
+    other = 1 - lax.axis_index("depth") % 2
+    for h in range(per):
+        out[h] = received[other * per + h]
+
+
+def finish_kernel(beside, passed, across, mine, out):
+    index = lax.axis_index("depth")
+    odd, chip = index % 2 == 1, index // 2
+    per = mine.shape[0]
+    for h in range(per):
+        direct = [beside[index % 2 * per + h, ch] for ch in range(4)]
+        other = [passed[h, ch] for ch in range(4)]
+        along_x = [jnp.where(odd, o, d) for o, d in zip(other, direct)]
+        along_y = [jnp.where(odd, d, o) for o, d in zip(other, direct)]
+        by_x, by_y = chip % 2 == 1, chip // 2 == 1
+        here_row = over(by_x, [mine[h, ch] for ch in range(4)], along_x)
+        there_row = over(by_x, along_y, [across[h, ch] for ch in range(4)])
+        image = over(by_y, here_row, there_row)
         here = slice(h * LANES, (h + 1) * LANES)
         for ch in range(3):
-            out[ch, :, here] = values[0][ch]
-        out[3, :, here] = 1.0 - values[0][3]
+            out[ch, :, here] = image[ch]
+        out[3, :, here] = 1.0 - image[3]
 
 
 def composite_over(nearer, farther):
@@ -299,17 +319,18 @@
     groups, strips = lax.axis_size("depth"), lax.axis_size("strip")
     width = columns // groups
     chips, half = groups // 2, tiles // 2
-    paired = chips & (chips - 1) == 0 and width % LANES == 0
-    per = width // LANES if paired else half
-    ks = chip_order(chips) if paired else [0]
+    squared = chips == 4 and width % LANES == 0
+    per = width // LANES if squared else half
 
     def order(other, i):
         index = lax.axis_index("depth")
         parity = (index + other) % 2
-        if not paired:
+        if not squared:
             return parity * half + i
-        k = sum(jnp.where(i // per == n, ks[n], 0) for n in range(chips))
-        return ((index // 2 ^ k) * 2 + parity) * per + i % per
+        n = i // per
+        away = jnp.where(n < 2, 1 + parity, jnp.where(n == 2, 3, 0))
+        core = jnp.where(n < 2, n, parity)
+        return ((index // 2 ^ away) * 2 + core) * per + i % per
 
     given = (density, materials, occupancy_flags[0], tf_color.transpose(1, 0, 2), tf_opacity)
     whole = array(slices, rows, columns + half * LANES + LANES)
@@ -330,7 +351,7 @@
     near_y = lax.ppermute(inner_y, "strip", inner_pairs(strips))
     far_y = lax.ppermute(outer_y, both, outer_pairs(groups, strips, "strip"))
 
-    far = (chips - 1) * per if paired else half
+    far = 3 * per if squared else half
 
     def weigh(first, count, after=()):
         lookup = functools.partial(lookup_kernel, order, columns, first)
@@ -348,9 +369,16 @@
         )
         return lax.ppermute(handing, "depth", inner_pairs(groups))
 
-    handed = hand(0, far, (weights_beside,))
-
-    def images(first, count, blocks, handed, weights, weights_beside):
+    handed = hand(0, half, (weights_beside,))
+
+    def images(first, counts, handed, weights, weights_beside):
+        count = sum(counts)
+        steps = call(
+            functools.partial(steps_kernel, order, columns, first),
+            array(count, slices, rows, LANES),
+            (beside,),
+            (weights_beside,),
+        )
         mine = call(
             functools.partial(own_kernel, order, columns, first),
             array(count, 4, rows, LANES),
@@ -358,21 +386,21 @@
         )
         return call(
             functools.partial(chip_kernel, order, columns, first),
-            [array(count // blocks, 4, rows, LANES)] * blocks,
-            (beside, brick, weights_beside, handed, mine),
+            [array(tiles_here, 4, rows, LANES) for tiles_here in counts],
+            (beside, brick, weights_beside, steps, handed, mine),
         )
 
-    if paired:
-        sent = images(0, far, chips - 1, handed, weights, weights_beside)
-        moved = [
-            lax.ppermute(image, "depth", [(i, i ^ (2 * k)) for i in range(groups)])
-            for image, k in zip(sent, ks)
-        ]
-        late = sent[-1:]
-        (kept,) = images(far, per, 1, hand(far, per, late), *weigh(far, per, late))
-        return call(finish_kernel, array(4, rows, width), (*moved, kept))
-
-    (image,) = images(0, half, 1, handed, weights, weights_beside)
+    if squared:
+        to_side, to_across = images(0, (2 * per, per), handed, weights, weights_beside)
+        from_side = lax.ppermute(to_side, "depth", [(i, i ^ 2 << i % 2) for i in range(groups)])
+        from_across = lax.ppermute(to_across, "depth", [(i, i ^ 6) for i in range(groups)])
+        late = (to_side,)
+        (kept,) = images(far, (per,), handed, *weigh(far, per, late))
+        (passing,) = call(pass_kernel, [array(per, 4, rows, LANES)], (from_side,), (kept,))
+        passed = lax.ppermute(passing, "depth", inner_pairs(groups))
+        return call(finish_kernel, array(4, rows, width), (from_side, passed, from_across, kept))
+
+    (image,) = images(0, (half,), handed, weights, weights_beside)
     clear = jnp.zeros_like(image).at[:, 3].set(1.0)
     odd = lax.axis_index("depth") % 2 == 1
     partial_value = jnp.concatenate(

time: 18.5 us -> 18.5 us (level)
  starting transfers between devices: 8.31 us -> 7.9 us
  Pallas kernels: 5.34 us -> 5.59 us
  waiting for transfers between devices: 4.6 us -> 4.83 us
    ppermute x3, waiting for transfers between devices: 2.51 us -> 3.05 us  [the longest x1 1.75 us: on_device(): lax.ppermute(to_across, 'depth', [(i, i ^ 6) for i in range(groups)])]
    ppermute x3, starting transfers between devices: 3.74 us -> 3.33 us  [the longest x1 2.27 us: on_device(): lax.ppermute(to_side, 'depth', [(i, i ^ 2 << i % 2) for i in range(groups)])]
    ppermute x2 -> x1, waiting for transfers between devices: 1.11 us -> 0.8 us  [hand(): return lax.ppermute(handing, 'depth', inner_pairs(groups))]
    pallas_call x11 -> x13, Pallas kernels: 4.03 us -> 4.27 us  [call(): pl.pallas_call(body, out_shape=out_shape, in_specs=[VMEM] * count + [pl.B...]
  transfers between devices with their start and end apart: 9 -> 8, of which waited for: 6 -> 4; matrix products, arithmetic and copies ran while one was open for 0% -> 0% of each run, Pallas kernels for 17% -> 18%
where the time goes in v8:
time: 18.5 us; the launch traced here: 18.4 us
  starting transfers between devices  7.9 us (43%)
  Pallas kernels  5.59 us (30%)
  waiting for transfers between devices  4.83 us (26%)
    pallas_call x13, Pallas kernels, call(): pl.pallas_call(body, out_shape=out_shape, in_specs=[VMEM] * count + [pl.B...  4.27 us
    ppermute x1, starting transfers between devices, on_device(): far_z = lax.ppermute(layer, both, outer_pairs(groups, strips, 'depth'))  2.65 us
    ppermute x1, starting transfers between devices, on_device(): lax.ppermute(to_side, 'depth', [(i, i ^ 2 << i % 2) for i in range(groups)])  2.27 us
    ppermute x1, waiting for transfers between devices, on_device(): lax.ppermute(to_across, 'depth', [(i, i ^ 6) for i in range(groups)])  1.75 us
    pallas_call x1, Pallas kernels, on_device(): pl.pallas_call(functools.partial(load_kernel, order), out_shape=[whole] +...  1.31 us
    ppermute x1, waiting for transfers between devices, on_device(): lax.ppermute(to_side, 'depth', [(i, i ^ 2 << i % 2) for i in range(groups)])  1.3 us
    ppermute x1, starting transfers between devices, on_device(): far_y = lax.ppermute(outer_y, both, outer_pairs(groups, strips, 'strip'))  1.25 us
    ppermute x1, starting transfers between devices, on_device(): lax.ppermute(to_across, 'depth', [(i, i ^ 6) for i in range(groups)])  1.07 us
  transfers between devices with their start and end apart: 8, of which 4 were waited for; matrix products, arithmetic and copies ran while one was open for 0% of the time, Pallas kernels for 18%

profile of v8, /device:TPU:0, one launch (start us, length us, event | category | flops | bytes accessed | tf_op | source)
XLA Modules:
  0.0 18.4 jit_solution(3798479949488728224)
XLA Ops:
  0.0 1.3 %shard_map.55 = (f32[4,16,3200]{2,1,0:T(8,128)S(1)}, s32[4,16,2048]{2,1,0:T(8,128)S(1)}, f32[3,4,16]{2,1,0:T(4,128)S(1)}, f32[4,16]{1,0:T(4,128)S(1)}, f32[1,16,...) custom-call(f32[4,16,2048]{2,1,0:T(8,128)} %refs_0_.1, s32[4,16,2048]{2,1,0:T(8,128)} %refs_1_.1, ...), custom_call_target="tpu_custom_call" | custom-call | tf_op jit(solution)/shard_map/pallas_call | solution.py:338
  1.3 0.5 %collective-permute-start = (f32[4,16,3200]{2,1,0:T(8,128)S(1)}, f32[4,16,3200]{2,1,0:T(8,128)S(1)}, u32[]{:S(2)}, u32[]{:S(2)}) collective-permute-start(f32[4,16,3200]{2,1,0:T(8,128)S(1)} %get-tuple-element.14.refs_0_.refs_1_), channel_id=1, source_target_pairs={{0,4},{4,0},{8,12},{12,8},{16,20},{20,16},{24,28},{28,24},{1,5},{5... | collective-permute-start | bytes 2457608 | tf_op jit(solution)/shard_map/ppermute | solution.py:349
  1.8 2.6 %collective-permute-start.1 = (f32[1,16,2048]{2,1,0:T(8,128)S(1)}, f32[1,16,2048]{2,1,0:T(8,128)S(1)}, u32[]{:S(2)}, u32[]{:S(2)}) collective-permute-start(f32[1,16,2048]{2,1,0:T(8,128)S(1)} %get-tuple-element.18), channel_id=1, source_target_pairs={{0,1},{1,0},{2,3},{3,2},{4,8},{5,9},{6,10},{7,11},{8,4},{9,5},{10,... | collective-permute-start | bytes 393224 | tf_op jit(solution)/shard_map/ppermute | solution.py:350
  4.5 0.1 collective-permute-start.2
  4.6 1.2 %collective-permute-start.3 = (f32[4,2048]{1,0:T(4,128)S(1)}, f32[4,2048]{1,0:T(4,128)S(1)}, u32[]{:S(2)}, u32[]{:S(2)}) collective-permute-start(f32[4,2048]{1,0:T(4,128)S(1)} %get-tuple-element.20), channel_id=1, source_target_pairs={{0,4},{1,2},{2,1},{3,7},{4,0},{5,6},{6,5},{7,3},{8,12},{9,10},{10,... | collective-permute-start | bytes 98312 | tf_op jit(solution)/shard_map/ppermute | solution.py:352
  5.8 0.8 %shard_map.56.refs_3_.refs_2_ = f32[6,13,16,128]{3,2,1,0:T(8,128)S(1)} custom-call(f32[4,16,3200]{2,1,0:T(8,128)S(1)} %get-tuple-element.14.refs_0_.refs_1_, f32[3,4,16]{2,1,0:T(4,128)S(1)} %get-tuple-element.15.refs_1_, f32[4,16]{1,0:T(4,128)S(1)} %get-tuple-element.16.refs_2_, s32[4,16,2048]{2,1,0:T(8,128)S(1)} %get-tuple-element.17.refs_3_), custom_call_target="tpu_custom_call" | custom-call | flops 2000000 | bytes 2000000 | tf_op jit(solution)/shard_map/pallas_call | solution.py:43
  6.6 0.8 %shard_map.57.refs_1_.refs_3_.refs_2_ = f32[6,13,16,128]{3,2,1,0:T(8,128)S(1)} custom-call(f32[4,16,3200]{2,1,0:T(8,128)S(1)} %collective-permute-done.refs_0_.refs_1_, f32[3,4,16]{2,1,0:T(4,128)S(1)} %get-tuple-element.15.refs_1_, f32[4,16]{1,0:T(4,128)S(1)} %get-tuple-element.16.refs_2_, f32[6,13,16,128]{3,2,1,0:T(8,128)S(1)} %shard_map.56.refs_3_.refs_2_), custom_call_target="tpu_custom_call" | custom-call | flops 2000000 | bytes 2000000 | tf_op jit(solution)/shard_map/pallas_call | solution.py:43
  7.4 1.0 %collective-permute-done.2.refs_1_.refs_4_ = f32[4,2048]{1,0:T(4,128)S(1)} collective-permute-done((f32[4,2048]{1,0:T(4,128)S(1)}, f32[4,2048]{1,0:T(4,128)S(1)}, u32[]{:S(2)}, u32[]{:S(2)}) %collective-permute-start.2) | collective-permute-done | bytes 32800 | tf_op jit(solution)/shard_map/ppermute | solution.py:351
  8.4 0.1 collective-permute-start.4
  8.5 0.3 %shard_map.60.refs_5_ = f32[6,4,16,128]{3,2,1,0:T(8,128)S(1)} custom-call(f32[4,16,3200]{2,1,0:T(8,128)S(1)} %get-tuple-element.14.refs_0_.refs_1_, f32[4,16,3200]{2,1,0:T(8,128)S(1)} %collective-permute-done.refs_0_.refs_1_, f32[6,13,16,128]{3,2,1,0:T(8,128)S(1)} %shard_map.56.refs_3_.refs_2_, f32[1,16,2048]{2,1,0:T(8,128)S(1)} %collective-permute-done.1.refs_0_.refs_3_, ...), custom_call_target="tpu_custom_call" | custom-call | flops 2000000 | bytes 2000000 | tf_op jit(solution)/shard_map/pallas_call | solution.py:43
  8.8 0.2 %shard_map.58.refs_3_ = f32[6,4,16,128]{3,2,1,0:T(8,128)S(1)} custom-call(f32[4,16,3200]{2,1,0:T(8,128)S(1)} %collective-permute-done.refs_0_.refs_1_, f32[6,13,16,128]{3,2,1,0:T(8,128)S(1)} %shard_map.57.refs_1_.refs_3_.refs_2_), custom_call_target="tpu_custom_call" | custom-call | flops 2000000 | bytes 2000000 | tf_op jit(solution)/shard_map/pallas_call | solution.py:43
  9.0 0.8 %collective-permute-done.4.refs_4_ = f32[8,24,128]{2,1,0:T(8,128)S(1)} collective-permute-done((f32[8,24,128]{2,1,0:T(8,128)S(1)}, f32[8,24,128]{2,1,0:T(8,128)S(1)}, u32[]{:S(2)}, u32[]{:S(2)}) %collective-permute-start.4) | collective-permute-done | bytes 98336 | tf_op jit(solution)/shard_map/ppermute | solution.py:370
  9.8 0.2 %shard_map.61 = (f32[4,4,16,128]{3,2,1,0:T(8,128)S(1)}, f32[2,4,16,128]{3,2,1,0:T(8,128)S(1)}) custom-call(f32[4,16,3200]{2,1,0:T(8,128)S(1)} %collective-permute-done.refs_0_.refs_1_, f32[4,16,3200]{2,1,0:T(8,128)S(1)} %get-tuple-element.14.refs_0_.refs_1_, f32[6,13,16,128]{3,2,1,0:T(8,128)S(1)} %shard_map.57.refs_1_.refs_3_.refs_2_, ...), custom_call_target="tpu_custom_call" | custom-call | flops 2000000 | bytes 2000000 | tf_op jit(solution)/shard_map/pallas_call | solution.py:43
  10.0 2.3 %collective-permute-start.5 = (f32[4,4,16,128]{3,2,1,0:T(8,128)S(1)}, f32[4,4,16,128]{3,2,1,0:T(8,128)S(1)}, u32[]{:S(2)}, u32[]{:S(2)}) collective-permute-start(f32[4,4,16,128]{3,2,1,0:T(8,128)S(1)} %get-tuple-element.21.refs_4_), channel_id=1, source_target_pairs={{0,8},{4,20},{8,0},{12,28},{16,24},{20,4},{24,16},{28,12},{1,9},{5... | collective-permute-start | bytes 393224 | tf_op jit(solution)/shard_map/ppermute | solution.py:395
  12.3 1.1 %collective-permute-start.7 = (f32[2,4,16,128]{3,2,1,0:T(8,128)S(1)}, f32[2,4,16,128]{3,2,1,0:T(8,128)S(1)}, u32[]{:S(2)}, u32[]{:S(2)}) collective-permute-start(f32[2,4,16,128]{3,2,1,0:T(8,128)S(1)} %get-tuple-element.22), channel_id=1, source_target_pairs={{0,24},{4,28},{8,16},{12,20},{16,8},{20,12},{24,0},{28,4},{1,25},{... | collective-permute-start | bytes 196616 | tf_op jit(solution)/shard_map/ppermute | solution.py:396
  13.4 0.4 %shard_map.62.refs_3_.refs_2_ = f32[2,13,16,128]{3,2,1,0:T(8,128)S(1)} custom-call(f32[4,16,3200]{2,1,0:T(8,128)S(1)} %get-tuple-element.14.refs_0_.refs_1_, f32[3,4,16]{2,1,0:T(4,128)S(1)} %get-tuple-element.15.refs_1_, f32[4,16]{1,0:T(4,128)S(1)} %get-tuple-element.16.refs_2_, s32[4,16,2048]{2,1,0:T(8,128)S(1)} %get-tuple-element.17.refs_3_, ...), custom_call_target="tpu_custom_call" | custom-call | flops 2000000 | bytes 2000000 | tf_op jit(solution)/shard_map/pallas_call | solution.py:43
  13.8 0.1 shard_map.65.refs_5_
  14.0 0.4 %shard_map.63.refs_1_.refs_2_ = f32[2,13,16,128]{3,2,1,0:T(8,128)S(1)} custom-call(f32[4,16,3200]{2,1,0:T(8,128)S(1)} %collective-permute-done.refs_0_.refs_1_, f32[3,4,16]{2,1,0:T(4,128)S(1)} %get-tuple-element.15.refs_1_, f32[4,16]{1,0:T(4,128)S(1)} %get-tuple-element.16.refs_2_, f32[2,13,16,128]{3,2,1,0:T(8,128)S(1)} %shard_map.62.refs_3_.refs_2_), custom_call_target="tpu_custom_call" | custom-call | flops 2000000 | bytes 2000000 | tf_op jit(solution)/shard_map/pallas_call | solution.py:43
  14.4 0.1 shard_map.64.refs_3_
  14.6 0.1 shard_map.66.refs_1_.refs_3_
  14.7 1.3 %collective-permute-done.5.refs_0_ = f32[4,4,16,128]{3,2,1,0:T(8,128)S(1)} collective-permute-done((f32[4,4,16,128]{3,2,1,0:T(8,128)S(1)}, f32[4,4,16,128]{3,2,1,0:T(8,128)S(1)}, u32[]{:S(2)}, u32[]{:S(2)}) %collective-permute-start.5) | collective-permute-done | bytes 131104 | tf_op jit(solution)/shard_map/ppermute | solution.py:395
  16.0 0.0 collective-permute-start.6
  16.0 1.7 %collective-permute-done.7.refs_2_ = f32[2,4,16,128]{3,2,1,0:T(8,128)S(1)} collective-permute-done((f32[2,4,16,128]{3,2,1,0:T(8,128)S(1)}, f32[2,4,16,128]{3,2,1,0:T(8,128)S(1)}, u32[]{:S(2)}, u32[]{:S(2)}) %collective-permute-start.7) | collective-permute-done | bytes 65568 | tf_op jit(solution)/shard_map/ppermute | solution.py:396
  17.7 0.7 %shard_map.68 = f32[4,16,256]{2,1,0:T(8,128)} custom-call(f32[4,4,16,128]{3,2,1,0:T(8,128)S(1)} %collective-permute-done.5.refs_0_, f32[2,4,16,128]{3,2,1,0:T(8,128)S(1)} %collective-permute-done.6.refs_1_, f32[2,4,16,128]{3,2,1,0:T(8,128)S(1)} %collective-permute-done.7.refs_2_, f32[2,4,16,128]{3,2,1,0:T(8,128)S(1)} %shard_map.66.refs_1_.refs_3_), custom_call_target="tpu_custom_call" | custom-call | flops 2000000 | bytes 2000000 | tf_op jit(solution)/shard_map/pallas_call | solution.py:43
  (6 shorter events, 0.0 us)
Async XLA Ops:
  1.3 5.3 %collective-permute-start = (f32[4,16,3200]{2,1,0:T(8,128)S(1)}, f32[4,16,3200]{2,1,0:T(8,128)S(1)}, u32[]{:S(2)}, u32[]{:S(2)}) collective-permute-start(f32[4,16,3200]{2,1,0:T(8,128)S(1)} %get-tuple-element.14.refs_0_.refs_1_), channel_id=1, source_target_pairs={{0,4},{4,0},{8,12},{12,8},{16,20},{20,16},{24,28},{28,24},{1,5},{5... | collective-permute-start | bytes 2457608 | tf_op jit(solution)/shard_map/ppermute | solution.py:349
  1.8 6.6 %collective-permute-start.1 = (f32[1,16,2048]{2,1,0:T(8,128)S(1)}, f32[1,16,2048]{2,1,0:T(8,128)S(1)}, u32[]{:S(2)}, u32[]{:S(2)}) collective-permute-start(f32[1,16,2048]{2,1,0:T(8,128)S(1)} %get-tuple-element.18), channel_id=1, source_target_pairs={{0,1},{1,0},{2,3},{3,2},{4,8},{5,9},{6,10},{7,11},{8,4},{9,5},{10,... | collective-permute-start | bytes 393224 | tf_op jit(solution)/shard_map/ppermute | solution.py:350
  4.5 3.9 %collective-permute-start.2 = (f32[4,2048]{1,0:T(4,128)S(1)}, f32[4,2048]{1,0:T(4,128)S(1)}, u32[]{:S(2)}, u32[]{:S(2)}) collective-permute-start(f32[4,2048]{1,0:T(4,128)S(1)} %get-tuple-element.19), channel_id=1, source_target_pairs={{0,1},{1,0},{2,3},{3,2},{4,5},{5,4},{6,7},{7,6},{8,9},{9,8},{10,11... | collective-permute-start | bytes 98312 | tf_op jit(solution)/shard_map/ppermute | solution.py:351
  4.6 3.8 %collective-permute-start.3 = (f32[4,2048]{1,0:T(4,128)S(1)}, f32[4,2048]{1,0:T(4,128)S(1)}, u32[]{:S(2)}, u32[]{:S(2)}) collective-permute-start(f32[4,2048]{1,0:T(4,128)S(1)} %get-tuple-element.20), channel_id=1, source_target_pairs={{0,4},{1,2},{2,1},{3,7},{4,0},{5,6},{6,5},{7,3},{8,12},{9,10},{10,... | collective-permute-start | bytes 98312 | tf_op jit(solution)/shard_map/ppermute | solution.py:352
  8.4 1.4 %collective-permute-start.4 = (f32[8,24,128]{2,1,0:T(8,128)S(1)}, f32[8,24,128]{2,1,0:T(8,128)S(1)}, u32[]{:S(2)}, u32[]{:S(2)}) collective-permute-start(f32[8,24,128]{2,1,0:T(8,128)S(1)} %shard_map.59), channel_id=1, source_target_pairs={{0,4},{4,0},{8,12},{12,8},{16,20},{20,16},{24,28},{28,24},{1,5},{5... | collective-permute-start | bytes 294920 | tf_op jit(solution)/shard_map/ppermute | solution.py:370
  10.0 5.9 %collective-permute-start.5 = (f32[4,4,16,128]{3,2,1,0:T(8,128)S(1)}, f32[4,4,16,128]{3,2,1,0:T(8,128)S(1)}, u32[]{:S(2)}, u32[]{:S(2)}) collective-permute-start(f32[4,4,16,128]{3,2,1,0:T(8,128)S(1)} %get-tuple-element.21.refs_4_), channel_id=1, source_target_pairs={{0,8},{4,20},{8,0},{12,28},{16,24},{20,4},{24,16},{28,12},{1,9},{5... | collective-permute-start | bytes 393224 | tf_op jit(solution)/shard_map/ppermute | solution.py:395
  12.3 5.4 %collective-permute-start.7 = (f32[2,4,16,128]{3,2,1,0:T(8,128)S(1)}, f32[2,4,16,128]{3,2,1,0:T(8,128)S(1)}, u32[]{:S(2)}, u32[]{:S(2)}) collective-permute-start(f32[2,4,16,128]{3,2,1,0:T(8,128)S(1)} %get-tuple-element.22), channel_id=1, source_target_pairs={{0,24},{4,28},{8,16},{12,20},{16,8},{20,12},{24,0},{28,4},{1,25},{... | collective-permute-start | bytes 196616 | tf_op jit(solution)/shard_map/ppermute | solution.py:396
  16.0 1.8 %collective-permute-start.6 = (f32[2,4,16,128]{3,2,1,0:T(8,128)S(1)}, f32[2,4,16,128]{3,2,1,0:T(8,128)S(1)}, u32[]{:S(2)}, u32[]{:S(2)}) collective-permute-start(f32[2,4,16,128]{3,2,1,0:T(8,128)S(1)} %shard_map.67), channel_id=1, source_target_pairs={{0,4},{4,0},{8,12},{12,8},{16,20},{20,16},{24,28},{28,24},{1,5},{5... | collective-permute-start | bytes 196616 | tf_op jit(solution)/shard_map/ppermute | solution.py:400

commit v9 on v7

--- a/solution.py
+++ b/solution.py
@@ -166,10 +166,29 @@
         out[i, rows + slices :, :] = far_y[:, here]
 
 
-def shade(order, columns, start, outs, brick, beside, weights, layer, near_row, far_row, odd_slab, finish):
+def column_step(brick, columns, c, z, band, v):
+    tiles = columns // LANES
+    lane = lax.broadcasted_iota(jnp.int32, (ROWS, LANES), 1)
+    vl = brick[z, band, tile(jnp.maximum(c - 1, 0))] * jnp.where(c > 0, 1.0, 0.0)
+    vr = brick[z, band, tile(jnp.minimum(c + 1, tiles - 1))] * jnp.where(c < tiles - 1, 1.0, 0.0)
+    return pltpu.roll(jnp.where(lane == 0, vr, v), LANES - 1, 1) - pltpu.roll(
+        jnp.where(lane == LANES - 1, vl, v), 1, 1
+    )
+
+
+def steps_kernel(order, columns, start, brick, out):
     slices, rows = brick.shape[:2]
-    tiles, bands = columns // LANES, rows // ROWS
-    lane = lax.broadcasted_iota(jnp.int32, (ROWS, LANES), 1)
+    for i in range(out.shape[0]):
+        c = order(0, start + i)
+        for z in range(slices):
+            for b in range(rows // ROWS):
+                band = slice(b * ROWS, (b + 1) * ROWS)
+                out[i, z, band, :] = column_step(brick, columns, c, z, band, brick[z, band, tile(c)])
+
+
+def shade(order, columns, start, outs, brick, beside, weights, layer, near_row, far_row, across, odd_slab, finish):
+    slices, rows = brick.shape[:2]
+    bands = rows // ROWS
     row = lax.broadcasted_iota(jnp.int32, (ROWS, LANES), 0)
     chip, chips = lax.axis_index("depth") // 2, lax.axis_size("depth") // 2
     at_y = lax.axis_index("strip")
@@ -182,9 +201,7 @@
     work = [(out, h) for out in outs for h in range(out.shape[0])]
     for i, (out, h) in enumerate(work, start):
         c = order(0, i)
-        here, left, right = tile(c), tile(jnp.maximum(c - 1, 0)), tile(jnp.minimum(c + 1, tiles - 1))
-        has_left = jnp.where(c > 0, 1.0, 0.0)
-        has_right = jnp.where(c < tiles - 1, 1.0, 0.0)
+        here = tile(c)
         d = [[brick[z, b * ROWS : (b + 1) * ROWS, here] for b in range(bands)] for z in range(slices)]
         for b in range(bands):
             band = slice(b * ROWS, (b + 1) * ROWS)
@@ -213,11 +230,7 @@
                 dy = pltpu.roll(jnp.where(row == 0, bottom, v), ROWS - 1, 0) - pltpu.roll(
                     jnp.where(row == ROWS - 1, top, v), 1, 0
                 )
-                vl = brick[z, band, left] * has_left
-                vr = brick[z, band, right] * has_right
-                dx = pltpu.roll(jnp.where(lane == 0, vr, v), LANES - 1, 1) - pltpu.roll(
-                    jnp.where(lane == LANES - 1, vl, v), 1, 1
-                )
+                dx = across(i, c, z, band, v)
                 facing = jnp.abs(dx + 2.0 * (dy + dz))
                 lighting = ambient + (diffuse / 3.0) * facing * lax.rsqrt(
                     4.0 + (dx * dx + dy * dy + dz * dz)
@@ -242,12 +255,13 @@
         lambda i, c, band: far_z[0, band, tile(c)],
         lambda i, c, z: near_y[z : z + 1, tile(c)],
         lambda i, c, z: far_y[z : z + 1, tile(c)],
+        lambda i, c, z, band, v: column_step(brick, columns, c, z, band, v),
         lax.axis_index("depth") % 2 == 1,
         lambda i, band, image: image,
     )
 
 
-def chip_kernel(order, columns, start, brick, beside, weights, handed, mine, *outs):
+def chip_kernel(order, columns, start, brick, beside, weights, steps, handed, mine, *outs):
     slices, rows = brick.shape[:2]
     odd = lax.axis_index("depth") % 2 == 1
     shade(
@@ -261,6 +275,7 @@
         lambda i, c, band: handed[i - start, band, :],
         lambda i, c, z: handed[i - start, rows + z : rows + z + 1, :],
         lambda i, c, z: handed[i - start, rows + slices + z : rows + slices + z + 1, :],
+        lambda i, c, z, band, v: steps[i - start, z, band, :],
         lax.axis_index("depth") % 2 == 0,
         lambda i, band, image: over(odd, [mine[i, ch, band, :] for ch in range(4)], image),
     )
@@ -351,6 +366,12 @@
     handed = hand(0, far, (weights_beside,))
 
     def images(first, count, blocks, handed, weights, weights_beside):
+        steps = call(
+            functools.partial(steps_kernel, order, columns, first),
+            array(count, slices, rows, LANES),
+            (beside,),
+            (weights_beside,),
+        )
         mine = call(
             functools.partial(own_kernel, order, columns, first),
             array(count, 4, rows, LANES),
@@ -359,7 +380,7 @@
         return call(
             functools.partial(chip_kernel, order, columns, first),
             [array(count // blocks, 4, rows, LANES)] * blocks,
-            (beside, brick, weights_beside, handed, mine),
+            (beside, brick, weights_beside, steps, handed, mine),
         )
 
     if paired:

time: 18.5 us -> 18.4 us (level)
  waiting for transfers between devices: 4.6 us -> 4.29 us
  Pallas kernels: 5.34 us -> 5.59 us
    ppermute x2, waiting for transfers between devices: 1.11 us -> 0.77 us  [hand(): return lax.ppermute(handing, 'depth', inner_pairs(groups))]
    pallas_call x11 -> x13, Pallas kernels: 4.03 us -> 4.28 us  [call(): pl.pallas_call(body, out_shape=out_shape, in_specs=[VMEM] * count + [pl.B...]
  transfers between devices with their start and end apart: 9 -> 9, of which waited for: 6 -> 5; matrix products, arithmetic and copies ran while one was open for 0% -> 0% of each run, Pallas kernels for 17% -> 18%
where the time goes in v9:
time: 18.4 us; the launch traced here: 18.3 us
  starting transfers between devices  8.31 us (45%)
  Pallas kernels  5.59 us (30%)
  waiting for transfers between devices  4.29 us (23%)
    pallas_call x13, Pallas kernels, call(): pl.pallas_call(body, out_shape=out_shape, in_specs=[VMEM] * count + [pl.B...  4.28 us
    ppermute x3, starting transfers between devices, on_device(): lax.ppermute(image, 'depth', [(i, i ^ 2 * k) for i in range(groups)])  3.75 us
    ppermute x1, starting transfers between devices, on_device(): far_z = lax.ppermute(layer, both, outer_pairs(groups, strips, 'depth'))  2.65 us
    ppermute x3, waiting for transfers between devices, on_device(): lax.ppermute(image, 'depth', [(i, i ^ 2 * k) for i in range(groups)])  2.54 us
    pallas_call x1, Pallas kernels, on_device(): pl.pallas_call(functools.partial(load_kernel, order), out_shape=[whole] +...  1.31 us
    ppermute x1, starting transfers between devices, on_device(): far_y = lax.ppermute(outer_y, both, outer_pairs(groups, strips, 'strip'))  1.25 us
    ppermute x1, waiting for transfers between devices, on_device(): near_y = lax.ppermute(inner_y, 'strip', inner_pairs(strips))  0.97 us
    ppermute x2, waiting for transfers between devices, hand(): return lax.ppermute(handing, 'depth', inner_pairs(groups))  0.77 us
  transfers between devices with their start and end apart: 9, of which 5 were waited for; matrix products, arithmetic and copies ran while one was open for 0% of the time, Pallas kernels for 18%

profile of v9, /device:TPU:0, one launch (start us, length us, event | category | flops | bytes accessed | tf_op | source)
XLA Modules:
  0.0 18.3 jit_solution(8018617078369805345)
XLA Ops:
  0.0 1.3 %shard_map.55 = (f32[4,16,3200]{2,1,0:T(8,128)S(1)}, s32[4,16,2048]{2,1,0:T(8,128)S(1)}, f32[3,4,16]{2,1,0:T(4,128)S(1)}, f32[4,16]{1,0:T(4,128)S(1)}, f32[1,16,...) custom-call(f32[4,16,2048]{2,1,0:T(8,128)} %refs_0_.1, s32[4,16,2048]{2,1,0:T(8,128)} %refs_1_.1, ...), custom_call_target="tpu_custom_call" | custom-call | tf_op jit(solution)/shard_map/pallas_call | solution.py:332
  1.3 0.5 %collective-permute-start = (f32[4,16,3200]{2,1,0:T(8,128)S(1)}, f32[4,16,3200]{2,1,0:T(8,128)S(1)}, u32[]{:S(2)}, u32[]{:S(2)}) collective-permute-start(f32[4,16,3200]{2,1,0:T(8,128)S(1)} %get-tuple-element.15.refs_0_.refs_1_), channel_id=1, source_target_pairs={{0,4},{4,0},{8,12},{12,8},{16,20},{20,16},{24,28},{28,24},{1,5},{5... | collective-permute-start | bytes 2457608 | tf_op jit(solution)/shard_map/ppermute | solution.py:343
  1.8 2.6 %collective-permute-start.1 = (f32[1,16,2048]{2,1,0:T(8,128)S(1)}, f32[1,16,2048]{2,1,0:T(8,128)S(1)}, u32[]{:S(2)}, u32[]{:S(2)}) collective-permute-start(f32[1,16,2048]{2,1,0:T(8,128)S(1)} %get-tuple-element.19), channel_id=1, source_target_pairs={{0,1},{1,0},{2,3},{3,2},{4,8},{5,9},{6,10},{7,11},{8,4},{9,5},{10,... | collective-permute-start | bytes 393224 | tf_op jit(solution)/shard_map/ppermute | solution.py:344
  4.5 0.1 collective-permute-start.2
  4.6 1.2 %collective-permute-start.3 = (f32[4,2048]{1,0:T(4,128)S(1)}, f32[4,2048]{1,0:T(4,128)S(1)}, u32[]{:S(2)}, u32[]{:S(2)}) collective-permute-start(f32[4,2048]{1,0:T(4,128)S(1)} %get-tuple-element.21), channel_id=1, source_target_pairs={{0,4},{1,2},{2,1},{3,7},{4,0},{5,6},{6,5},{7,3},{8,12},{9,10},{10,... | collective-permute-start | bytes 98312 | tf_op jit(solution)/shard_map/ppermute | solution.py:346
  5.8 0.8 %shard_map.56.refs_3_.refs_2_ = f32[6,13,16,128]{3,2,1,0:T(8,128)S(1)} custom-call(f32[4,16,3200]{2,1,0:T(8,128)S(1)} %get-tuple-element.15.refs_0_.refs_1_, f32[3,4,16]{2,1,0:T(4,128)S(1)} %get-tuple-element.16.refs_1_, f32[4,16]{1,0:T(4,128)S(1)} %get-tuple-element.17.refs_2_, s32[4,16,2048]{2,1,0:T(8,128)S(1)} %get-tuple-element.18.refs_3_), custom_call_target="tpu_custom_call" | custom-call | flops 2000000 | bytes 2000000 | tf_op jit(solution)/shard_map/pallas_call | solution.py:43
  6.6 0.8 %shard_map.57.refs_1_.refs_3_.refs_2_ = f32[6,13,16,128]{3,2,1,0:T(8,128)S(1)} custom-call(f32[4,16,3200]{2,1,0:T(8,128)S(1)} %collective-permute-done.refs_0_.refs_1_, f32[3,4,16]{2,1,0:T(4,128)S(1)} %get-tuple-element.16.refs_1_, f32[4,16]{1,0:T(4,128)S(1)} %get-tuple-element.17.refs_2_, f32[6,13,16,128]{3,2,1,0:T(8,128)S(1)} %shard_map.56.refs_3_.refs_2_), custom_call_target="tpu_custom_call" | custom-call | flops 2000000 | bytes 2000000 | tf_op jit(solution)/shard_map/pallas_call | solution.py:43
  7.4 1.0 %collective-permute-done.2.refs_1_.refs_4_ = f32[4,2048]{1,0:T(4,128)S(1)} collective-permute-done((f32[4,2048]{1,0:T(4,128)S(1)}, f32[4,2048]{1,0:T(4,128)S(1)}, u32[]{:S(2)}, u32[]{:S(2)}) %collective-permute-start.2) | collective-permute-done | bytes 32800 | tf_op jit(solution)/shard_map/ppermute | solution.py:345
  8.5 0.3 %shard_map.60.refs_5_ = f32[6,4,16,128]{3,2,1,0:T(8,128)S(1)} custom-call(f32[4,16,3200]{2,1,0:T(8,128)S(1)} %get-tuple-element.15.refs_0_.refs_1_, f32[4,16,3200]{2,1,0:T(8,128)S(1)} %collective-permute-done.refs_0_.refs_1_, f32[6,13,16,128]{3,2,1,0:T(8,128)S(1)} %shard_map.56.refs_3_.refs_2_, f32[1,16,2048]{2,1,0:T(8,128)S(1)} %collective-permute-done.1.refs_0_.refs_3_, ...), custom_call_target="tpu_custom_call" | custom-call | flops 2000000 | bytes 2000000 | tf_op jit(solution)/shard_map/pallas_call | solution.py:43
  8.8 0.2 %shard_map.58.refs_3_ = f32[6,4,16,128]{3,2,1,0:T(8,128)S(1)} custom-call(f32[4,16,3200]{2,1,0:T(8,128)S(1)} %collective-permute-done.refs_0_.refs_1_, f32[6,13,16,128]{3,2,1,0:T(8,128)S(1)} %shard_map.57.refs_1_.refs_3_.refs_2_), custom_call_target="tpu_custom_call" | custom-call | flops 2000000 | bytes 2000000 | tf_op jit(solution)/shard_map/pallas_call | solution.py:43
  9.0 0.8 %collective-permute-done.4.refs_4_ = f32[6,24,128]{2,1,0:T(8,128)S(1)} collective-permute-done((f32[6,24,128]{2,1,0:T(8,128)S(1)}, f32[6,24,128]{2,1,0:T(8,128)S(1)}, u32[]{:S(2)}, u32[]{:S(2)}) %collective-permute-start.4) | collective-permute-done | bytes 73760 | tf_op jit(solution)/shard_map/ppermute | solution.py:364
  9.8 0.2 %shard_map.61 = (f32[2,4,16,128]{3,2,1,0:T(8,128)S(1)}, f32[2,4,16,128]{3,2,1,0:T(8,128)S(1)}, f32[2,4,16,128]{3,2,1,0:T(8,128)S(1)}) custom-call(f32[4,16,3200]{2,1,0:T(8,128)S(1)} %collective-permute-done.refs_0_.refs_1_, f32[4,16,3200]{2,1,0:T(8,128)S(1)} %get-tuple-element.15.refs_0_.refs_1_, f32[6,13,16,128]{3,2,1,0:T(8,128)S(1)} %shard_map.57.refs_1_.refs_3_.refs_2_, ...), custom_call_target="tpu_custom_call" | custom-call | flops 2000000 | bytes 2000000 | tf_op jit(solution)/shard_map/pallas_call | solution.py:43
  10.0 2.3 %collective-permute-start.5 = (f32[2,4,16,128]{3,2,1,0:T(8,128)S(1)}, f32[2,4,16,128]{3,2,1,0:T(8,128)S(1)}, u32[]{:S(2)}, u32[]{:S(2)}) collective-permute-start(f32[2,4,16,128]{3,2,1,0:T(8,128)S(1)} %get-tuple-element.22), channel_id=1, source_target_pairs={{0,24},{4,28},{8,16},{12,20},{16,8},{20,12},{24,0},{28,4},{1,25},{... | collective-permute-start | bytes 196616 | tf_op jit(solution)/shard_map/ppermute | solution.py:389
  12.3 1.0 %collective-permute-start.6 = (f32[2,4,16,128]{3,2,1,0:T(8,128)S(1)}, f32[2,4,16,128]{3,2,1,0:T(8,128)S(1)}, u32[]{:S(2)}, u32[]{:S(2)}) collective-permute-start(f32[2,4,16,128]{3,2,1,0:T(8,128)S(1)} %get-tuple-element.23), channel_id=1, source_target_pairs={{0,8},{4,12},{8,0},{12,4},{16,24},{20,28},{24,16},{28,20},{1,9},{5... | collective-permute-start | bytes 196616 | tf_op jit(solution)/shard_map/ppermute | solution.py:389
  13.3 0.4 %collective-permute-start.7 = (f32[2,4,16,128]{3,2,1,0:T(8,128)S(1)}, f32[2,4,16,128]{3,2,1,0:T(8,128)S(1)}, u32[]{:S(2)}, u32[]{:S(2)}) collective-permute-start(f32[2,4,16,128]{3,2,1,0:T(8,128)S(1)} %get-tuple-element.24.refs_4_.refs_3_), channel_id=1, source_target_pairs={{0,16},{4,20},{8,24},{12,28},{16,0},{20,4},{24,8},{28,12},{1,17},{... | collective-permute-start | bytes 196616 | tf_op jit(solution)/shard_map/ppermute | solution.py:389
  13.8 0.4 %shard_map.62.refs_3_.refs_2_ = f32[2,13,16,128]{3,2,1,0:T(8,128)S(1)} custom-call(f32[4,16,3200]{2,1,0:T(8,128)S(1)} %get-tuple-element.15.refs_0_.refs_1_, f32[3,4,16]{2,1,0:T(4,128)S(1)} %get-tuple-element.16.refs_1_, f32[4,16]{1,0:T(4,128)S(1)} %get-tuple-element.17.refs_2_, s32[4,16,2048]{2,1,0:T(8,128)S(1)} %get-tuple-element.18.refs_3_, ...), custom_call_target="tpu_custom_call" | custom-call | flops 2000000 | bytes 2000000 | tf_op jit(solution)/shard_map/pallas_call | solution.py:43
  14.2 0.1 shard_map.66.refs_5_
  14.4 0.4 %shard_map.63.refs_1_.refs_2_ = f32[2,13,16,128]{3,2,1,0:T(8,128)S(1)} custom-call(f32[4,16,3200]{2,1,0:T(8,128)S(1)} %collective-permute-done.refs_0_.refs_1_, f32[3,4,16]{2,1,0:T(4,128)S(1)} %get-tuple-element.16.refs_1_, f32[4,16]{1,0:T(4,128)S(1)} %get-tuple-element.17.refs_2_, f32[2,13,16,128]{3,2,1,0:T(8,128)S(1)} %shard_map.62.refs_3_.refs_2_), custom_call_target="tpu_custom_call" | custom-call | flops 2000000 | bytes 2000000 | tf_op jit(solution)/shard_map/pallas_call | solution.py:43
  14.8 0.1 shard_map.64.refs_3_
  15.0 0.1 shard_map.67.refs_3_
  15.1 0.2 collective-permute-done.5.refs_0_
  15.2 1.7 %collective-permute-done.6.refs_1_ = f32[2,4,16,128]{3,2,1,0:T(8,128)S(1)} collective-permute-done((f32[2,4,16,128]{3,2,1,0:T(8,128)S(1)}, f32[2,4,16,128]{3,2,1,0:T(8,128)S(1)}, u32[]{:S(2)}, u32[]{:S(2)}) %collective-permute-start.6) | collective-permute-done | bytes 65568 | tf_op jit(solution)/shard_map/ppermute | solution.py:389
  16.9 0.7 %collective-permute-done.7.refs_2_ = f32[2,4,16,128]{3,2,1,0:T(8,128)S(1)} collective-permute-done((f32[2,4,16,128]{3,2,1,0:T(8,128)S(1)}, f32[2,4,16,128]{3,2,1,0:T(8,128)S(1)}, u32[]{:S(2)}, u32[]{:S(2)}) %collective-permute-start.7) | collective-permute-done | bytes 65568 | tf_op jit(solution)/shard_map/ppermute | solution.py:389
  17.6 0.7 %shard_map.68 = f32[4,16,256]{2,1,0:T(8,128)} custom-call(f32[2,4,16,128]{3,2,1,0:T(8,128)S(1)} %collective-permute-done.5.refs_0_, f32[2,4,16,128]{3,2,1,0:T(8,128)S(1)} %collective-permute-done.6.refs_1_, f32[2,4,16,128]{3,2,1,0:T(8,128)S(1)} %collective-permute-done.7.refs_2_, f32[2,4,16,128]{3,2,1,0:T(8,128)S(1)} %shard_map.67.refs_3_), custom_call_target="tpu_custom_call" | custom-call | flops 2000000 | bytes 2000000 | tf_op jit(solution)/shard_map/pallas_call | solution.py:43
  (8 shorter events, 0.1 us)
Async XLA Ops:
  1.3 5.3 %collective-permute-start = (f32[4,16,3200]{2,1,0:T(8,128)S(1)}, f32[4,16,3200]{2,1,0:T(8,128)S(1)}, u32[]{:S(2)}, u32[]{:S(2)}) collective-permute-start(f32[4,16,3200]{2,1,0:T(8,128)S(1)} %get-tuple-element.15.refs_0_.refs_1_), channel_id=1, source_target_pairs={{0,4},{4,0},{8,12},{12,8},{16,20},{20,16},{24,28},{28,24},{1,5},{5... | collective-permute-start | bytes 2457608 | tf_op jit(solution)/shard_map/ppermute | solution.py:343
  1.8 6.6 %collective-permute-start.1 = (f32[1,16,2048]{2,1,0:T(8,128)S(1)}, f32[1,16,2048]{2,1,0:T(8,128)S(1)}, u32[]{:S(2)}, u32[]{:S(2)}) collective-permute-start(f32[1,16,2048]{2,1,0:T(8,128)S(1)} %get-tuple-element.19), channel_id=1, source_target_pairs={{0,1},{1,0},{2,3},{3,2},{4,8},{5,9},{6,10},{7,11},{8,4},{9,5},{10,... | collective-permute-start | bytes 393224 | tf_op jit(solution)/shard_map/ppermute | solution.py:344
  4.5 3.9 %collective-permute-start.2 = (f32[4,2048]{1,0:T(4,128)S(1)}, f32[4,2048]{1,0:T(4,128)S(1)}, u32[]{:S(2)}, u32[]{:S(2)}) collective-permute-start(f32[4,2048]{1,0:T(4,128)S(1)} %get-tuple-element.20), channel_id=1, source_target_pairs={{0,1},{1,0},{2,3},{3,2},{4,5},{5,4},{6,7},{7,6},{8,9},{9,8},{10,11... | collective-permute-start | bytes 98312 | tf_op jit(solution)/shard_map/ppermute | solution.py:345
  4.6 3.8 %collective-permute-start.3 = (f32[4,2048]{1,0:T(4,128)S(1)}, f32[4,2048]{1,0:T(4,128)S(1)}, u32[]{:S(2)}, u32[]{:S(2)}) collective-permute-start(f32[4,2048]{1,0:T(4,128)S(1)} %get-tuple-element.21), channel_id=1, source_target_pairs={{0,4},{1,2},{2,1},{3,7},{4,0},{5,6},{6,5},{7,3},{8,12},{9,10},{10,... | collective-permute-start | bytes 98312 | tf_op jit(solution)/shard_map/ppermute | solution.py:346
  8.4 1.3 %collective-permute-start.4 = (f32[6,24,128]{2,1,0:T(8,128)S(1)}, f32[6,24,128]{2,1,0:T(8,128)S(1)}, u32[]{:S(2)}, u32[]{:S(2)}) collective-permute-start(f32[6,24,128]{2,1,0:T(8,128)S(1)} %shard_map.59), channel_id=1, source_target_pairs={{0,4},{4,0},{8,12},{12,8},{16,20},{20,16},{24,28},{28,24},{1,5},{5... | collective-permute-start | bytes 221192 | tf_op jit(solution)/shard_map/ppermute | solution.py:364
  10.0 5.2 %collective-permute-start.5 = (f32[2,4,16,128]{3,2,1,0:T(8,128)S(1)}, f32[2,4,16,128]{3,2,1,0:T(8,128)S(1)}, u32[]{:S(2)}, u32[]{:S(2)}) collective-permute-start(f32[2,4,16,128]{3,2,1,0:T(8,128)S(1)} %get-tuple-element.22), channel_id=1, source_target_pairs={{0,24},{4,28},{8,16},{12,20},{16,8},{20,12},{24,0},{28,4},{1,25},{... | collective-permute-start | bytes 196616 | tf_op jit(solution)/shard_map/ppermute | solution.py:389
  12.3 4.6 %collective-permute-start.6 = (f32[2,4,16,128]{3,2,1,0:T(8,128)S(1)}, f32[2,4,16,128]{3,2,1,0:T(8,128)S(1)}, u32[]{:S(2)}, u32[]{:S(2)}) collective-permute-start(f32[2,4,16,128]{3,2,1,0:T(8,128)S(1)} %get-tuple-element.23), channel_id=1, source_target_pairs={{0,8},{4,12},{8,0},{12,4},{16,24},{20,28},{24,16},{28,20},{1,9},{5... | collective-permute-start | bytes 196616 | tf_op jit(solution)/shard_map/ppermute | solution.py:389
  13.3 4.3 %collective-permute-start.7 = (f32[2,4,16,128]{3,2,1,0:T(8,128)S(1)}, f32[2,4,16,128]{3,2,1,0:T(8,128)S(1)}, u32[]{:S(2)}, u32[]{:S(2)}) collective-permute-start(f32[2,4,16,128]{3,2,1,0:T(8,128)S(1)} %get-tuple-element.24.refs_4_.refs_3_), channel_id=1, source_target_pairs={{0,16},{4,20},{8,24},{12,28},{16,0},{20,4},{24,8},{28,12},{1,17},{... | collective-permute-start | bytes 196616 | tf_op jit(solution)/shard_map/ppermute | solution.py:389
  13.8 1.2 %collective-permute-start.8 = (f32[2,24,128]{2,1,0:T(8,128)S(1)}, f32[2,24,128]{2,1,0:T(8,128)S(1)}, u32[]{:S(2)}, u32[]{:S(2)}) collective-permute-start(f32[2,24,128]{2,1,0:T(8,128)S(1)} %shard_map.65), channel_id=1, source_target_pairs={{0,4},{4,0},{8,12},{12,8},{16,20},{20,16},{24,28},{28,24},{1,5},{5... | collective-permute-start | bytes 73736 | tf_op jit(solution)/shard_map/ppermute | solution.py:364

commit v10 on v9

--- a/solution.py
+++ b/solution.py
@@ -291,6 +291,11 @@
     chip = lax.axis_index("depth") // 2
     for h in range(pieces[0].shape[0]):
         values = [[piece[h, ch] for ch in range(4)] for piece in pieces]
+        if len(values) == 4:
+            turned = lax.axis_index("strip") > 0
+            one, two = values[1], values[2]
+            values[1] = [jnp.where(turned, y, x) for x, y in zip(one, two)]
+            values[2] = [jnp.where(turned, x, y) for x, y in zip(one, two)]
         bit = 0
         while len(values) > 1:
             swap = (chip >> bit) % 2 == 1
@@ -324,6 +329,7 @@
         if not paired:
             return parity * half + i
         k = sum(jnp.where(i // per == n, ks[n], 0) for n in range(chips))
+        k = jnp.where((lax.axis_index("strip") > 0) & (k > 0) & (k < 3) & (chips == 4), 3 - k, k)
         return ((index // 2 ^ k) * 2 + parity) * per + i % per
 
     given = (density, materials, occupancy_flags[0], tf_color.transpose(1, 0, 2), tf_opacity)
@@ -386,7 +392,10 @@
     if paired:
         sent = images(0, far, chips - 1, handed, weights, weights_beside)
         moved = [
-            lax.ppermute(image, "depth", [(i, i ^ (2 * k)) for i in range(groups)])
+            lax.ppermute(image, both, [
+                (g * strips + t, (g ^ 2 * (3 - k if t and k < 3 and chips == 4 else k)) * strips + t)
+                for g in range(groups) for t in range(strips)
+            ])
             for image, k in zip(sent, ks)
         ]
         late = sent[-1:]

time: 18.4 us -> 18.4 us (level)
  no operation moved by 1% of the time
where the time goes in v10:
time: 18.4 us; the launch traced here: 18.3 us
  starting transfers between devices  8.31 us (45%)
  Pallas kernels  5.59 us (30%)
  waiting for transfers between devices  4.29 us (23%)
    pallas_call x13, Pallas kernels, call(): pl.pallas_call(body, out_shape=out_shape, in_specs=[VMEM] * count + [pl.B...  4.28 us
    ppermute x3, starting transfers between devices, on_device(): lax.ppermute(image, both, [(g * strips + t, (g ^ 2 * (3 - k if t and k <...  3.75 us
    ppermute x1, starting transfers between devices, on_device(): far_z = lax.ppermute(layer, both, outer_pairs(groups, strips, 'depth'))  2.65 us
    ppermute x3, waiting for transfers between devices, on_device(): lax.ppermute(image, both, [(g * strips + t, (g ^ 2 * (3 - k if t and k <...  2.54 us
    pallas_call x1, Pallas kernels, on_device(): pl.pallas_call(functools.partial(load_kernel, order), out_shape=[whole] +...  1.31 us
    ppermute x1, starting transfers between devices, on_device(): far_y = lax.ppermute(outer_y, both, outer_pairs(groups, strips, 'strip'))  1.25 us
    ppermute x1, waiting for transfers between devices, on_device(): near_y = lax.ppermute(inner_y, 'strip', inner_pairs(strips))  0.97 us
    ppermute x2, waiting for transfers between devices, hand(): return lax.ppermute(handing, 'depth', inner_pairs(groups))  0.77 us
  transfers between devices with their start and end apart: 9, of which 5 were waited for; matrix products, arithmetic and copies ran while one was open for 0% of the time, Pallas kernels for 18%

profile of v10, /device:TPU:0, one launch (start us, length us, event | category | flops | bytes accessed | tf_op | source)
XLA Modules:
  0.0 18.3 jit_solution(10885749305651172173)
XLA Ops:
  0.0 1.3 %shard_map.55 = (f32[4,16,3200]{2,1,0:T(8,128)S(1)}, s32[4,16,2048]{2,1,0:T(8,128)S(1)}, f32[3,4,16]{2,1,0:T(4,128)S(1)}, f32[4,16]{1,0:T(4,128)S(1)}, f32[1,16,...) custom-call(f32[4,16,2048]{2,1,0:T(8,128)} %refs_0_.1, s32[4,16,2048]{2,1,0:T(8,128)} %refs_1_.1, ...), custom_call_target="tpu_custom_call" | custom-call | tf_op jit(solution)/shard_map/pallas_call | solution.py:338
  1.3 0.5 %collective-permute-start = (f32[4,16,3200]{2,1,0:T(8,128)S(1)}, f32[4,16,3200]{2,1,0:T(8,128)S(1)}, u32[]{:S(2)}, u32[]{:S(2)}) collective-permute-start(f32[4,16,3200]{2,1,0:T(8,128)S(1)} %get-tuple-element.15.refs_0_.refs_1_), channel_id=1, source_target_pairs={{0,4},{4,0},{8,12},{12,8},{16,20},{20,16},{24,28},{28,24},{1,5},{5... | collective-permute-start | bytes 2457608 | tf_op jit(solution)/shard_map/ppermute | solution.py:349
  1.8 2.6 %collective-permute-start.1 = (f32[1,16,2048]{2,1,0:T(8,128)S(1)}, f32[1,16,2048]{2,1,0:T(8,128)S(1)}, u32[]{:S(2)}, u32[]{:S(2)}) collective-permute-start(f32[1,16,2048]{2,1,0:T(8,128)S(1)} %get-tuple-element.19), channel_id=1, source_target_pairs={{0,1},{1,0},{2,3},{3,2},{4,8},{5,9},{6,10},{7,11},{8,4},{9,5},{10,... | collective-permute-start | bytes 393224 | tf_op jit(solution)/shard_map/ppermute | solution.py:350
  4.5 0.1 collective-permute-start.2
  4.6 1.2 %collective-permute-start.3 = (f32[4,2048]{1,0:T(4,128)S(1)}, f32[4,2048]{1,0:T(4,128)S(1)}, u32[]{:S(2)}, u32[]{:S(2)}) collective-permute-start(f32[4,2048]{1,0:T(4,128)S(1)} %get-tuple-element.21), channel_id=1, source_target_pairs={{0,4},{1,2},{2,1},{3,7},{4,0},{5,6},{6,5},{7,3},{8,12},{9,10},{10,... | collective-permute-start | bytes 98312 | tf_op jit(solution)/shard_map/ppermute | solution.py:352
  5.8 0.8 %shard_map.56.refs_3_.refs_2_ = f32[6,13,16,128]{3,2,1,0:T(8,128)S(1)} custom-call(f32[4,16,3200]{2,1,0:T(8,128)S(1)} %get-tuple-element.15.refs_0_.refs_1_, f32[3,4,16]{2,1,0:T(4,128)S(1)} %get-tuple-element.16.refs_1_, f32[4,16]{1,0:T(4,128)S(1)} %get-tuple-element.17.refs_2_, s32[4,16,2048]{2,1,0:T(8,128)S(1)} %get-tuple-element.18.refs_3_), custom_call_target="tpu_custom_call" | custom-call | flops 2000000 | bytes 2000000 | tf_op jit(solution)/shard_map/pallas_call | solution.py:43
  6.6 0.8 %shard_map.57.refs_1_.refs_3_.refs_2_ = f32[6,13,16,128]{3,2,1,0:T(8,128)S(1)} custom-call(f32[4,16,3200]{2,1,0:T(8,128)S(1)} %collective-permute-done.refs_0_.refs_1_, f32[3,4,16]{2,1,0:T(4,128)S(1)} %get-tuple-element.16.refs_1_, f32[4,16]{1,0:T(4,128)S(1)} %get-tuple-element.17.refs_2_, f32[6,13,16,128]{3,2,1,0:T(8,128)S(1)} %shard_map.56.refs_3_.refs_2_), custom_call_target="tpu_custom_call" | custom-call | flops 2000000 | bytes 2000000 | tf_op jit(solution)/shard_map/pallas_call | solution.py:43
  7.4 1.0 %collective-permute-done.2.refs_1_.refs_4_ = f32[4,2048]{1,0:T(4,128)S(1)} collective-permute-done((f32[4,2048]{1,0:T(4,128)S(1)}, f32[4,2048]{1,0:T(4,128)S(1)}, u32[]{:S(2)}, u32[]{:S(2)}) %collective-permute-start.2) | collective-permute-done | bytes 32800 | tf_op jit(solution)/shard_map/ppermute | solution.py:351
  8.5 0.3 %shard_map.60.refs_5_ = f32[6,4,16,128]{3,2,1,0:T(8,128)S(1)} custom-call(f32[4,16,3200]{2,1,0:T(8,128)S(1)} %get-tuple-element.15.refs_0_.refs_1_, f32[4,16,3200]{2,1,0:T(8,128)S(1)} %collective-permute-done.refs_0_.refs_1_, f32[6,13,16,128]{3,2,1,0:T(8,128)S(1)} %shard_map.56.refs_3_.refs_2_, f32[1,16,2048]{2,1,0:T(8,128)S(1)} %collective-permute-done.1.refs_0_.refs_3_, ...), custom_call_target="tpu_custom_call" | custom-call | flops 2000000 | bytes 2000000 | tf_op jit(solution)/shard_map/pallas_call | solution.py:43
  8.8 0.2 %shard_map.58.refs_3_ = f32[6,4,16,128]{3,2,1,0:T(8,128)S(1)} custom-call(f32[4,16,3200]{2,1,0:T(8,128)S(1)} %collective-permute-done.refs_0_.refs_1_, f32[6,13,16,128]{3,2,1,0:T(8,128)S(1)} %shard_map.57.refs_1_.refs_3_.refs_2_), custom_call_target="tpu_custom_call" | custom-call | flops 2000000 | bytes 2000000 | tf_op jit(solution)/shard_map/pallas_call | solution.py:43
  9.0 0.8 %collective-permute-done.4.refs_4_ = f32[6,24,128]{2,1,0:T(8,128)S(1)} collective-permute-done((f32[6,24,128]{2,1,0:T(8,128)S(1)}, f32[6,24,128]{2,1,0:T(8,128)S(1)}, u32[]{:S(2)}, u32[]{:S(2)}) %collective-permute-start.4) | collective-permute-done | bytes 73760 | tf_op jit(solution)/shard_map/ppermute | solution.py:370
  9.8 0.2 %shard_map.61 = (f32[2,4,16,128]{3,2,1,0:T(8,128)S(1)}, f32[2,4,16,128]{3,2,1,0:T(8,128)S(1)}, f32[2,4,16,128]{3,2,1,0:T(8,128)S(1)}) custom-call(f32[4,16,3200]{2,1,0:T(8,128)S(1)} %collective-permute-done.refs_0_.refs_1_, f32[4,16,3200]{2,1,0:T(8,128)S(1)} %get-tuple-element.15.refs_0_.refs_1_, f32[6,13,16,128]{3,2,1,0:T(8,128)S(1)} %shard_map.57.refs_1_.refs_3_.refs_2_, ...), custom_call_target="tpu_custom_call" | custom-call | flops 2000000 | bytes 2000000 | tf_op jit(solution)/shard_map/pallas_call | solution.py:43
  10.0 2.3 %collective-permute-start.5 = (f32[2,4,16,128]{3,2,1,0:T(8,128)S(1)}, f32[2,4,16,128]{3,2,1,0:T(8,128)S(1)}, u32[]{:S(2)}, u32[]{:S(2)}) collective-permute-start(f32[2,4,16,128]{3,2,1,0:T(8,128)S(1)} %get-tuple-element.22), channel_id=1, source_target_pairs={{0,24},{1,25},{2,26},{3,27},{4,28},{5,29},{6,30},{7,31},{8,16},{9,... | collective-permute-start | bytes 196616 | tf_op jit(solution)/shard_map/ppermute | solution.py:395
  12.3 1.0 %collective-permute-start.6 = (f32[2,4,16,128]{3,2,1,0:T(8,128)S(1)}, f32[2,4,16,128]{3,2,1,0:T(8,128)S(1)}, u32[]{:S(2)}, u32[]{:S(2)}) collective-permute-start(f32[2,4,16,128]{3,2,1,0:T(8,128)S(1)} %get-tuple-element.23), channel_id=1, source_target_pairs={{0,8},{1,17},{2,18},{3,19},{4,12},{5,21},{6,22},{7,23},{8,0},{9,25... | collective-permute-start | bytes 196616 | tf_op jit(solution)/shard_map/ppermute | solution.py:395
  13.3 0.4 %collective-permute-start.7 = (f32[2,4,16,128]{3,2,1,0:T(8,128)S(1)}, f32[2,4,16,128]{3,2,1,0:T(8,128)S(1)}, u32[]{:S(2)}, u32[]{:S(2)}) collective-permute-start(f32[2,4,16,128]{3,2,1,0:T(8,128)S(1)} %get-tuple-element.24.refs_4_.refs_3_), channel_id=1, source_target_pairs={{0,16},{1,9},{2,10},{3,11},{4,20},{5,13},{6,14},{7,15},{8,24},{9,1... | collective-permute-start | bytes 196616 | tf_op jit(solution)/shard_map/ppermute | solution.py:395
  13.8 0.4 %shard_map.62.refs_3_.refs_2_ = f32[2,13,16,128]{3,2,1,0:T(8,128)S(1)} custom-call(f32[4,16,3200]{2,1,0:T(8,128)S(1)} %get-tuple-element.15.refs_0_.refs_1_, f32[3,4,16]{2,1,0:T(4,128)S(1)} %get-tuple-element.16.refs_1_, f32[4,16]{1,0:T(4,128)S(1)} %get-tuple-element.17.refs_2_, s32[4,16,2048]{2,1,0:T(8,128)S(1)} %get-tuple-element.18.refs_3_, ...), custom_call_target="tpu_custom_call" | custom-call | flops 2000000 | bytes 2000000 | tf_op jit(solution)/shard_map/pallas_call | solution.py:43
  14.2 0.1 shard_map.66.refs_5_
  14.4 0.4 %shard_map.63.refs_1_.refs_2_ = f32[2,13,16,128]{3,2,1,0:T(8,128)S(1)} custom-call(f32[4,16,3200]{2,1,0:T(8,128)S(1)} %collective-permute-done.refs_0_.refs_1_, f32[3,4,16]{2,1,0:T(4,128)S(1)} %get-tuple-element.16.refs_1_, f32[4,16]{1,0:T(4,128)S(1)} %get-tuple-element.17.refs_2_, f32[2,13,16,128]{3,2,1,0:T(8,128)S(1)} %shard_map.62.refs_3_.refs_2_), custom_call_target="tpu_custom_call" | custom-call | flops 2000000 | bytes 2000000 | tf_op jit(solution)/shard_map/pallas_call | solution.py:43
  14.8 0.1 shard_map.64.refs_3_
  15.0 0.1 shard_map.67.refs_3_
  15.1 0.2 collective-permute-done.5.refs_0_
  15.2 1.7 %collective-permute-done.6.refs_1_ = f32[2,4,16,128]{3,2,1,0:T(8,128)S(1)} collective-permute-done((f32[2,4,16,128]{3,2,1,0:T(8,128)S(1)}, f32[2,4,16,128]{3,2,1,0:T(8,128)S(1)}, u32[]{:S(2)}, u32[]{:S(2)}) %collective-permute-start.6) | collective-permute-done | bytes 65568 | tf_op jit(solution)/shard_map/ppermute | solution.py:395
  16.9 0.7 %collective-permute-done.7.refs_2_ = f32[2,4,16,128]{3,2,1,0:T(8,128)S(1)} collective-permute-done((f32[2,4,16,128]{3,2,1,0:T(8,128)S(1)}, f32[2,4,16,128]{3,2,1,0:T(8,128)S(1)}, u32[]{:S(2)}, u32[]{:S(2)}) %collective-permute-start.7) | collective-permute-done | bytes 65568 | tf_op jit(solution)/shard_map/ppermute | solution.py:395
  17.6 0.7 %shard_map.68 = f32[4,16,256]{2,1,0:T(8,128)} custom-call(f32[2,4,16,128]{3,2,1,0:T(8,128)S(1)} %collective-permute-done.5.refs_0_, f32[2,4,16,128]{3,2,1,0:T(8,128)S(1)} %collective-permute-done.6.refs_1_, f32[2,4,16,128]{3,2,1,0:T(8,128)S(1)} %collective-permute-done.7.refs_2_, f32[2,4,16,128]{3,2,1,0:T(8,128)S(1)} %shard_map.67.refs_3_), custom_call_target="tpu_custom_call" | custom-call | flops 2000000 | bytes 2000000 | tf_op jit(solution)/shard_map/pallas_call | solution.py:43
  (8 shorter events, 0.1 us)
Async XLA Ops:
  1.3 5.3 %collective-permute-start = (f32[4,16,3200]{2,1,0:T(8,128)S(1)}, f32[4,16,3200]{2,1,0:T(8,128)S(1)}, u32[]{:S(2)}, u32[]{:S(2)}) collective-permute-start(f32[4,16,3200]{2,1,0:T(8,128)S(1)} %get-tuple-element.15.refs_0_.refs_1_), channel_id=1, source_target_pairs={{0,4},{4,0},{8,12},{12,8},{16,20},{20,16},{24,28},{28,24},{1,5},{5... | collective-permute-start | bytes 2457608 | tf_op jit(solution)/shard_map/ppermute | solution.py:349
  1.8 6.6 %collective-permute-start.1 = (f32[1,16,2048]{2,1,0:T(8,128)S(1)}, f32[1,16,2048]{2,1,0:T(8,128)S(1)}, u32[]{:S(2)}, u32[]{:S(2)}) collective-permute-start(f32[1,16,2048]{2,1,0:T(8,128)S(1)} %get-tuple-element.19), channel_id=1, source_target_pairs={{0,1},{1,0},{2,3},{3,2},{4,8},{5,9},{6,10},{7,11},{8,4},{9,5},{10,... | collective-permute-start | bytes 393224 | tf_op jit(solution)/shard_map/ppermute | solution.py:350
  4.5 3.9 %collective-permute-start.2 = (f32[4,2048]{1,0:T(4,128)S(1)}, f32[4,2048]{1,0:T(4,128)S(1)}, u32[]{:S(2)}, u32[]{:S(2)}) collective-permute-start(f32[4,2048]{1,0:T(4,128)S(1)} %get-tuple-element.20), channel_id=1, source_target_pairs={{0,1},{1,0},{2,3},{3,2},{4,5},{5,4},{6,7},{7,6},{8,9},{9,8},{10,11... | collective-permute-start | bytes 98312 | tf_op jit(solution)/shard_map/ppermute | solution.py:351
  4.6 3.8 %collective-permute-start.3 = (f32[4,2048]{1,0:T(4,128)S(1)}, f32[4,2048]{1,0:T(4,128)S(1)}, u32[]{:S(2)}, u32[]{:S(2)}) collective-permute-start(f32[4,2048]{1,0:T(4,128)S(1)} %get-tuple-element.21), channel_id=1, source_target_pairs={{0,4},{1,2},{2,1},{3,7},{4,0},{5,6},{6,5},{7,3},{8,12},{9,10},{10,... | collective-permute-start | bytes 98312 | tf_op jit(solution)/shard_map/ppermute | solution.py:352
  8.4 1.3 %collective-permute-start.4 = (f32[6,24,128]{2,1,0:T(8,128)S(1)}, f32[6,24,128]{2,1,0:T(8,128)S(1)}, u32[]{:S(2)}, u32[]{:S(2)}) collective-permute-start(f32[6,24,128]{2,1,0:T(8,128)S(1)} %shard_map.59), channel_id=1, source_target_pairs={{0,4},{4,0},{8,12},{12,8},{16,20},{20,16},{24,28},{28,24},{1,5},{5... | collective-permute-start | bytes 221192 | tf_op jit(solution)/shard_map/ppermute | solution.py:370
  10.0 5.2 %collective-permute-start.5 = (f32[2,4,16,128]{3,2,1,0:T(8,128)S(1)}, f32[2,4,16,128]{3,2,1,0:T(8,128)S(1)}, u32[]{:S(2)}, u32[]{:S(2)}) collective-permute-start(f32[2,4,16,128]{3,2,1,0:T(8,128)S(1)} %get-tuple-element.22), channel_id=1, source_target_pairs={{0,24},{1,25},{2,26},{3,27},{4,28},{5,29},{6,30},{7,31},{8,16},{9,... | collective-permute-start | bytes 196616 | tf_op jit(solution)/shard_map/ppermute | solution.py:395
  12.3 4.6 %collective-permute-start.6 = (f32[2,4,16,128]{3,2,1,0:T(8,128)S(1)}, f32[2,4,16,128]{3,2,1,0:T(8,128)S(1)}, u32[]{:S(2)}, u32[]{:S(2)}) collective-permute-start(f32[2,4,16,128]{3,2,1,0:T(8,128)S(1)} %get-tuple-element.23), channel_id=1, source_target_pairs={{0,8},{1,17},{2,18},{3,19},{4,12},{5,21},{6,22},{7,23},{8,0},{9,25... | collective-permute-start | bytes 196616 | tf_op jit(solution)/shard_map/ppermute | solution.py:395
  13.3 4.3 %collective-permute-start.7 = (f32[2,4,16,128]{3,2,1,0:T(8,128)S(1)}, f32[2,4,16,128]{3,2,1,0:T(8,128)S(1)}, u32[]{:S(2)}, u32[]{:S(2)}) collective-permute-start(f32[2,4,16,128]{3,2,1,0:T(8,128)S(1)} %get-tuple-element.24.refs_4_.refs_3_), channel_id=1, source_target_pairs={{0,16},{1,9},{2,10},{3,11},{4,20},{5,13},{6,14},{7,15},{8,24},{9,1... | collective-permute-start | bytes 196616 | tf_op jit(solution)/shard_map/ppermute | solution.py:395
  13.8 1.2 %collective-permute-start.8 = (f32[2,24,128]{2,1,0:T(8,128)S(1)}, f32[2,24,128]{2,1,0:T(8,128)S(1)}, u32[]{:S(2)}, u32[]{:S(2)}) collective-permute-start(f32[2,24,128]{2,1,0:T(8,128)S(1)} %shard_map.65), channel_id=1, source_target_pairs={{0,4},{4,0},{8,12},{12,8},{16,20},{20,16},{24,28},{28,24},{1,5},{5... | collective-permute-start | bytes 73736 | tf_op jit(solution)/shard_map/ppermute | solution.py:370
